TPU v7x, 128 devices: a whole 4x4x4 slice. The times are simulated.
128 devices in a mesh: leaf: 32 (over x, y, core), sub: 4 (over z).
Axes of the slice: x: 4, y: 4, z: 4, core: 2. Of those that a mesh axis runs over, the one named last changes fastest.
Arguments:
- densities: bfloat16 [16, 524288], P(None, ('leaf', 'sub')), may hold values from -6 to 6
- basis: bfloat16 [2048, 64, 256], P(('leaf', 'sub')), may hold values from -0.375 to 0.375
- near_blocks: bfloat16 [2048, 2048, 256], P(('leaf', 'sub')), may hold values from -0.125 to 0.125
- near_source: int32 [2048, 8], P(('leaf', 'sub')), may hold values from 0 to 2047, as said below
- near_valid: int32 [2048, 8], P(('leaf', 'sub')), may hold values from 0 to 1
- leaf_coupling: bfloat16 [2048, 64, 2048], P(('leaf', 'sub')), may hold values from -0.125 to 0.125
- leaf_source: int32 [2048, 32], P(('leaf', 'sub')), may hold values from 0 to 2047, as said below
- leaf_valid: int32 [2048, 32], P(('leaf', 'sub')), may hold values from 0 to 1
- parent_transfer: bfloat16 [256, 64, 512], P(('leaf', 'sub')), may hold values from -0.4375 to 0.4375
- parent_coupling: bfloat16 [256, 64, 2048], P(('leaf', 'sub')), may hold values from -0.125 to 0.125
- parent_source: int32 [256, 32], P(('leaf', 'sub')), may hold values from 0 to 255
- parent_valid: int32 [256, 32], P(('leaf', 'sub')), may hold values 0 or 1
- grand_transfer: bfloat16 [32, 64, 512], replicated, may hold values from -0.4375 to 0.4375
- grand_coupling: bfloat16 [32, 64, 1024], P('leaf'), may hold values from -0.1875 to 0.1875
- grand_source: int32 [32, 16], P('leaf'), may hold values from 0 to 31
- grand_valid: int32 [32, 16], P('leaf'), may hold values 0 or 1
Outputs:
- potential: bfloat16 [16, 524288], P(None, ('leaf', 'sub'))
Inputs may be any that keep to these rules, and one draw needn't show every extreme that they name: `leaf_source`: for the 16 leaves of one device (aligned blocks of rows), the slots with leaf_valid = 1 name leaves of any one aligned block of 16 leaves at most 8 times; this bound is reached in every draw. `near_source`: every near source leaf lies within 8 leaves of its target leaf in the curve order; both ends of the reach occur.
All inputs are finite; a program needn't handle non-finite values. No bound on the sum of `parent_valid` or of `grand_valid` on one device may be relied on, other than what follows from the above.
Results may differ from a plain program's by a relative error of at most 0.009.
Values may be sent and summed in bfloat16 or wider, within the bound.
No kernel may reach another device: no remote copies, remote signals or barrier semaphores. Data moves between devices by JAX's collectives and lax.ppermute only.
A program may use at most 128 MiB of HBM per device.

v0:
```python
import jax
import jax.numpy as jnp
from jax import lax
from jax.sharding import PartitionSpec as P


def padded_2(cells, sides, width):
    for axis, dim in sides:
        count = lax.axis_size(axis)
        ends = count - 1
        head = lax.slice_in_dim(cells, 0, width, axis=dim)
        tail = lax.slice_in_dim(cells, cells.shape[dim] - width, cells.shape[dim], axis=dim)
        cells = jnp.concatenate(
            [
                lax.ppermute(tail, axis, [(i, (i + 1) % count) for i in range(ends)]),
                cells,
                lax.ppermute(head, axis, [((i + 1) % count, i) for i in range(ends)]),
            ],
            axis=dim,
        )
    return cells


def couple_rows(flat_coefficients, source, valid_slots, blocks, right_sides, rank_width):
    picked = jnp.take(flat_coefficients, source.reshape(-1), axis=0)
    picked = jnp.where(
        valid_slots.reshape(-1)[:, None] == 1, picked, jnp.zeros((), flat_coefficients.dtype)
    )
    picked = picked.reshape(source.shape[0], source.shape[1], right_sides, rank_width)
    coupling_view = blocks.reshape(blocks.shape[0], rank_width, source.shape[1], rank_width)
    return jnp.einsum("tjrb,tajb->tra", picked, coupling_view, preferred_element_type=jnp.float32)


def body(
    densities,
    basis,
    near_blocks,
    near_source,
    near_valid,
    leaf_coupling,
    leaf_source,
    leaf_valid,
    parent_transfer,
    parent_coupling,
    parent_source,
    parent_valid,
    grand_transfer,
    grand_coupling,
    grand_source,
    grand_valid,
):
    right_sides = densities.shape[0]
    owned_leaves, rank_width, leaf_width = basis.shape
    shard_count = lax.axis_size(("leaf", "sub"))
    device_index = lax.axis_index(("leaf", "sub"))
    group_index = lax.axis_index("leaf")
    reach_leaves = owned_leaves // 2
    owned_parents = owned_leaves // 8
    owned_grands = grand_coupling.shape[0]
    row_width = right_sides * rank_width
    blocked = densities.reshape(right_sides, owned_leaves, leaf_width)
    upward = jnp.einsum("rtp,tkp->trk", blocked, basis, preferred_element_type=jnp.float32).astype(
        jnp.bfloat16
    )
    flat_upward = upward.reshape(owned_leaves, row_width)
    children = upward.reshape(owned_parents, 8, right_sides, rank_width)
    parent_view = parent_transfer.reshape(owned_parents, rank_width, 8, rank_width)
    parent_up = jnp.einsum(
        "pcrb,pkcb->prk", children, parent_view, preferred_element_type=jnp.float32
    ).astype(jnp.bfloat16)
    flat_parent = parent_up.reshape(owned_parents, row_width)
    padded = padded_2(densities, ((("leaf", "sub"), 1),), reach_leaves * leaf_width)
    padded = padded.reshape(right_sides, owned_leaves + 2 * reach_leaves, leaf_width)
    local_index = near_source - (device_index * owned_leaves - reach_leaves)
    picked = jnp.take(padded, local_index, axis=1)
    picked = jnp.where(near_valid[None, :, :, None] == 1, picked, jnp.zeros((), jnp.bfloat16))
    picked = picked.reshape(right_sides, owned_leaves, -1)
    near_field = jnp.einsum("rtm,tmq->rtq", picked, near_blocks, preferred_element_type=jnp.float32)
    slot_source = leaf_source.reshape(-1)
    live_slots = leaf_valid.reshape(-1)
    slot_count = slot_source.shape[0]
    capacity = 2 * slot_count // shard_count
    peer_index = slot_source // owned_leaves
    member_leaf = slot_source - peer_index * owned_leaves
    onehot = (
        (peer_index[:, None] == jnp.arange(shard_count, dtype=jnp.int32)[None, :])
        & (live_slots[:, None] == 1)
    ).astype(jnp.int32)
    before = jnp.cumsum(onehot, axis=0) - onehot
    position = jnp.sum(before * onehot, axis=1)
    target_row = jnp.where(live_slots == 1, peer_index, shard_count)
    matches = (
        target_row[:, None, None] == jnp.arange(shard_count, dtype=jnp.int32)[None, :, None]
    ) & (position[:, None, None] == jnp.arange(capacity, dtype=jnp.int32)[None, None, :])
    requested = jnp.sum(jnp.where(matches, member_leaf[:, None, None], 0), axis=0)
    answer = jnp.take(
        flat_upward,
        lax.all_to_all(requested, ("leaf", "sub"), split_axis=0, concat_axis=0, tiled=True),
        axis=0,
    )
    answered = lax.all_to_all(answer, ("leaf", "sub"), split_axis=0, concat_axis=0, tiled=True)
    fetched = answered[
        jnp.where(live_slots == 1, peer_index, 0), jnp.where(live_slots == 1, position, 0)
    ]
    every_parent = lax.all_gather(flat_parent, ("leaf", "sub"), axis=0, tiled=True)
    fetched = jnp.where(live_slots[:, None] == 1, fetched, jnp.zeros((), jnp.bfloat16))
    fetched = fetched.reshape(owned_leaves, leaf_source.shape[1], right_sides, rank_width)
    leaf_view = leaf_coupling.reshape(owned_leaves, rank_width, leaf_source.shape[1], rank_width)
    leaf_far = jnp.einsum("tjrb,tajb->tra", fetched, leaf_view, preferred_element_type=jnp.float32)
    parent_far = couple_rows(
        every_parent, parent_source, parent_valid, parent_coupling, right_sides, rank_width
    )
    first_parent = group_index * (owned_grands * 8)
    own_transfer = lax.dynamic_slice_in_dim(
        grand_transfer, group_index * owned_grands, owned_grands, 0
    )
    group_parents = lax.dynamic_slice_in_dim(every_parent, first_parent, owned_grands * 8, 0)
    group_parents = group_parents.reshape(owned_grands, 8, right_sides, rank_width)
    own_view = own_transfer.reshape(owned_grands, rank_width, 8, rank_width)
    grand_up = jnp.einsum(
        "gcrb,gkcb->grk", group_parents, own_view, preferred_element_type=jnp.float32
    ).astype(jnp.bfloat16)
    every_grand = lax.all_gather(
        grand_up.reshape(owned_grands, row_width), "leaf", axis=0, tiled=True
    )
    grand_total = couple_rows(
        every_grand, grand_source, grand_valid, grand_coupling, right_sides, rank_width
    ).astype(jnp.bfloat16)
    down_view = own_transfer.reshape(owned_grands, rank_width, 8, rank_width)
    down_two = jnp.einsum(
        "grk,gkcb->gcrb", grand_total, down_view, preferred_element_type=jnp.float32
    )
    down_two = down_two.reshape(owned_grands * 8, right_sides, rank_width)
    down_two = lax.dynamic_slice_in_dim(
        down_two, device_index * owned_parents - first_parent, owned_parents, 0
    )
    parent_total = (parent_far + down_two).astype(jnp.bfloat16)
    down_one = jnp.einsum(
        "prk,pkcb->pcrb", parent_total, parent_view, preferred_element_type=jnp.float32
    )
    down_one = down_one.reshape(owned_leaves, right_sides, rank_width)
    leaf_total = (leaf_far + down_one).astype(jnp.bfloat16)
    far_field = jnp.einsum("trk,tkq->rtq", leaf_total, basis, preferred_element_type=jnp.float32)
    summed = (far_field + near_field).astype(jnp.bfloat16)
    return summed.reshape(right_sides, owned_leaves * leaf_width)


def solution(mesh):
    return jax.shard_map(
        body,
        mesh=mesh,
        in_specs=(
            P(None, ("leaf", "sub")),
            P(("leaf", "sub"), None, None),
            P(("leaf", "sub"), None, None),
            P(("leaf", "sub"), None),
            P(("leaf", "sub"), None),
            P(("leaf", "sub"), None, None),
            P(("leaf", "sub"), None),
            P(("leaf", "sub"), None),
            P(("leaf", "sub"), None, None),
            P(("leaf", "sub"), None, None),
            P(("leaf", "sub"), None),
            P(("leaf", "sub"), None),
            P(),
            P("leaf", None, None),
            P("leaf", None),
            P("leaf", None),
        ),
        out_specs=P(None, ("leaf", "sub")),
        check_vma=False,
    )
```

profile of v0, /device:TPU:1, one launch (start us, length us, event | category | flops | bytes accessed | tf_op | source)
XLA Modules:
  0.0 200.8 jit_solution(8929304993072695901)
XLA Ops:
  0.0 0.9 broadcast_compare_fusion
  0.9 0.1 eq.134
  1.0 0.1 eq.124
  1.1 0.8 reshape.499
  1.8 0.8 reshape.498
  2.6 0.1 copy.94
  2.8 0.1 copy.93
  2.9 0.3 fusion.54
  3.4 0.3 fusion.47
  3.7 0.1 iota_compare_fusion
  3.8 0.1 iota_compare_fusion.3
  3.9 1.6 select_reduce_fusion
  5.6 0.0 copy-start.11
  5.6 0.7 copy.96
  6.3 11.5 %all-to-all-start = ((s32[128,1,8]{2,1,0:T(1,128)}), s32[128,1,8]{2,1,0:T(1,128)S(1)}, u32[]{:S(2)}, u32[]{:S(2)}) async-start(s32[128,1,8]{2,1,0:T(1,128)} %copy.96), calls=%async_computation | async-start | bytes 131072 | tf_op jit(solution)/shard_map/all_to_all | solution.py:98
  17.9 0.6 fusion.113
  18.5 3.4 %collective-permute-start = (bf16[16,2048]{1,0:T(8,128)(2,1)}, bf16[16,2048]{1,0:T(8,128)(2,1)}, u32[]{:S(2)}, u32[]{:S(2)}) collective-permute-start(bf16[16,2048]{1,0:T(8,128)(2,1)} %get-tuple-element.9), channel_id=1, source_target_pairs={{0,1},{1,2},{2,3},{3,4},{4,5},{5,6},{6,7},{7,8},{8,9},{9,10},{10,1... | collective-permute-start | bytes 196616 | tf_op jit(solution)/shard_map/ppermute | solution.py:15
  21.9 3.9 %collective-permute-start.1 = (bf16[16,2048]{1,0:T(8,128)(2,1)}, bf16[16,2048]{1,0:T(8,128)(2,1)}, u32[]{:S(2)}, u32[]{:S(2)}) collective-permute-start(bf16[16,2048]{1,0:T(8,128)(2,1)} %get-tuple-element.10), channel_id=1, source_target_pairs={{1,0},{2,1},{3,2},{4,3},{5,4},{6,5},{7,6},{8,7},{9,8},{10,9},{11,1... | collective-permute-start | bytes 196616 | tf_op jit(solution)/shard_map/ppermute | solution.py:17
  25.9 0.2 reshape.506
  26.1 0.2 convolution_convert_fusion
  26.4 0.2 fusion.27
  26.6 0.1 reshape.561
  26.6 0.1 copy-done.3
  26.8 53.9 %all-gather = bf16[128,2,1024]{2,1,0:T(2,128)(2,1)S(1)} all-gather(bf16[1,2,1024]{2,1,0:T(2,128)(2,1)S(1)} %reshape.561), channel_id=1, replica_groups=mesh['leaf'=32,'sub'=4] {'leaf','sub'}, dimensions={0}, use_global_device_ids=true | all-gather | bytes 528384 | tf_op jit(solution)/shard_map/all_gather | solution.py:105
  80.7 0.2 reshape.562
  80.9 0.1 reshape.512
  81.0 0.1 reshape.510
  81.1 0.0 copy-start.6
  81.1 0.1 fusion.30
  81.3 0.1 reshape.563
  81.4 0.0 copy-done.12
  81.4 0.1 reshape.508
  81.6 22.5 %all-gather.1 = bf16[32,1,1024]{2,1,0:T(2,128)(2,1)S(1)} all-gather(bf16[1,1,1024]{2,1,0:T(2,128)(2,1)S(1)} %reshape.563), channel_id=1, replica_groups=mesh['leaf'=32,'sub'=4] {'leaf'}, dimensions={0}, use_global_device_ids=true | all-gather | bytes 67584 | tf_op jit(solution)/shard_map/all_gather | solution.py:123
  104.0 0.1 reshape.502
  104.1 0.1 eq.138
  104.2 0.1 reshape.503
  104.3 0.6 gather_fusion.3
  104.9 0.7 gather.33
  105.7 1.8 reshape.515
  107.5 0.7 gather_fusion.2
  108.2 0.9 gather.31
  109.1 2.1 %reshape.509 = bf16[2,64,32,64]{3,2,1,0:T(8,128)(2,1)} reshape(bf16[2,64,2048]{2,1,0:T(8,128)(2,1)S(1)} %copy-done.4) | data formatting | bytes 1048576 | tf_op jit(solution)/shard_map/reshape | solution.py:30
  111.2 12.9 %reshape.504 = bf16[16,64,32,64]{3,2,1,0:T(8,128)(2,1)} reshape(bf16[16,64,2048]{2,1,0:T(8,128)(2,1)} %param.21) | data formatting | bytes 8388608 | tf_op jit(solution)/shard_map/reshape | solution.py:108
  124.1 0.1 copy.107
  124.2 0.1 reshape.552
  124.3 0.1 copy.106
  124.3 0.1 broadcast_in_dim.147
  124.5 0.1 copy.105
  124.6 0.1 broadcast_in_dim.144
  124.7 0.1 reshape.522
  124.8 5.4 %gather_fusion = bf16[1024,1024]{1,0:T(8,128)(2,1)} fusion(bf16[16,1024]{1,0:T(8,128)(2,1)S(1)} %reshape.502, s32[1024]{0:T(1024)S(1)} %broadcast_clamp_fusion), kind=kCustom, calls=%fused_computation | custom fusion | bytes 4198400 | tf_op jit(solution)/shard_map/jit(_take)/gather | solution.py:96
  130.2 3.2 %bitcast_select_fusion = bf16[128,8,1024]{2,1,0:T(8,128)(2,1)} fusion(bf16[1024,1024]{1,0:T(8,128)(2,1)} %gather_fusion, pred[128,8]{1,0:T(8,128)(4,1)S(1)} %compare_and_fusion), kind=kLoop, calls=%fused_computation.7 | loop fusion | flops 1048576 | bytes 4195328 | tf_op jit(solution)/shard_map/jit(_take)/select_n | solution.py:96
  133.4 5.7 %all-to-all-start.1 = ((bf16[128,8,1024]{2,1,0:T(8,128)(2,1)}), bf16[128,8,1024]{2,1,0:T(8,128)(2,1)}, u32[]{:S(2)}, u32[]{:S(2)}) async-start(bf16[128,8,1024]{2,1,0:T(8,128)(2,1)} %bitcast_select_fusion), calls=%async_computation.1 | async-start | bytes 4194304 | tf_op jit(solution)/shard_map/all_to_all | solution.py:101
  139.3 1.4 fusion.43
  140.6 2.3 %fusion.41 = f32[2,16,8,64]{3,1,2,0:T(8,128)} fusion(bf16[2,64,32,64]{3,2,1,0:T(8,128)(2,1)S(1)} %copy-done.2, bf16[2,32,16,64]{3,2,1,0:T(8,128)(2,1)} %gather.31, pred[2,32]{1,0:T(4,128)(4,1)S(1)} %get-tuple-element.11, pred[2,32]{1,0:T(4,128)(4,1)S(1)} %get-tuple-element.12, bf16[2,64,8,64]{3,2,1,0:T(8,128)(2,1)} %copy-done.3, ...), kind=kOutput, calls=%fused_computation.36 | convolution fusion | flops 10620928 | bytes 1393668 | tf_op jit(solution)/shard_map/prk,pkcb->pcrb/dot_general | solution.py:138
  143.0 0.9 pad_maximum_fusion
  143.9 1.7 gather_fusion.4
  145.6 1.3 copy.118
  146.9 22.7 %all-to-all-done.1 = bf16[128,8,1024]{2,1,0:T(8,128)(2,1)} async-done(((bf16[128,8,1024]{2,1,0:T(8,128)(2,1)}), bf16[128,8,1024]{2,1,0:T(8,128)(2,1)}, u32[]{:S(2)}, u32[]{:S(2)}) %all-to-all-start.1) | async-done | bytes 2097184 | tf_op jit(solution)/shard_map/all_to_all | solution.py:101
  169.6 10.8 %gather_fusion.1 = bf16[512,1024]{1,0:T(8,128)(2,1)} fusion(bf16[128,8,1024]{2,1,0:T(8,128)(2,1)} %all-to-all-done.1, s32[512]{0:T(512)S(1)} %bitcast.121), kind=kCustom, calls=%fused_computation.1 | custom fusion | bytes 2101248 | tf_op jit(solution)/shard_map/gather | solution.py:102
  180.4 4.1 %gather.29 = bf16[16,32,16,64]{3,2,1,0:T(8,128)(2,1)} reshape(bf16[512,1024]{1,0:T(8,128)(2,1)} %gather_fusion.1) | data formatting | bytes 2097152 | tf_op jit(solution)/shard_map/gather | solution.py:102
  184.5 7.6 %fusion.23 = f32[16,16,256]{2,1,0:T(8,128)} fusion(bf16[16,64,256]{2,1,0:T(8,128)(2,1)} %param.17, f32[16,16,64]{2,1,0:T(8,128)S(1)} %bitcast.140, bf16[16,64,32,64]{3,2,1,0:T(8,128)(2,1)} %reshape.504, bf16[16,32,16,64]{3,2,1,0:T(8,128)(2,1)} %gather.29, pred[16,32]{1,0:T(8,128)(4,1)S(1)} %broadcast_compare_fusion), kind=kOutput, calls=%fused_computation.17 | convolution fusion | flops 76054528 | bytes 6095360 | tf_op jit(solution)/shard_map/trk,tkq->rtq/dot_general | solution.py:143
  192.1 8.1 %fusion.5 = bf16[16,2,8,256]{3,2,1,0:T(8,128)(2,1)S(1)} fusion(f32[16,16,256]{2,1,0:T(8,128)} %fusion.23, bf16[16,2048,256]{2,1,0:T(8,128)(2,1)} %param.18, bf16[16,16,2048]{2,0,1:T(8,128)(2,1)S(1)} %bitcast.123, pred[16,2048]{1,0:T(8,128)(4,1)S(1)} %bitcast.133, pred[16,2048]{1,0:T(8,128)(4,1)S(1)} %bitcast.134), kind=kOutput, calls=%fused_computation.13 | convolution fusion | flops 269615104 | bytes 18284544 | tf_op jit(solution)/shard_map/rtm,tmq->rtq/dot_general | solution.py:78
  200.1 0.7 copy.119
  (62 shorter events, 0.4 us)
Async XLA Ops:
  0.0 81.0 %copy-start = (bf16[32,64,512]{2,1,0:T(8,128)(2,1)S(1)}, bf16[32,64,512]{2,1,0:T(8,128)(2,1)}, u32[]{:S(2)}) copy-start(bf16[32,64,512]{2,1,0:T(8,128)(2,1)} %param.28) | copy-start | bytes 6291460
  0.0 17.9 %copy-start.1 = (bf16[16,4096]{1,0:T(8,128)(2,1)S(1)}, bf16[16,4096]{1,0:T(8,128)(2,1)}, u32[]{:S(2)}) copy-start(bf16[16,4096]{1,0:T(8,128)(2,1)} %param.16) | copy-start | bytes 393220
  0.0 25.9 %copy-start.14 = (s32[1,16]{1,0:T(1,128)S(1)}, s32[1,16]{1,0:T(1,128)}, u32[]{:S(2)}) copy-start(s32[1,16]{1,0:T(1,128)} %param.30) | copy-start | bytes 196
  0.0 25.9 %copy-start.7 = (bf16[2,64,512]{2,1,0:T(8,128)(2,1)S(1)}, bf16[2,64,512]{2,1,0:T(8,128)(2,1)}, u32[]{:S(2)}) copy-start(bf16[2,64,512]{2,1,0:T(8,128)(2,1)} %param.24) | copy-start | bytes 393220
  0.0 26.1 %copy-start.5 = (bf16[16,64,256]{2,1,0:T(8,128)(2,1)S(1)}, bf16[16,64,256]{2,1,0:T(8,128)(2,1)}, u32[]{:S(2)}) copy-start(bf16[16,64,256]{2,1,0:T(8,128)(2,1)} %param.17) | copy-start | bytes 1572868
  5.6 75.8 %copy-start.12 = (s32[2,32]{1,0:T(2,128)S(1)}, s32[2,32]{1,0:T(2,128)}, u32[]{:S(2)}) copy-start(s32[2,32]{1,0:T(2,128)} %param.26) | copy-start | bytes 772
  5.6 75.9 %copy-start.10 = (s32[16,8]{0,1:T(8,128)S(1)}, s32[16,8]{0,1:T(8,128)}, u32[]{:S(2)}) copy-start(s32[16,8]{0,1:T(8,128)} %param.20) | copy-start | bytes 1540
  5.6 75.9 %copy-start.11 = (s32[16,8]{0,1:T(8,128)S(1)}, s32[16,8]{0,1:T(8,128)}, u32[]{:S(2)}) copy-start(s32[16,8]{0,1:T(8,128)} %param.19) | copy-start | bytes 1540
  6.3 118.3 %all-to-all-start = ((s32[128,1,8]{2,1,0:T(1,128)}), s32[128,1,8]{2,1,0:T(1,128)S(1)}, u32[]{:S(2)}, u32[]{:S(2)}) async-start(s32[128,1,8]{2,1,0:T(1,128)} %copy.96), calls=%async_computation | async-start | bytes 131072 | tf_op jit(solution)/shard_map/all_to_all | solution.py:98
  17.9 86.4 %copy-start.8 = (s32[16,32]{1,0:T(8,128)S(1)}, s32[16,32]{1,0:T(8,128)}, u32[]{:S(2)}) copy-start(s32[16,32]{1,0:T(8,128)} %param.22) | copy-start | bytes 6148
  18.5 124.4 %collective-permute-start = (bf16[16,2048]{1,0:T(8,128)(2,1)}, bf16[16,2048]{1,0:T(8,128)(2,1)}, u32[]{:S(2)}, u32[]{:S(2)}) collective-permute-start(bf16[16,2048]{1,0:T(8,128)(2,1)} %get-tuple-element.9), channel_id=1, source_target_pairs={{0,1},{1,2},{2,3},{3,4},{4,5},{5,6},{6,7},{7,8},{8,9},{9,10},{10,1... | collective-permute-start | bytes 196616 | tf_op jit(solution)/shard_map/ppermute | solution.py:15
  21.9 121.0 %collective-permute-start.1 = (bf16[16,2048]{1,0:T(8,128)(2,1)}, bf16[16,2048]{1,0:T(8,128)(2,1)}, u32[]{:S(2)}, u32[]{:S(2)}) collective-permute-start(bf16[16,2048]{1,0:T(8,128)(2,1)} %get-tuple-element.10), channel_id=1, source_target_pairs={{1,0},{2,1},{3,2},{4,3},{5,4},{6,5},{7,6},{8,7},{9,8},{10,9},{11,1... | collective-permute-start | bytes 196616 | tf_op jit(solution)/shard_map/ppermute | solution.py:17
  26.1 0.7 copy-start.3
  81.1 23.1 %copy-start.6 = (bf16[64,8,64]{2,1,0:T(8,128)(2,1)}, bf16[64,8,64]{2,1,0:T(8,128)(2,1)S(1)}, u32[]{:S(2)}) copy-start(bf16[64,8,64]{2,1,0:T(8,128)(2,1)S(1)} %reshape.510) | copy-start | bytes 196612
  104.9 4.2 %copy-start.4 = (bf16[2,64,2048]{2,1,0:T(8,128)(2,1)S(1)}, bf16[2,64,2048]{2,1,0:T(8,128)(2,1)}, u32[]{:S(2)}) copy-start(bf16[2,64,2048]{2,1,0:T(8,128)(2,1)} %param.25) | copy-start | bytes 1572868
  133.4 5.7 %copy-start.15 = (s32[1,16]{1,0:T(1,128)S(1)}, s32[1,16]{1,0:T(1,128)}, u32[]{:S(2)}) copy-start(s32[1,16]{1,0:T(1,128)} %param.31) | copy-start | bytes 196
  133.4 5.8 %copy-start.13 = (s32[2,32]{1,0:T(2,128)S(1)}, s32[2,32]{1,0:T(2,128)}, u32[]{:S(2)}) copy-start(s32[2,32]{1,0:T(2,128)} %param.27) | copy-start | bytes 772
  133.4 5.8 %copy-start.9 = (bf16[16,16,64]{2,1,0:T(8,128)(2,1)S(1)}, bf16[16,16,64]{2,1,0:T(8,128)(2,1)}, u32[]{:S(2)}) copy-start(bf16[16,16,64]{2,1,0:T(8,128)(2,1)} %gather.33) | copy-start | bytes 98308
  133.4 7.2 %copy-start.2 = (bf16[2,64,32,64]{3,2,1,0:T(8,128)(2,1)S(1)}, bf16[2,64,32,64]{3,2,1,0:T(8,128)(2,1)}, u32[]{:S(2)}) copy-start(bf16[2,64,32,64]{3,2,1,0:T(8,128)(2,1)} %reshape.509) | copy-start | bytes 1572868
  133.4 36.2 %all-to-all-start.1 = ((bf16[128,8,1024]{2,1,0:T(8,128)(2,1)}), bf16[128,8,1024]{2,1,0:T(8,128)(2,1)}, u32[]{:S(2)}, u32[]{:S(2)}) async-start(bf16[128,8,1024]{2,1,0:T(8,128)(2,1)} %bitcast_select_fusion), calls=%async_computation.1 | async-start | bytes 4194304 | tf_op jit(solution)/shard_map/all_to_all | solution.py:101
  180.4 4.1 %copy-start.16 = (f32[2,16,8,64]{3,1,2,0:T(8,128)S(1)}, f32[2,16,8,64]{3,1,2,0:T(8,128)}, u32[]{:S(2)}) copy-start(f32[2,16,8,64]{3,1,2,0:T(8,128)} %fusion.41) | copy-start | bytes 196612
where the time goes:
time: 202 us; the launch traced here: 201 us
  blocking collectives  76.3 us (38%)
  local copies, waits for them, and re-layouts  49.2 us (24%)
  starting transfers between devices  24.5 us (12%)
  waiting for transfers between devices  22.7 us (11%)
  matrix products  19.9 us (10%)
  other arithmetic  7.71 us (4%)
    all_gather x1, blocking collectives, body(): lax.all_gather(flat_parent, ('leaf', 'sub'), axis=0, tiled=True)  53.9 us
    all_to_all x1, waiting for transfers between devices, body(): lax.all_to_all(answer, ('leaf', 'sub'), split_axis=0, concat_axis=0, tile...  22.7 us
    all_gather x1, blocking collectives, body(): lax.all_gather(grand_up.reshape(owned_grands, row_width), 'leaf', axis=0,...  22.5 us
    gather x2, local copies, waits for them, and re-layouts, body(): answered[jnp.where(live_slots == 1, peer_index, 0), jnp.where(live_slots...  14.9 us
    reshape x1, local copies, waits for them, and re-layouts, body(): leaf_coupling.reshape(owned_leaves, rank_width, leaf_source.shape[1], ran...  12.9 us
    all_to_all x1, starting transfers between devices, body(): lax.all_to_all(requested, ('leaf', 'sub'), split_axis=0, concat_axis=0, t...  11.5 us
    dot_general x1, matrix products, body(): jnp.einsum('rtm,tmq->rtq', picked, near_blocks, preferred_element_type=jn...  8.07 us
    dot_general x1, matrix products, body(): jnp.einsum('trk,tkq->rtq', leaf_total, basis, preferred_element_type=jnp....  7.59 us
  transfers between devices with their start and end apart: 4, of which 1 were waited for; matrix products, arithmetic and copies ran while one was open for 19% of the time, Pallas kernels for 0%

commit v1 on v0

v1 whole, which is shorter than its diff:
```python
import jax
import jax.numpy as jnp
from jax import lax
from jax.experimental import pallas as pl
from jax.experimental.pallas import tpu as pltpu
from jax.sharding import Mesh, PartitionSpec as P

AXES = ("x", "y", "c", "z")
BF16, F32 = jnp.bfloat16, jnp.float32
TILES = 9
VMEM_LIMIT = 50 * 1024 * 1024


def flat_index(x, y, c, z):
    return ((x * 4 + y) * 2 + c) * 4 + z


def pairs_of(move):
    return [
        (flat_index(x, y, c, z), flat_index(*move(x, y, c, z)))
        for x in range(4)
        for y in range(4)
        for c in range(2)
        for z in range(4)
    ]


def dot_t(a, b):
    return lax.dot_general(a, b, (((1,), (1,)), ((), ())), preferred_element_type=F32)


def dot(a, b):
    return lax.dot_general(a, b, (((1,), (0,)), ((), ())), preferred_element_type=F32)


def up_kernel(dens_ref, basis_ref, pt_ref, out_ref):
    tiles = []
    for i in range(8):
        pair = [
            dot_t(dens_ref[:, t * 256 : (t + 1) * 256], basis_ref[t]).astype(BF16)
            for t in (2 * i, 2 * i + 1)
        ]
        tile = jnp.concatenate(pair, axis=1)
        out_ref[i] = tile
        tiles.append(tile)
    pair = [
        dot_t(jnp.concatenate(tiles[4 * p : 4 * p + 4], axis=1), pt_ref[p]).astype(BF16)
        for p in range(2)
    ]
    out_ref[8] = jnp.concatenate(pair, axis=1)


def near_kernel(idx_ref, left_ref, dens_ref, right_ref, blocks_ref, out_ref, padded):
    t = pl.program_id(0)

    @pl.when(t == 0)
    def _():
        for i in range(8):
            padded[i] = left_ref[:, i * 256 : (i + 1) * 256]
            padded[24 + i] = right_ref[:, i * 256 : (i + 1) * 256]
        for i in range(16):
            padded[8 + i] = dens_ref[:, i * 256 : (i + 1) * 256]
        padded[32] = jnp.zeros((16, 256), BF16)

    picked = jnp.concatenate([padded[idx_ref[t * 8 + j]] for j in range(8)], axis=1)
    out_ref[...] = dot(picked, blocks_ref[0])


def down_kernel(
    leaf_ref, parent_ref, grand_ref, own_ref,
    p0, p1, p2, p3, p4, p5, p6, p7,
    lc_hbm, pc_hbm, gc_hbm, gt_hbm, pt_ref, basis_ref, near_ref,
    out_ref,
    table, lc, pc, gc, gt, picked, leaf_far, sems,
):
    pieces = (p0, p1, p2, p3, p4, p5, p6, p7)
    copies = [
        pltpu.make_async_copy(p, table.at[pl.ds(k * 144, 144)], sems.at[k])
        for k, p in enumerate(pieces)
    ]
    others = [
        pltpu.make_async_copy(a, b, sems.at[8 + k])
        for k, (a, b) in enumerate(((gt_hbm, gt), (gc_hbm, gc), (pc_hbm, pc), (lc_hbm, lc)))
    ]
    for copy in copies + others:
        copy.start()
    table[1152] = jnp.zeros((16, 128), BF16)
    low = lax.broadcasted_iota(jnp.int32, (16, 128), 1) < 64
    for copy in copies:
        copy.wait()

    def pair_tile(ref, at):
        halves = []
        for k in range(2):
            code = ref[at + k]
            tile = table[code // 2].astype(F32)
            halves.append(pltpu.roll(tile, (code % 2) * 64, 1))
        return jnp.where(low, halves[0], halves[1]).astype(BF16)

    others[0].wait()
    ups = []
    for j in range(16):
        children = jnp.concatenate([table[grand_ref[j * 5 + 1 + z]] for z in range(4)], axis=1)
        ups.append(dot_t(children, gt[grand_ref[j * 5]]).astype(BF16))
    others[1].wait()
    grand_total = dot_t(jnp.concatenate(ups, axis=1), gc[0]).astype(BF16)
    down_two = dot(grand_total, gt[own_ref[0], :, pl.ds(pl.multiple_of(own_ref[1] * 128, 128), 128)])

    others[2].wait()
    down_one = []
    for p in range(2):
        coefs = jnp.concatenate([pair_tile(parent_ref, p * 32 + 2 * i) for i in range(16)], axis=1)
        far = dot_t(coefs, pc[p])
        total = (far + down_two[:, p * 64 : (p + 1) * 64]).astype(BF16)
        down_one.append(dot(total, pt_ref[p]))

    def gather(t, carry):
        for i in range(16):
            picked[t, :, i * 128 : (i + 1) * 128] = pair_tile(leaf_ref, t * 32 + 2 * i)
        return carry

    lax.fori_loop(0, 16, gather, 0)
    others[3].wait()
    for t in range(16):
        far = dot_t(picked[t], lc[t])
        total = (far + down_one[t // 8][:, (t % 8) * 64 : (t % 8 + 1) * 64]).astype(BF16)
        cols = slice(t * 256, (t + 1) * 256)
        out_ref[:, cols] = (dot(total, basis_ref[t]) + near_ref[:, cols]).astype(BF16)


def gather_z(v):
    step = lax.ppermute(v, "z", [(i, i ^ 1) for i in range(4)])
    v = jnp.concatenate([v, step], axis=0)
    step = lax.ppermute(v, "z", [(i, i ^ 3) for i in range(4)])
    return jnp.concatenate([v, step], axis=0)


def shift_plane(v, k, y_core):
    return lax.ppermute(
        v,
        AXES,
        pairs_of(
            lambda x, y, c, z: (x, (y + k) % 4, c, z) if c == y_core else ((x + k) % 4, y, c, z)
        ),
    )


def body(
    densities, basis, near_blocks, near_source, near_valid, leaf_coupling, leaf_source, leaf_valid,
    parent_transfer, parent_coupling, parent_source, parent_valid, grand_transfer, grand_coupling,
    grand_source, grand_valid,
):
    mx, my, mc, mz = (lax.axis_index(a) for a in AXES)
    me = lax.axis_index(AXES)

    def block_tile(device):
        z, c, y, x = device % 4, device // 4 % 2, device // 8 % 4, device // 32
        w = z ^ mz
        kz = w ^ (w >> 1)
        ky, kx = (my - y) % 4, (mx - x) % 4
        block = jnp.where(c == 0, kx * 16 + ky * 4, ky * 16 + kx * 4) + kz
        return (jnp.where(c == mc, 0, 64) + block) * TILES

    slot = jnp.arange(32, dtype=jnp.int32)
    leaf_code = (block_tile(leaf_source // 16) + leaf_source % 16 // 2) * 2 + (leaf_source + slot) % 2
    leaf_code = jnp.where(leaf_valid == 1, leaf_code, 1152 * 2).reshape(-1)
    parent_code = (block_tile(parent_source // 2) + 8) * 2 + (parent_source + slot) % 2
    parent_code = jnp.where(parent_valid == 1, parent_code, 1152 * 2).reshape(-1)
    grand_tiles = block_tile(grand_source[0][:, None] * 4 + jnp.arange(4, dtype=jnp.int32)) + 8
    grand_tiles = jnp.where(grand_valid[0][:, None] == 1, grand_tiles, 1152)
    grand_code = jnp.concatenate([grand_source[0][:, None], grand_tiles], axis=1).reshape(-1)
    own = jnp.stack([me // 4, mz]).astype(jnp.int32)
    near_code = jnp.where(near_valid == 1, near_source - (me * 16 - 8), 32).reshape(-1)

    coefs = pl.pallas_call(
        up_kernel,
        out_shape=jax.ShapeDtypeStruct((TILES, 16, 128), BF16),
        compiler_params=pltpu.CompilerParams(vmem_limit_bytes=VMEM_LIMIT),
        name="upward",
    )(densities, basis, parent_transfer)

    coefs = gather_z(coefs)
    coefs = jnp.concatenate([coefs] + [shift_plane(coefs, k, 0) for k in (1, 2, 3)], axis=0)
    pieces = [coefs] + [shift_plane(coefs, k, 1) for k in (1, 2, 3)]
    other = [lax.ppermute(p, "c", [(0, 1), (1, 0)]) for p in pieces]

    left = lax.ppermute(densities[:, 2048:], AXES, [(i, i + 1) for i in range(127)])
    right = lax.ppermute(densities[:, :2048], AXES, [(i + 1, i) for i in range(127)])
    near = pl.pallas_call(
        near_kernel,
        out_shape=jax.ShapeDtypeStruct((16, 4096), F32),
        grid_spec=pltpu.PrefetchScalarGridSpec(
            num_scalar_prefetch=1,
            grid=(16,),
            in_specs=[
                pl.BlockSpec((16, 2048), lambda t, i: (0, 0)),
                pl.BlockSpec((16, 4096), lambda t, i: (0, 0)),
                pl.BlockSpec((16, 2048), lambda t, i: (0, 0)),
                pl.BlockSpec((1, 2048, 256), lambda t, i: (t, 0, 0)),
            ],
            out_specs=pl.BlockSpec((16, 256), lambda t, i: (0, t)),
            scratch_shapes=[pltpu.VMEM((33, 16, 256), BF16)],
        ),
        compiler_params=pltpu.CompilerParams(vmem_limit_bytes=VMEM_LIMIT),
        cost_estimate=pl.CostEstimate(
            flops=2 * 16 * 16 * 2048 * 256, bytes_accessed=17_500_000, transcendentals=0
        ),
        name="near",
    )(near_code, left, densities, right, near_blocks)

    anywhere = pl.BlockSpec(memory_space=pl.ANY)
    vmem = pl.BlockSpec(memory_space=pltpu.VMEM)
    smem = pl.BlockSpec(memory_space=pltpu.SMEM)
    return pl.pallas_call(
        down_kernel,
        out_shape=jax.ShapeDtypeStruct((16, 4096), BF16),
        in_specs=[smem] * 4 + [anywhere] * 12 + [vmem] * 3,
        out_specs=vmem,
        scratch_shapes=[
            pltpu.VMEM((1153, 16, 128), BF16),
            pltpu.VMEM((16, 64, 2048), BF16),
            pltpu.VMEM((2, 64, 2048), BF16),
            pltpu.VMEM((1, 64, 1024), BF16),
            pltpu.VMEM((32, 64, 512), BF16),
            pltpu.VMEM((16, 16, 2048), BF16),
            pltpu.VMEM((16, 16, 64), F32),
            pltpu.SemaphoreType.DMA((12,)),
        ],
        compiler_params=pltpu.CompilerParams(vmem_limit_bytes=VMEM_LIMIT),
        name="downward",
    )(
        leaf_code, parent_code, grand_code, own, *pieces, *other,
        leaf_coupling, parent_coupling, grand_coupling, grand_transfer, parent_transfer, basis, near,
    )


def solution(mesh):
    grid = Mesh(mesh.devices.reshape(4, 4, 2, 4), AXES)
    leaf, both = ("x", "y", "c"), AXES
    row, cube = P(both, None), P(both, None, None)
    return jax.shard_map(
        body,
        mesh=grid,
        in_specs=(
            P(None, both), cube, cube, row, row, cube, row, row, cube, cube, row, row, P(),
            P(leaf, None, None), P(leaf, None), P(leaf, None),
        ),
        out_specs=P(None, both),
        check_vma=False,
    )
```

time: 202 us -> 87.6 us (0.43)
  blocking collectives: 76.3 us -> 0 us
  local copies, waits for them, and re-layouts: 49.2 us -> 5.79 us
  Pallas kernels: 0 us -> 27.8 us
  matrix products: 19.9 us -> 0 us
  starting transfers between devices: 24.5 us -> 32 us
  waiting for transfers between devices: 22.7 us -> 17.4 us
  other arithmetic: 7.71 us -> 3.83 us
    all_gather x2 -> x0, blocking collectives: 76.3 us -> none  [the longest x1 53.9 us: body(): lax.all_gather(flat_parent, ('leaf', 'sub'), axis=0, tiled=True)]
    pallas_call x0 -> x3, Pallas kernels: none -> 27.8 us  [the longest x1 14 us: body(): pl.pallas_call(down_kernel, out_shape=jax.ShapeDtypeStruct((16, 4096), BF...]
    gather x9 -> x0, local copies, waits for them, and re-layouts: 26.2 us -> none  [the longest x2 14.9 us: body(): answered[jnp.where(live_slots == 1, peer_index, 0), jnp.where(live_slots...]
    ppermute x2 -> x14, starting transfers between devices: 7.32 us -> 32 us  [the longest x4 13.1 us: body(): other = [lax.ppermute(p, 'c', [(0, 1), (1, 0)]) for p in pieces]]
    all_to_all x2 -> x0, waiting for transfers between devices: 22.7 us -> none  [the longest x1 22.7 us: body(): lax.all_to_all(answer, ('leaf', 'sub'), split_axis=0, concat_axis=0, tile...]
    dot_general x7 -> x0, matrix products: 19.9 us -> none  [the longest x1 8.07 us: body(): jnp.einsum('rtm,tmq->rtq', picked, near_blocks, preferred_element_type=jn...]
    ppermute x2 -> x14, waiting for transfers between devices: 0.01 us -> 17.4 us  [the longest x6 8.66 us: shift_plane(): lax.ppermute(v, AXES, pairs_of(lambda x, y, c, z: (x, (y + k) % 4, c, z)...]
    reshape x10 -> x4, local copies, waits for them, and re-layouts: 17.7 us -> 0.34 us  [the longest x1 0.09 us: body(): jnp.concatenate([grand_source[0][:, None], grand_tiles], axis=1).reshape(-1)]
  transfers between devices with their start and end apart: 4 -> 14, of which waited for: 1 -> 5; matrix products, arithmetic and copies ran while one was open for 19% -> 6% of each run, Pallas kernels for 0% -> 15%
where the time goes in v1:
time: 87.6 us; the launch traced here: 87 us
  starting transfers between devices  32 us (37%)
  Pallas kernels  27.8 us (32%)
  waiting for transfers between devices  17.4 us (20%)
  local copies, waits for them, and re-layouts  5.79 us (7%)
  other arithmetic  3.83 us (4%)
    pallas_call x1, Pallas kernels, body(): pl.pallas_call(down_kernel, out_shape=jax.ShapeDtypeStruct((16, 4096), BF...  14 us
    pallas_call x1, Pallas kernels, body(): pl.pallas_call(near_kernel, out_shape=jax.ShapeDtypeStruct((16, 4096), F3...  13.3 us
    ppermute x4, starting transfers between devices, body(): other = [lax.ppermute(p, 'c', [(0, 1), (1, 0)]) for p in pieces]  13.1 us
    ppermute x6, starting transfers between devices, shift_plane(): lax.ppermute(v, AXES, pairs_of(lambda x, y, c, z: (x, (y + k) % 4, c, z)...  8.94 us
    ppermute x6, waiting for transfers between devices, shift_plane(): lax.ppermute(v, AXES, pairs_of(lambda x, y, c, z: (x, (y + k) % 4, c, z)...  8.66 us
    ppermute x1, starting transfers between devices, body(): lax.ppermute(densities[:, :2048], AXES, [(i + 1, i) for i in range(127)])  4.99 us
    ppermute x1, waiting for transfers between devices, body(): lax.ppermute(densities[:, 2048:], AXES, [(i, i + 1) for i in range(127)])  4.79 us
    unnamed x23, local copies, waits for them, and re-layouts  4.61 us
  transfers between devices with their start and end apart: 14, of which 5 were waited for; matrix products, arithmetic and copies ran while one was open for 6% of the time, Pallas kernels for 15%

profile of v1, /device:TPU:1, one launch (start us, length us, event | category | flops | bytes accessed | tf_op | source)
XLA Modules:
  0.0 87.0 jit_solution(6096662551725740227)
XLA Ops:
  0.0 0.0 copy-start
  0.0 1.0 %copy-done = bf16[16,64,256]{2,1,0:T(8,128)(2,1)S(1)} copy-done((bf16[16,64,256]{2,1,0:T(8,128)(2,1)S(1)}, bf16[16,64,256]{2,1,0:T(8,128)(2,1)}, u32[]{:S(2)}) %copy-start) | copy-done | bytes 524312
  1.0 0.0 copy-start.2
  1.0 0.9 %copy-done.2 = bf16[16,4096]{1,0:T(8,128)(2,1)S(1)} copy-done((bf16[16,4096]{1,0:T(8,128)(2,1)S(1)}, bf16[16,4096]{1,0:T(8,128)(2,1)}, u32[]{:S(2)}) %copy-start.2) | copy-done | bytes 131096
  1.9 0.0 copy-start.4
  1.9 0.9 %copy-done.4 = bf16[2,64,512]{2,1,0:T(8,128)(2,1)S(1)} copy-done((bf16[2,64,512]{2,1,0:T(8,128)(2,1)S(1)}, bf16[2,64,512]{2,1,0:T(8,128)(2,1)}, u32[]{:S(2)}) %copy-start.4) | copy-done | bytes 131096
  2.9 0.5 upward.1
  3.3 2.5 %collective-permute-start = (bf16[9,16,128]{2,1,0:T(8,128)(2,1)S(1)}, bf16[9,16,128]{2,1,0:T(8,128)(2,1)S(1)}, u32[]{:S(2)}, u32[]{:S(2)}) collective-permute-start(bf16[9,16,128]{2,1,0:T(8,128)(2,1)S(1)} %upward.1), channel_id=1, source_target_pairs={{0,1},{1,0},{2,3},{3,2},{4,5},{5,4},{6,7},{7,6},{8,9},{9,8},{10,11... | collective-permute-start | bytes 110600 | tf_op jit(solution)/shard_map/ppermute | solution.py:132
  5.8 5.0 %collective-permute-start.13 = (bf16[16,2048]{1,0:T(8,128)(2,1)S(1)}, bf16[16,2048]{1,0:T(8,128)(2,1)S(1)}, u32[]{:S(2)}, u32[]{:S(2)}) collective-permute-start(bf16[16,2048]{1,0:T(8,128)(2,1)S(1)} %get-tuple-element.5), channel_id=1, source_target_pairs={{1,0},{2,1},{3,2},{4,3},{5,4},{6,5},{7,6},{8,7},{9,8},{10,9},{11,1... | collective-permute-start | bytes 196616 | tf_op jit(solution)/shard_map/ppermute | solution.py:188
  10.8 0.7 compare_select_fusion.12
  11.6 0.1 reshape.31.parent_ref
  11.7 0.0 collective-permute-done
  11.7 0.6 collective-permute-start.1
  12.3 3.9 %collective-permute-done.1 = bf16[18,16,128]{2,1,0:T(8,128)(2,1)S(1)} collective-permute-done((bf16[18,16,128]{2,1,0:T(8,128)(2,1)S(1)}, bf16[18,16,128]{2,1,0:T(8,128)(2,1)S(1)}, u32[]{:S(2)}, u32[]{:S(2)}) %collective-permute-start.1) | collective-permute-done | bytes 73760 | tf_op jit(solution)/shard_map/ppermute | solution.py:134
  16.3 1.2 %collective-permute-start.2 = (bf16[36,16,128]{2,1,0:T(8,128)(2,1)S(1)}, bf16[36,16,128]{2,1,0:T(8,128)(2,1)S(1)}, u32[]{:S(2)}, u32[]{:S(2)}) collective-permute-start(bf16[36,16,128]{2,1,0:T(8,128)(2,1)S(1)} %pad_maximum_fusion), channel_id=1, source_target_pairs={{0,8},{1,9},{2,10},{3,11},{4,36},{5,37},{6,38},{7,39},{8,16},{9,17... | collective-permute-start | bytes 442376 | tf_op jit(solution)/shard_map/ppermute | solution.py:139
  17.5 1.5 %collective-permute-start.4 = (bf16[36,16,128]{2,1,0:T(8,128)(2,1)S(1)}, bf16[36,16,128]{2,1,0:T(8,128)(2,1)S(1)}, u32[]{:S(2)}, u32[]{:S(2)}) collective-permute-start(bf16[36,16,128]{2,1,0:T(8,128)(2,1)S(1)} %pad_maximum_fusion), channel_id=1, source_target_pairs={{0,24},{1,25},{2,26},{3,27},{4,100},{5,101},{6,102},{7,103},{8,0},... | collective-permute-start | bytes 442376 | tf_op jit(solution)/shard_map/ppermute | solution.py:139
  19.0 1.5 %collective-permute-start.3 = (bf16[36,16,128]{2,1,0:T(8,128)(2,1)S(1)}, bf16[36,16,128]{2,1,0:T(8,128)(2,1)S(1)}, u32[]{:S(2)}, u32[]{:S(2)}) collective-permute-start(bf16[36,16,128]{2,1,0:T(8,128)(2,1)S(1)} %pad_maximum_fusion), channel_id=1, source_target_pairs={{0,16},{1,17},{2,18},{3,19},{4,68},{5,69},{6,70},{7,71},{8,24},{9,... | collective-permute-start | bytes 442376 | tf_op jit(solution)/shard_map/ppermute | solution.py:139
  20.5 1.0 %collective-permute-done.2 = bf16[36,16,128]{2,1,0:T(8,128)(2,1)S(1)} collective-permute-done((bf16[36,16,128]{2,1,0:T(8,128)(2,1)S(1)}, bf16[36,16,128]{2,1,0:T(8,128)(2,1)S(1)}, u32[]{:S(2)}, u32[]{:S(2)}) %collective-permute-start.2) | collective-permute-done | bytes 147488 | tf_op jit(solution)/shard_map/ppermute | solution.py:139
  21.6 3.0 %collective-permute-done.3 = bf16[36,16,128]{2,1,0:T(8,128)(2,1)S(1)} collective-permute-done((bf16[36,16,128]{2,1,0:T(8,128)(2,1)S(1)}, bf16[36,16,128]{2,1,0:T(8,128)(2,1)S(1)}, u32[]{:S(2)}, u32[]{:S(2)}) %collective-permute-start.3) | collective-permute-done | bytes 147488 | tf_op jit(solution)/shard_map/ppermute | solution.py:139
  24.5 0.0 collective-permute-done.4
  24.6 4.0 %collective-permute-start.7 = (bf16[144,16,128]{2,1,0:T(8,128)(2,1)S(1)}, bf16[144,16,128]{2,1,0:T(8,128)(2,1)S(1)}, u32[]{:S(2)}, u32[]{:S(2)}) collective-permute-start(bf16[144,16,128]{2,1,0:T(8,128)(2,1)S(1)} %constant_dynamic-update-slice_fusion.p0), channel_id=1, source_target_pairs={{0,96},{1,97},{2,98},{3,99},{4,28},{5,29},{6,30},{7,31},{8,104},{9... | collective-permute-start | bytes 1769480 | tf_op jit(solution)/shard_map/ppermute | solution.py:139
  28.5 0.0 collective-permute-start.6
  28.6 0.7 collective-permute-start.5
  29.3 0.7 subtract_select_fusion
  30.0 0.1 copy.20
  30.1 0.1 reshape.33.idx_ref
  30.2 0.8 fusion.15
  30.9 0.1 reshape.30.leaf_ref
  31.0 0.7 copy.19
  31.7 0.7 multiply_bitcast_fusion
  32.4 4.6 %collective-permute-start.8 = (bf16[144,16,128]{2,1,0:T(8,128)(2,1)S(1)}, bf16[144,16,128]{2,1,0:T(8,128)(2,1)S(1)}, u32[]{:S(2)}, u32[]{:S(2)}) collective-permute-start(bf16[144,16,128]{2,1,0:T(8,128)(2,1)S(1)} %constant_dynamic-update-slice_fusion.p0), channel_id=1, source_target_pairs={{0,4},{4,0},{1,5},{5,1},{2,6},{6,2},{3,7},{7,3},{8,12},{12,8},{9,1... | collective-permute-start | bytes 1769480 | tf_op jit(solution)/shard_map/ppermute | solution.py:185
  37.0 4.7 %collective-permute-done.7.p3 = bf16[144,16,128]{2,1,0:T(8,128)(2,1)S(1)} collective-permute-done((bf16[144,16,128]{2,1,0:T(8,128)(2,1)S(1)}, bf16[144,16,128]{2,1,0:T(8,128)(2,1)S(1)}, u32[]{:S(2)}, u32[]{:S(2)}) %collective-permute-start.7) | collective-permute-done | bytes 589856 | tf_op jit(solution)/shard_map/ppermute | solution.py:139
  41.7 4.5 %collective-permute-start.11 = (bf16[144,16,128]{2,1,0:T(8,128)(2,1)S(1)}, bf16[144,16,128]{2,1,0:T(8,128)(2,1)}, u32[]{:S(2)}, u32[]{:S(2)}) collective-permute-start(bf16[144,16,128]{2,1,0:T(8,128)(2,1)S(1)} %collective-permute-done.7.p3), channel_id=1, source_target_pairs={{0,4},{4,0},{1,5},{5,1},{2,6},{6,2},{3,7},{7,3},{8,12},{12,8},{9,1... | collective-permute-start | bytes 1769480 | tf_op jit(solution)/shard_map/ppermute | solution.py:185
  46.2 0.0 collective-permute-done.6.p2
  46.2 0.0 collective-permute-start.10
  46.2 0.0 collective-permute-done.5.p1
  46.2 4.0 %collective-permute-start.9 = (bf16[144,16,128]{2,1,0:T(8,128)(2,1)S(1)}, bf16[144,16,128]{2,1,0:T(8,128)(2,1)}, u32[]{:S(2)}, u32[]{:S(2)}) collective-permute-start(bf16[144,16,128]{2,1,0:T(8,128)(2,1)S(1)} %collective-permute-done.5.p1), channel_id=1, source_target_pairs={{0,4},{4,0},{1,5},{5,1},{2,6},{6,2},{3,7},{7,3},{8,12},{12,8},{9,1... | collective-permute-start | bytes 1769480 | tf_op jit(solution)/shard_map/ppermute | solution.py:185
  50.2 0.7 compare_bitcast_fusion
  50.9 0.1 fusion.31
  51.0 0.1 pad_add_fusion
  51.1 0.1 reshape.32.grand_ref
  51.2 0.0 collective-permute-done.13.right_ref
  51.2 1.9 %collective-permute-start.12 = (bf16[16,2048]{1,0:T(8,128)(2,1)S(1)}, bf16[16,2048]{1,0:T(8,128)(2,1)S(1)}, u32[]{:S(2)}, u32[]{:S(2)}) collective-permute-start(bf16[16,2048]{1,0:T(8,128)(2,1)S(1)} %get-tuple-element.6), channel_id=1, source_target_pairs={{0,1},{1,2},{2,3},{3,4},{4,5},{5,6},{6,7},{7,8},{8,9},{9,10},{10,1... | collective-permute-start | bytes 196616 | tf_op jit(solution)/shard_map/ppermute | solution.py:187
  53.1 0.1 pad_add_fusion.1.own_ref
  53.2 0.0 copy-start.1
  53.2 4.8 %collective-permute-done.12.left_ref = bf16[16,2048]{1,0:T(8,128)(2,1)S(1)} collective-permute-done((bf16[16,2048]{1,0:T(8,128)(2,1)S(1)}, bf16[16,2048]{1,0:T(8,128)(2,1)S(1)}, u32[]{:S(2)}, u32[]{:S(2)}) %collective-permute-start.12) | collective-permute-done | bytes 65568 | tf_op jit(solution)/shard_map/ppermute | solution.py:187
  58.0 0.0 copy-start.3
  58.0 0.9 %copy-done.3 = bf16[16,4096]{1,0:T(8,128)(2,1)S(1)} copy-done((bf16[16,4096]{1,0:T(8,128)(2,1)S(1)}, bf16[16,4096]{1,0:T(8,128)(2,1)}, u32[]{:S(2)}) %copy-start.3) | copy-done | bytes 131096
  58.9 0.0 copy-start.5
  58.9 0.0 copy-start.6
  58.9 0.0 copy-start.7
  58.9 13.3 %near.1.near_ref = f32[16,4096]{1,0:T(8,128)S(1)} custom-call(s32[128]{0:T(128)S(1)} %reshape.33.idx_ref, bf16[16,2048]{1,0:T(8,128)(2,1)S(1)} %collective-permute-done.12.left_ref, bf16[16,4096]{1,0:T(8,128)(2,1)S(1)} %copy-done.3, bf16[16,2048]{1,0:T(8,128)(2,1)S(1)} %collective-permute-done.13.right_ref, bf16[16,2048,256]{2,1,0:T(8,128)(2,1)} %blocks_ref.1), custom_call_target="tpu_custom_call" | custom-call | flops 268435456 | bytes 17500000 | tf_op jit(solution)/shard_map/near/pallas_call | solution.py:189
  72.2 0.0 collective-permute-done.8.p4
  72.2 0.0 copy-start.8
  72.2 0.0 collective-permute-done.11.p7
  72.2 0.0 collective-permute-done.10.p6
  72.2 0.0 collective-permute-done.9.p5
  72.2 0.8 copy-done.8
  73.0 0.0 copy-done.1
  73.0 0.0 copy-done.5
  73.0 0.0 copy-done.6
  73.0 0.0 copy-done.7
  73.0 14.0 %downward.1 = bf16[16,4096]{1,0:T(8,128)(2,1)} custom-call(s32[512]{0:T(512)S(1)} %reshape.30.leaf_ref, s32[64]{0:T(128)S(1)} %reshape.31.parent_ref, s32[80]{0:T(128)S(1)} %reshape.32.grand_ref, s32[2]{0:T(128)S(1)} %pad_add_fusion.1.own_ref, bf16[144,16,128]{2,1,0:T(8,128)(2,1)S(1)} %constant_dynamic-update-slice_fusion.p0, ...), custom_call_target="tpu_custom_call" | custom-call | tf_op jit(solution)/shard_map/downward/pallas_call | solution.py:214
  (9 shorter events, 0.1 us)
Async XLA Ops:
  0.0 1.0 %copy-start = (bf16[16,64,256]{2,1,0:T(8,128)(2,1)S(1)}, bf16[16,64,256]{2,1,0:T(8,128)(2,1)}, u32[]{:S(2)}) copy-start(bf16[16,64,256]{2,1,0:T(8,128)(2,1)} %basis_ref.3) | copy-start | bytes 1572868
  1.0 0.9 %copy-start.2 = (bf16[16,4096]{1,0:T(8,128)(2,1)S(1)}, bf16[16,4096]{1,0:T(8,128)(2,1)}, u32[]{:S(2)}) copy-start(bf16[16,4096]{1,0:T(8,128)(2,1)} %dens_ref.3) | copy-start | bytes 393220
  1.9 0.9 %copy-start.4 = (bf16[2,64,512]{2,1,0:T(8,128)(2,1)S(1)}, bf16[2,64,512]{2,1,0:T(8,128)(2,1)}, u32[]{:S(2)}) copy-start(bf16[2,64,512]{2,1,0:T(8,128)(2,1)} %pt_ref.3) | copy-start | bytes 393220
  3.3 8.4 %collective-permute-start = (bf16[9,16,128]{2,1,0:T(8,128)(2,1)S(1)}, bf16[9,16,128]{2,1,0:T(8,128)(2,1)S(1)}, u32[]{:S(2)}, u32[]{:S(2)}) collective-permute-start(bf16[9,16,128]{2,1,0:T(8,128)(2,1)S(1)} %upward.1), channel_id=1, source_target_pairs={{0,1},{1,0},{2,3},{3,2},{4,5},{5,4},{6,7},{7,6},{8,9},{9,8},{10,11... | collective-permute-start | bytes 110600 | tf_op jit(solution)/shard_map/ppermute | solution.py:132
  5.8 45.3 %collective-permute-start.13 = (bf16[16,2048]{1,0:T(8,128)(2,1)S(1)}, bf16[16,2048]{1,0:T(8,128)(2,1)S(1)}, u32[]{:S(2)}, u32[]{:S(2)}) collective-permute-start(bf16[16,2048]{1,0:T(8,128)(2,1)S(1)} %get-tuple-element.5), channel_id=1, source_target_pairs={{1,0},{2,1},{3,2},{4,3},{5,4},{6,5},{7,6},{8,7},{9,8},{10,9},{11,1... | collective-permute-start | bytes 196616 | tf_op jit(solution)/shard_map/ppermute | solution.py:188
  11.7 4.5 %collective-permute-start.1 = (bf16[18,16,128]{2,1,0:T(8,128)(2,1)S(1)}, bf16[18,16,128]{2,1,0:T(8,128)(2,1)S(1)}, u32[]{:S(2)}, u32[]{:S(2)}) collective-permute-start(bf16[18,16,128]{2,1,0:T(8,128)(2,1)S(1)} %pad_maximum_fusion.1), channel_id=1, source_target_pairs={{0,3},{1,2},{2,1},{3,0},{4,7},{5,6},{6,5},{7,4},{8,11},{9,10},{10,... | collective-permute-start | bytes 221192 | tf_op jit(solution)/shard_map/ppermute | solution.py:134
  16.3 5.3 %collective-permute-start.2 = (bf16[36,16,128]{2,1,0:T(8,128)(2,1)S(1)}, bf16[36,16,128]{2,1,0:T(8,128)(2,1)S(1)}, u32[]{:S(2)}, u32[]{:S(2)}) collective-permute-start(bf16[36,16,128]{2,1,0:T(8,128)(2,1)S(1)} %pad_maximum_fusion), channel_id=1, source_target_pairs={{0,8},{1,9},{2,10},{3,11},{4,36},{5,37},{6,38},{7,39},{8,16},{9,17... | collective-permute-start | bytes 442376 | tf_op jit(solution)/shard_map/ppermute | solution.py:139
  17.5 7.0 %collective-permute-start.4 = (bf16[36,16,128]{2,1,0:T(8,128)(2,1)S(1)}, bf16[36,16,128]{2,1,0:T(8,128)(2,1)S(1)}, u32[]{:S(2)}, u32[]{:S(2)}) collective-permute-start(bf16[36,16,128]{2,1,0:T(8,128)(2,1)S(1)} %pad_maximum_fusion), channel_id=1, source_target_pairs={{0,24},{1,25},{2,26},{3,27},{4,100},{5,101},{6,102},{7,103},{8,0},... | collective-permute-start | bytes 442376 | tf_op jit(solution)/shard_map/ppermute | solution.py:139
  19.0 5.5 %collective-permute-start.3 = (bf16[36,16,128]{2,1,0:T(8,128)(2,1)S(1)}, bf16[36,16,128]{2,1,0:T(8,128)(2,1)S(1)}, u32[]{:S(2)}, u32[]{:S(2)}) collective-permute-start(bf16[36,16,128]{2,1,0:T(8,128)(2,1)S(1)} %pad_maximum_fusion), channel_id=1, source_target_pairs={{0,16},{1,17},{2,18},{3,19},{4,68},{5,69},{6,70},{7,71},{8,24},{9,... | collective-permute-start | bytes 442376 | tf_op jit(solution)/shard_map/ppermute | solution.py:139
  24.6 17.1 %collective-permute-start.7 = (bf16[144,16,128]{2,1,0:T(8,128)(2,1)S(1)}, bf16[144,16,128]{2,1,0:T(8,128)(2,1)S(1)}, u32[]{:S(2)}, u32[]{:S(2)}) collective-permute-start(bf16[144,16,128]{2,1,0:T(8,128)(2,1)S(1)} %constant_dynamic-update-slice_fusion.p0), channel_id=1, source_target_pairs={{0,96},{1,97},{2,98},{3,99},{4,28},{5,29},{6,30},{7,31},{8,104},{9... | collective-permute-start | bytes 1769480 | tf_op jit(solution)/shard_map/ppermute | solution.py:139
  28.5 17.7 %collective-permute-start.6 = (bf16[144,16,128]{2,1,0:T(8,128)(2,1)S(1)}, bf16[144,16,128]{2,1,0:T(8,128)(2,1)S(1)}, u32[]{:S(2)}, u32[]{:S(2)}) collective-permute-start(bf16[144,16,128]{2,1,0:T(8,128)(2,1)S(1)} %constant_dynamic-update-slice_fusion.p0), channel_id=1, source_target_pairs={{0,64},{1,65},{2,66},{3,67},{4,20},{5,21},{6,22},{7,23},{8,72},{9,... | collective-permute-start | bytes 1769480 | tf_op jit(solution)/shard_map/ppermute | solution.py:139
  28.6 17.6 %collective-permute-start.5 = (bf16[144,16,128]{2,1,0:T(8,128)(2,1)S(1)}, bf16[144,16,128]{2,1,0:T(8,128)(2,1)S(1)}, u32[]{:S(2)}, u32[]{:S(2)}) collective-permute-start(bf16[144,16,128]{2,1,0:T(8,128)(2,1)S(1)} %constant_dynamic-update-slice_fusion.p0), channel_id=1, source_target_pairs={{0,32},{1,33},{2,34},{3,35},{4,12},{5,13},{6,14},{7,15},{8,40},{9,... | collective-permute-start | bytes 1769480 | tf_op jit(solution)/shard_map/ppermute | solution.py:139
  32.4 39.8 %collective-permute-start.8 = (bf16[144,16,128]{2,1,0:T(8,128)(2,1)S(1)}, bf16[144,16,128]{2,1,0:T(8,128)(2,1)S(1)}, u32[]{:S(2)}, u32[]{:S(2)}) collective-permute-start(bf16[144,16,128]{2,1,0:T(8,128)(2,1)S(1)} %constant_dynamic-update-slice_fusion.p0), channel_id=1, source_target_pairs={{0,4},{4,0},{1,5},{5,1},{2,6},{6,2},{3,7},{7,3},{8,12},{12,8},{9,1... | collective-permute-start | bytes 1769480 | tf_op jit(solution)/shard_map/ppermute | solution.py:185
  41.7 30.5 %collective-permute-start.11 = (bf16[144,16,128]{2,1,0:T(8,128)(2,1)S(1)}, bf16[144,16,128]{2,1,0:T(8,128)(2,1)}, u32[]{:S(2)}, u32[]{:S(2)}) collective-permute-start(bf16[144,16,128]{2,1,0:T(8,128)(2,1)S(1)} %collective-permute-done.7.p3), channel_id=1, source_target_pairs={{0,4},{4,0},{1,5},{5,1},{2,6},{6,2},{3,7},{7,3},{8,12},{12,8},{9,1... | collective-permute-start | bytes 1769480 | tf_op jit(solution)/shard_map/ppermute | solution.py:185
  46.2 26.0 %collective-permute-start.10 = (bf16[144,16,128]{2,1,0:T(8,128)(2,1)S(1)}, bf16[144,16,128]{2,1,0:T(8,128)(2,1)}, u32[]{:S(2)}, u32[]{:S(2)}) collective-permute-start(bf16[144,16,128]{2,1,0:T(8,128)(2,1)S(1)} %collective-permute-done.6.p2), channel_id=1, source_target_pairs={{0,4},{4,0},{1,5},{5,1},{2,6},{6,2},{3,7},{7,3},{8,12},{12,8},{9,1... | collective-permute-start | bytes 1769480 | tf_op jit(solution)/shard_map/ppermute | solution.py:185
  46.2 26.0 %collective-permute-start.9 = (bf16[144,16,128]{2,1,0:T(8,128)(2,1)S(1)}, bf16[144,16,128]{2,1,0:T(8,128)(2,1)}, u32[]{:S(2)}, u32[]{:S(2)}) collective-permute-start(bf16[144,16,128]{2,1,0:T(8,128)(2,1)S(1)} %collective-permute-done.5.p1), channel_id=1, source_target_pairs={{0,4},{4,0},{1,5},{5,1},{2,6},{6,2},{3,7},{7,3},{8,12},{12,8},{9,1... | collective-permute-start | bytes 1769480 | tf_op jit(solution)/shard_map/ppermute | solution.py:185
  51.2 6.8 %collective-permute-start.12 = (bf16[16,2048]{1,0:T(8,128)(2,1)S(1)}, bf16[16,2048]{1,0:T(8,128)(2,1)S(1)}, u32[]{:S(2)}, u32[]{:S(2)}) collective-permute-start(bf16[16,2048]{1,0:T(8,128)(2,1)S(1)} %get-tuple-element.6), channel_id=1, source_target_pairs={{0,1},{1,2},{2,3},{3,4},{4,5},{5,6},{6,7},{7,8},{8,9},{9,10},{10,1... | collective-permute-start | bytes 196616 | tf_op jit(solution)/shard_map/ppermute | solution.py:187
  53.2 19.8 %copy-start.1 = (bf16[16,64,256]{2,1,0:T(8,128)(2,1)S(1)}, bf16[16,64,256]{2,1,0:T(8,128)(2,1)}, u32[]{:S(2)}) copy-start(bf16[16,64,256]{2,1,0:T(8,128)(2,1)} %basis_ref.3) | copy-start | bytes 1572868
  58.0 0.9 %copy-start.3 = (bf16[16,4096]{1,0:T(8,128)(2,1)S(1)}, bf16[16,4096]{1,0:T(8,128)(2,1)}, u32[]{:S(2)}) copy-start(bf16[16,4096]{1,0:T(8,128)(2,1)} %dens_ref.3) | copy-start | bytes 393220
  58.9 14.1 %copy-start.5 = (bf16[2,64,512]{2,1,0:T(8,128)(2,1)S(1)}, bf16[2,64,512]{2,1,0:T(8,128)(2,1)}, u32[]{:S(2)}) copy-start(bf16[2,64,512]{2,1,0:T(8,128)(2,1)} %pt_ref.3) | copy-start | bytes 393220
  58.9 14.1 %copy-start.6 = (bf16[2,64,2048]{2,1,0:T(8,128)(2,1)S(1)}, bf16[2,64,2048]{2,1,0:T(8,128)(2,1)}, u32[]{:S(2)}) copy-start(bf16[2,64,2048]{2,1,0:T(8,128)(2,1)} %pc_hbm.1) | copy-start | bytes 1572868
  58.9 14.1 %copy-start.7 = (bf16[1,64,1024]{2,1,0:T(8,128)(2,1)S(1)}, bf16[1,64,1024]{2,1,0:T(8,128)(2,1)}, u32[]{:S(2)}) copy-start(bf16[1,64,1024]{2,1,0:T(8,128)(2,1)} %gc_hbm.1) | copy-start | bytes 393220
  72.2 0.8 copy-start.8

commit v2 on v1

v2 whole, which is shorter than its diff:
```python
import functools

import jax
import jax.numpy as jnp
from jax import lax
from jax.experimental import pallas as pl
from jax.experimental.pallas import tpu as pltpu
from jax.sharding import Mesh, PartitionSpec as P

AXES = ("x", "y", "c", "z")
BF16, F32 = jnp.bfloat16, jnp.float32
TILES = 9
HALF = 8 * TILES
UP_VMEM, CODE_VMEM, STAGE_VMEM, NEAR_VMEM = 56_500_000, 65_000_000, 1 << 20, 40_000_000
AHEAD = 4
DOWN_VMEM = 20 * 1024 * 1024


def flat_index(x, y, c, z):
    return ((x * 4 + y) * 2 + c) * 4 + z


def pairs_of(move):
    return [
        (flat_index(x, y, c, z), flat_index(*move(x, y, c, z)))
        for x in range(4)
        for y in range(4)
        for c in range(2)
        for z in range(4)
    ]


def dot_t(a, b):
    return lax.dot_general(a, b, (((1,), (1,)), ((), ())), preferred_element_type=F32)


def dot(a, b):
    return lax.dot_general(a, b, (((1,), (0,)), ((), ())), preferred_element_type=F32)


def up_kernel(
    dens_hbm, basis_hbm, pt_hbm, out_ref, inner_ref, outer_ref, dens_ref, basis_ref, pt_ref, sems
):
    copies = [
        pltpu.make_async_copy(a, b, sems.at[k])
        for k, (a, b) in enumerate(
            ((dens_hbm, dens_ref), (basis_hbm, basis_ref), (pt_hbm, pt_ref))
        )
    ]
    for copy in copies:
        copy.start()
    for copy in copies:
        copy.wait()
    even = lax.axis_index("z") % 2 == 0
    for i in range(8):
        cols = slice(i * 256, (i + 1) * 256)
        head, tail = dens_ref[:, cols], dens_ref[:, 2048 + i * 256 : 2304 + i * 256]
        inner_ref[:, cols] = jnp.where(even, tail, head)
        outer_ref[:, cols] = jnp.where(even, head, tail)
    tiles = []
    for i in range(8):
        pair = [
            dot_t(dens_ref[:, t * 256 : (t + 1) * 256], basis_ref[t]).astype(BF16)
            for t in (2 * i, 2 * i + 1)
        ]
        tile = jnp.concatenate(pair, axis=1)
        out_ref[i] = tile
        tiles.append(tile)
    pair = [
        dot_t(jnp.concatenate(tiles[4 * p : 4 * p + 4], axis=1), pt_ref[p]).astype(BF16)
        for p in range(2)
    ]
    out_ref[8] = jnp.concatenate(pair, axis=1)


def code_kernel(
    ns_ref, nv_ref, ls_ref, lv_ref, ps_ref, pv_ref, gs_ref, gv_ref,
    near_ref, leaf_ref, parent_ref, grand_ref,
):
    mx, my, mc, mz = (lax.axis_index(a) for a in AXES)
    me = flat_index(mx, my, mc, mz)

    def block_tile(device):
        z, c, y, x = device & 3, (device >> 2) & 1, (device >> 3) & 3, device >> 5
        w = z ^ mz
        kz = w ^ (w >> 1)
        ky, kx = (my - y) & 3, (mx - x) & 3
        near_step, far_step = jnp.where(c == 0, ky, kx), jnp.where(c == 0, kx, ky)
        half = near_step >> 1
        unit = jnp.where(far_step == 1, 2 + 2 * half, jnp.where(far_step == 3, 5 - 2 * half, 6 + half))
        unit = jnp.where(far_step == 0, half, unit) + jnp.where(c == mc, 0, 8)
        return unit * HALF + ((near_step & 1) * 4 + kz) * TILES

    def code(tile, source, valid):
        flip = (source + lax.broadcasted_iota(jnp.int32, source.shape, 1)) & 1
        return tile * 4 + valid * 2 + flip

    near_ref[...] = jnp.where(nv_ref[...] == 1, ns_ref[...] - (me * 16 - 8), 32)
    ls = ls_ref[...]
    leaf_ref[...] = code(block_tile(ls >> 4) + ((ls >> 1) & 7), ls, lv_ref[...])
    ps = ps_ref[...]
    parent_ref[...] = code(block_tile(ps >> 1) + 8, ps, pv_ref[...])
    gs = gs_ref[...]
    grand_ref[0:1] = gs
    for z in range(4):
        grand_ref[1 + z : 2 + z] = block_tile(gs * 4 + z) + 8
    grand_ref[5:6] = gv_ref[...]


def stage_kernel(code_ref, dens_ref, out_ref, tiles_ref):
    out_ref[...] = code_ref[...]
    for i in range(16):
        tiles_ref[i] = dens_ref[:, i * 256 : (i + 1) * 256]


def near_kernel(turn, idx_ref, halo_ref, tiles_ref, blocks_hbm, out_ref, padded, blocks, sems):
    half = (lax.axis_index("z") + 1 + turn) & 1
    copies = [
        pltpu.make_async_copy(blocks_hbm.at[half * 8 + t], blocks.at[t], sems.at[t])
        for t in range(8)
    ]
    for copy in copies[:AHEAD]:
        copy.start()
    for i in range(8):
        padded[24 * half + i] = halo_ref[:, i * 256 : (i + 1) * 256]
    for i in range(16):
        padded[8 + i] = tiles_ref[i]
    padded[32] = jnp.zeros((16, 256), BF16)
    for t in range(8):
        if t + AHEAD < 8:
            copies[t + AHEAD].start()
        picked = jnp.concatenate([padded[idx_ref[j, half * 8 + t]] for j in range(8)], axis=1)
        copies[t].wait()
        out_ref[:, t * 256 : (t + 1) * 256] = dot(picked, blocks[t])


def down_kernel(
    leaf_ref, parent_ref, grand_ref, own_ref,
    table, lc, pc, gc, gt, pt_ref, basis_ref, near0_ref, near1_ref,
    out_ref,
):
    first = lax.axis_index("z") % 2 == 1
    second = jnp.logical_not(first)
    low = lax.broadcasted_iota(jnp.int32, (16, 128), 1) < 64
    zero = jnp.zeros((16, 128), BF16)

    def pair_tile(ref, t, j):
        first, second = ref[t, j], ref[t, j + 1]
        a, b = table[first >> 2], table[second >> 2]
        straight = jnp.where(low, a, b)
        crossed = pltpu.roll(jnp.where(low, b, a), 64, 1)
        kind = jnp.where(low, first, second) & 3
        return jnp.where(kind == 2, straight, jnp.where(kind == 3, crossed, zero))

    ups = []
    for j in range(16):
        children = jnp.concatenate([table[grand_ref[1 + z, j]] for z in range(4)], axis=1)
        up = dot_t(children, gt[grand_ref[0, j]])
        ups.append(jnp.where(grand_ref[5, j] == 1, up, 0.0).astype(BF16))
    grand_total = dot_t(jnp.concatenate(ups, axis=1), gc[0]).astype(BF16)
    down_two = dot(grand_total, gt[own_ref[0], :, pl.ds(pl.multiple_of(own_ref[1] * 128, 128), 128)])

    down_one = []
    for p in range(2):
        coefs = jnp.concatenate([pair_tile(parent_ref, p, 2 * i) for i in range(16)], axis=1)
        far = dot_t(coefs, pc[p])
        total = (far + down_two[:, p * 64 : (p + 1) * 64]).astype(BF16)
        down_one.append(dot(total, pt_ref[p]))

    for g in range(4):
        coefs = jnp.concatenate(
            [
                jnp.concatenate([pair_tile(leaf_ref, t, 2 * i) for i in range(16)], axis=1)
                for t in range(4 * g, 4 * g + 4)
            ],
            axis=0,
        )
        far = dot_t(coefs, lc[4 * g : 4 * g + 4].reshape(256, 2048))
        for k in range(4):
            t = 4 * g + k
            total = far[k * 16 : (k + 1) * 16, k * 64 : (k + 1) * 64]
            total = total + down_one[t // 8][:, (t % 8) * 64 : (t % 8 + 1) * 64]
            cols = slice(t * 256, (t + 1) * 256)
            here = slice((t % 8) * 256, (t % 8 + 1) * 256)
            near = jnp.where(second if t < 8 else first, near1_ref[:, here], near0_ref[:, here])
            out_ref[:, cols] = (dot(total.astype(BF16), basis_ref[t]) + near).astype(BF16)


def shift_plane(v, k, y_core):
    return lax.ppermute(
        v,
        AXES,
        pairs_of(
            lambda x, y, c, z: (x, (y + k) % 4, c, z) if c == y_core else ((x + k) % 4, y, c, z)
        ),
    )


def body(
    densities, basis, near_blocks, near_source, near_valid, leaf_coupling, leaf_source, leaf_valid,
    parent_transfer, parent_coupling, parent_source, parent_valid, grand_transfer, grand_coupling,
    grand_source, grand_valid,
):
    anywhere = pl.BlockSpec(memory_space=pl.ANY)
    vmem = pl.BlockSpec(memory_space=pltpu.VMEM)
    smem = pl.BlockSpec(memory_space=pltpu.SMEM)
    mz = lax.axis_index("z")
    own = jnp.stack([lax.axis_index(("x", "y", "c")), mz]).astype(jnp.int32)

    coefs, inner, outer = pl.pallas_call(
        up_kernel,
        out_shape=[
            jax.ShapeDtypeStruct((TILES, 16, 128), BF16),
            jax.ShapeDtypeStruct((16, 2048), BF16),
            jax.ShapeDtypeStruct((16, 2048), BF16),
        ],
        in_specs=[anywhere] * 3,
        out_specs=[vmem] * 3,
        scratch_shapes=[
            pltpu.VMEM((16, 4096), BF16),
            pltpu.VMEM((16, 64, 256), BF16),
            pltpu.VMEM((2, 64, 512), BF16),
            pltpu.SemaphoreType.DMA((3,)),
        ],
        compiler_params=pltpu.CompilerParams(vmem_limit_bytes=UP_VMEM),
        name="upward",
    )(densities, basis, parent_transfer)

    barrier = lax.optimization_barrier
    swap = [(0, 1), (1, 0)]

    def near_half(turn, halo, near_code):
        return pl.pallas_call(
            functools.partial(near_kernel, turn),
            out_shape=jax.ShapeDtypeStruct((16, 2048), F32),
            in_specs=[smem, vmem, vmem, anywhere],
            out_specs=vmem,
            scratch_shapes=[
                pltpu.VMEM((33, 16, 256), BF16),
                pltpu.VMEM((8, 2048, 256), BF16),
                pltpu.SemaphoreType.DMA((8,)),
            ],
            compiler_params=pltpu.CompilerParams(vmem_limit_bytes=NEAR_VMEM),
            cost_estimate=pl.CostEstimate(
                flops=16 * 16 * 2048 * 256, bytes_accessed=8_700_000, transcendentals=0
            ),
            name="near",
        )(near_code, halo, tiles, near_blocks)

    coefs, sources = barrier(
        (
            coefs,
            (near_source.T, near_valid.T, leaf_source, leaf_valid, parent_source, parent_valid,
             grand_source, grand_valid),
        )
    )
    step = lax.ppermute(coefs, "z", [(i, i ^ 1) for i in range(4)])
    inner = lax.ppermute(inner, AXES, [(i, i ^ 1) for i in range(128)])
    near_code, leaf_code, parent_code, grand_code = pl.pallas_call(
        code_kernel,
        out_shape=[
            jax.ShapeDtypeStruct(n, jnp.int32) for n in ((8, 16), (16, 32), (2, 32), (6, 16))
        ],
        compiler_params=pltpu.CompilerParams(vmem_limit_bytes=CODE_VMEM),
        name="codes",
    )(*sources)
    coefs, near_code, densities = barrier(
        (jnp.concatenate([coefs, step], axis=0), near_code, densities)
    )
    step = lax.ppermute(coefs, "z", [(i, i ^ 3) for i in range(4)])
    near_code, tiles = pl.pallas_call(
        stage_kernel,
        out_shape=[
            jax.ShapeDtypeStruct((8, 16), jnp.int32),
            jax.ShapeDtypeStruct((16, 16, 256), BF16),
        ],
        in_specs=[vmem] * 2,
        out_specs=[vmem] * 2,
        compiler_params=pltpu.CompilerParams(vmem_limit_bytes=STAGE_VMEM),
        name="stage",
    )(near_code, densities)
    coefs, inner, outer, near_code, tiles = barrier(
        (jnp.concatenate([coefs, step], axis=0), inner, outer, near_code, tiles)
    )

    steps = [shift_plane(coefs, k, 0) for k in (1, 2, 3)]
    near0 = near_half(0, inner, near_code)
    coefs, near0, outer = barrier((jnp.concatenate([coefs] + steps, axis=0), near0, outer))

    first, second = coefs[:HALF], coefs[HALF:]
    ahead1, back2 = shift_plane(first, 1, 1), shift_plane(second, 3, 1)
    outer = lax.ppermute(
        outer, AXES, [(i, i + 1) for i in range(1, 127, 2)] + [(i + 1, i) for i in range(1, 127, 2)]
    )
    ahead2, back1 = shift_plane(second, 1, 1), shift_plane(first, 3, 1)
    ahead1, back2, near_code = barrier((ahead1, back2, near_code))
    far1, far2 = shift_plane(ahead1, 1, 1), shift_plane(back2, 3, 1)
    near1 = near_half(1, outer, near_code)
    parts = [[coefs], [ahead1, back2], [ahead2, back1], [far1, far2]]
    other = [lax.ppermute(jnp.concatenate(p, axis=0), "c", swap) for p in parts]
    table = jnp.concatenate(sum(parts, []) + other, axis=0)

    return pl.pallas_call(
        down_kernel,
        out_shape=jax.ShapeDtypeStruct((16, 4096), BF16),
        in_specs=[smem] * 4 + [vmem] * 9,
        out_specs=vmem,
        compiler_params=pltpu.CompilerParams(vmem_limit_bytes=DOWN_VMEM),
        name="downward",
    )(
        leaf_code, parent_code, grand_code, own, table,
        leaf_coupling, parent_coupling, grand_coupling, grand_transfer, parent_transfer, basis,
        near0, near1,
    )


def solution(mesh):
    grid = Mesh(mesh.devices.reshape(4, 4, 2, 4), AXES)
    leaf, both = ("x", "y", "c"), AXES
    row, cube = P(both, None), P(both, None, None)
    return jax.shard_map(
        body,
        mesh=grid,
        in_specs=(
            P(None, both), cube, cube, row, row, cube, row, row, cube, cube, row, row, P(),
            P(leaf, None, None), P(leaf, None), P(leaf, None),
        ),
        out_specs=P(None, both),
        check_vma=False,
    )
```

time: 87.6 us -> 57.1 us (0.65)
  the two profiles are of different devices: /device:TPU:1 before, /device:TPU:5 now
where the time goes in v2:
time: 57.1 us; the launch traced here: 56.9 us
  starting transfers between devices  30.9 us (54%)
  Pallas kernels  18.4 us (32%)
  waiting for transfers between devices  3.83 us (7%)
  local copies, waits for them, and re-layouts  3.03 us (5%)
    ppermute x9, starting transfers between devices, shift_plane(): lax.ppermute(v, AXES, pairs_of(lambda x, y, c, z: (x, (y + k) % 4, c, z)...  10.7 us
    pallas_call x2, Pallas kernels, near_half(): pl.pallas_call(functools.partial(near_kernel, turn), out_shape=jax.ShapeD...  9.99 us
    ppermute x4, starting transfers between devices, body(): other = [lax.ppermute(jnp.concatenate(p, axis=0), 'c', swap) for p in parts]  9.82 us
    ppermute x1, starting transfers between devices, body(): lax.ppermute(outer, AXES, [(i, i + 1) for i in range(1, 127, 2)] + [(i +...  5.1 us
    pallas_call x1, Pallas kernels, body(): pl.pallas_call(down_kernel, out_shape=jax.ShapeDtypeStruct((16, 4096), BF...  4.76 us
    ppermute x1, starting transfers between devices, body(): step = lax.ppermute(coefs, 'z', [(i, i ^ 3) for i in range(4)])  3.61 us
    unnamed x34, local copies, waits for them, and re-layouts  2.79 us
    pallas_call x1, Pallas kernels, body(): pl.pallas_call(up_kernel, out_shape=[jax.ShapeDtypeStruct((TILES, 16, 128...  2.23 us
  transfers between devices with their start and end apart: 17, of which 4 were waited for; matrix products, arithmetic and copies ran while one was open for 2% of the time, Pallas kernels for 20%

profile of v2, /device:TPU:5, one launch (start us, length us, event | category | flops | bytes accessed | tf_op | source)
XLA Modules:
  0.0 56.9 jit_solution(13562452207054331589)
XLA Ops:
  0.0 2.2 %upward.1 = (bf16[9,16,128]{2,1,0:T(8,128)(2,1)S(1)}, bf16[16,2048]{1,0:T(8,128)(2,1)}, bf16[16,2048]{1,0:T(8,128)(2,1)}) custom-call(bf16[16,4096]{1,0:T(8,128)(2,1)} %dens_ref, bf16[16,64,256]{2,1,0:T(8,128)(2,1)} %basis_ref.1, bf16[2,64,512]{2,1,0:T(8,128)(2,1)} %pt_ref.1), custom_call_target="tpu_custom_call" | custom-call | tf_op jit(solution)/shard_map/upward/pallas_call | solution.py:210
  2.2 1.7 %collective-permute-start = (bf16[9,16,128]{2,1,0:T(8,128)(2,1)S(1)}, bf16[9,16,128]{2,1,0:T(8,128)(2,1)S(1)}, u32[]{:S(2)}, u32[]{:S(2)}) collective-permute-start(bf16[9,16,128]{2,1,0:T(8,128)(2,1)S(1)} %get-tuple-element.49), channel_id=1, source_target_pairs={{0,1},{1,0},{2,3},{3,2},{4,5},{5,4},{6,7},{7,6},{8,9},{9,8},{10,11... | collective-permute-start | bytes 110600 | tf_op jit(solution)/shard_map/ppermute | solution.py:257
  4.0 1.4 %codes.1 = (s32[8,16]{1,0:T(8,128)}, s32[16,32]{1,0:T(8,128)}, s32[2,32]{1,0:T(2,128)}, s32[6,16]{1,0:T(8,128)}) custom-call(s32[8,16]{1,0:T(8,128)} %bitcast.4, s32[8,16]{1,0:T(8,128)} %bitcast.5, s32[16,32]{1,0:T(8,128)} %ls_ref, s32[16,32]{1,0:T(8,128)} %lv_ref, s32[2,32]{1,0:T(2,128)} %ps_ref, s32[2,32]{1,0:T(2,128)} %pv_ref, s32[1,16]{1,0:T(1,128)} %gs_ref, ...), custom_call_target="tpu_custom_call" | custom-call | tf_op jit(solution)/shard_map/codes/pallas_call | solution.py:259
  5.4 0.0 collective-permute-done
  5.4 3.6 %collective-permute-start.1 = (bf16[18,16,128]{2,1,0:T(8,128)(2,1)S(1)}, bf16[18,16,128]{2,1,0:T(8,128)(2,1)S(1)}, u32[]{:S(2)}, u32[]{:S(2)}) collective-permute-start(bf16[18,16,128]{2,1,0:T(8,128)(2,1)S(1)} %pad_maximum_fusion.5), channel_id=1, source_target_pairs={{0,3},{1,2},{2,1},{3,0},{4,7},{5,6},{6,5},{7,4},{8,11},{9,10},{10,... | collective-permute-start | bytes 221192 | tf_op jit(solution)/shard_map/ppermute | solution.py:270
  9.0 0.0 collective-permute-start.2
  9.0 0.9 %copy-done.5 = bf16[16,4096]{1,0:T(8,128)(2,1)S(1)} copy-done((bf16[16,4096]{1,0:T(8,128)(2,1)S(1)}, bf16[16,4096]{1,0:T(8,128)(2,1)}, u32[]{:S(2)}) %copy-start.5) | copy-done | bytes 131096
  9.9 0.7 %copy-done.9 = s32[8,16]{1,0:T(8,128)S(1)} copy-done((s32[8,16]{1,0:T(8,128)S(1)}, s32[8,16]{1,0:T(8,128)}, u32[]{:S(2)}) %copy-start.9) | copy-done | bytes 536
  10.6 0.1 collective-permute-done.1
  10.7 1.9 %collective-permute-done.2.halo_ref = bf16[16,2048]{1,0:T(8,128)(2,1)S(1)} collective-permute-done((bf16[16,2048]{1,0:T(8,128)(2,1)}, bf16[16,2048]{1,0:T(8,128)(2,1)S(1)}, u32[]{:S(2)}, u32[]{:S(2)}) %collective-permute-start.2) | collective-permute-done | bytes 65568 | tf_op jit(solution)/shard_map/ppermute | solution.py:258
  12.6 0.9 %collective-permute-start.3 = (bf16[36,16,128]{2,1,0:T(8,128)(2,1)S(1)}, bf16[36,16,128]{2,1,0:T(8,128)(2,1)S(1)}, u32[]{:S(2)}, u32[]{:S(2)}) collective-permute-start(bf16[36,16,128]{2,1,0:T(8,128)(2,1)S(1)} %pad_maximum_fusion.4), channel_id=1, source_target_pairs={{0,8},{1,9},{2,10},{3,11},{4,36},{5,37},{6,38},{7,39},{8,16},{9,17... | collective-permute-start | bytes 442376 | tf_op jit(solution)/shard_map/ppermute | solution.py:190
  13.5 0.5 collective-permute-start.4
  14.0 0.9 %collective-permute-start.5 = (bf16[36,16,128]{2,1,0:T(8,128)(2,1)S(1)}, bf16[36,16,128]{2,1,0:T(8,128)(2,1)S(1)}, u32[]{:S(2)}, u32[]{:S(2)}) collective-permute-start(bf16[36,16,128]{2,1,0:T(8,128)(2,1)S(1)} %pad_maximum_fusion.4), channel_id=1, source_target_pairs={{0,24},{1,25},{2,26},{3,27},{4,100},{5,101},{6,102},{7,103},{8,0},... | collective-permute-start | bytes 442376 | tf_op jit(solution)/shard_map/ppermute | solution.py:190
  14.9 5.0 %near.2.near0_ref = f32[16,2048]{1,0:T(8,128)S(1)} custom-call(s32[8,16]{1,0:T(8,128)S(1)} %get-tuple-element.67.idx_ref, bf16[16,2048]{1,0:T(8,128)(2,1)S(1)} %collective-permute-done.2.halo_ref, bf16[16,16,256]{2,1,0:T(8,128)(2,1)S(1)} %get-tuple-element.61.tiles_ref, bf16[16,2048,256]{2,1,0:T(8,128)(2,1)} %blocks_hbm.3), custom_call_target="tpu_custom_call" | custom-call | flops 134217728 | bytes 8700000 | tf_op jit(solution)/shard_map/near/pallas_call | solution.py:233
  19.9 0.0 collective-permute-done.3
  19.9 0.0 collective-permute-done.4
  19.9 0.4 collective-permute-done.5
  20.3 0.1 pad_maximum_fusion
  20.4 0.1 fusion
  20.5 1.4 %collective-permute-start.6 = (bf16[72,16,128]{2,1,0:T(8,128)(2,1)S(1)}, bf16[72,16,128]{2,1,0:T(8,128)(2,1)S(1)}, u32[]{:S(2)}, u32[]{:S(2)}) collective-permute-start(bf16[72,16,128]{2,1,0:T(8,128)(2,1)S(1)} %get-tuple-element.70), channel_id=1, source_target_pairs={{0,32},{1,33},{2,34},{3,35},{4,12},{5,13},{6,14},{7,15},{8,40},{9,... | collective-permute-start | bytes 884744 | tf_op jit(solution)/shard_map/ppermute | solution.py:190
  21.9 1.5 %collective-permute-start.7 = (bf16[72,16,128]{2,1,0:T(8,128)(2,1)S(1)}, bf16[72,16,128]{2,1,0:T(8,128)(2,1)S(1)}, u32[]{:S(2)}, u32[]{:S(2)}) collective-permute-start(bf16[72,16,128]{2,1,0:T(8,128)(2,1)S(1)} %get-tuple-element.69), channel_id=1, source_target_pairs={{0,96},{1,97},{2,98},{3,99},{4,28},{5,29},{6,30},{7,31},{8,104},{9... | collective-permute-start | bytes 884744 | tf_op jit(solution)/shard_map/ppermute | solution.py:190
  23.4 0.1 pad_add_fusion.own_ref
  23.5 0.0 collective-permute-start.8
  23.5 2.7 %collective-permute-start.9 = (bf16[72,16,128]{2,1,0:T(8,128)(2,1)S(1)}, bf16[72,16,128]{2,1,0:T(8,128)(2,1)S(1)}, u32[]{:S(2)}, u32[]{:S(2)}) collective-permute-start(bf16[72,16,128]{2,1,0:T(8,128)(2,1)S(1)} %get-tuple-element.70), channel_id=1, source_target_pairs={{0,96},{1,97},{2,98},{3,99},{4,28},{5,29},{6,30},{7,31},{8,104},{9... | collective-permute-start | bytes 884744 | tf_op jit(solution)/shard_map/ppermute | solution.py:190
  26.1 0.1 constant_dynamic-update-slice_fusion.10
  26.2 4.8 %collective-permute-start.12 = (bf16[144,16,128]{2,1,0:T(8,128)(2,1)S(1)}, bf16[144,16,128]{2,1,0:T(8,128)(2,1)S(1)}, u32[]{:S(2)}, u32[]{:S(2)}) collective-permute-start(bf16[144,16,128]{2,1,0:T(8,128)(2,1)S(1)} %pad_maximum_fusion), channel_id=1, source_target_pairs={{0,4},{4,0},{1,5},{5,1},{2,6},{6,2},{3,7},{7,3},{8,12},{12,8},{9,1... | collective-permute-start | bytes 1769480 | tf_op jit(solution)/shard_map/ppermute | solution.py:300
  31.0 0.0 collective-permute-done.6
  31.0 0.0 copy-done.11
  31.0 5.1 %collective-permute-start.16 = (bf16[16,2048]{1,0:T(8,128)(2,1)S(1)}, bf16[16,2048]{1,0:T(8,128)(2,1)S(1)}, u32[]{:S(2)}, u32[]{:S(2)}) collective-permute-start(bf16[16,2048]{1,0:T(8,128)(2,1)S(1)} %copy-done.11), channel_id=1, source_target_pairs={{1,2},{3,4},{5,6},{7,8},{9,10},{11,12},{13,14},{15,16},{17,18},{19... | collective-permute-start | bytes 196616 | tf_op jit(solution)/shard_map/ppermute | solution.py:292
  36.1 0.0 collective-permute-done.7
  36.1 0.5 collective-permute-start.10
  36.6 0.1 pad_maximum_fusion.1
  36.7 0.0 collective-permute-done.8
  36.7 2.3 %collective-permute-start.11 = (bf16[72,16,128]{2,1,0:T(8,128)(2,1)S(1)}, bf16[72,16,128]{2,1,0:T(8,128)(2,1)S(1)}, u32[]{:S(2)}, u32[]{:S(2)}) collective-permute-start(bf16[72,16,128]{2,1,0:T(8,128)(2,1)S(1)} %collective-permute-done.7), channel_id=1, source_target_pairs={{0,96},{1,97},{2,98},{3,99},{4,28},{5,29},{6,30},{7,31},{8,104},{9... | collective-permute-start | bytes 884744 | tf_op jit(solution)/shard_map/ppermute | solution.py:190
  39.1 0.0 collective-permute-done.9
  39.1 0.1 pad_maximum_fusion.2
  39.2 0.1 collective-permute-start.13
  39.3 0.0 collective-permute-done.16.halo_ref
  39.3 4.7 %collective-permute-start.14 = (bf16[144,16,128]{2,1,0:T(8,128)(2,1)S(1)}, bf16[144,16,128]{2,1,0:T(8,128)(2,1)S(1)}, u32[]{:S(2)}, u32[]{:S(2)}) collective-permute-start(bf16[144,16,128]{2,1,0:T(8,128)(2,1)S(1)} %pad_maximum_fusion.2), channel_id=1, source_target_pairs={{0,4},{4,0},{1,5},{5,1},{2,6},{6,2},{3,7},{7,3},{8,12},{12,8},{9,1... | collective-permute-start | bytes 1769480 | tf_op jit(solution)/shard_map/ppermute | solution.py:300
  44.0 5.0 %near.3.near1_ref = f32[16,2048]{1,0:T(8,128)S(1)} custom-call(s32[8,16]{1,0:T(8,128)S(1)} %get-tuple-element.67.idx_ref, bf16[16,2048]{1,0:T(8,128)(2,1)S(1)} %collective-permute-done.16.halo_ref, bf16[16,16,256]{2,1,0:T(8,128)(2,1)S(1)} %get-tuple-element.61.tiles_ref, bf16[16,2048,256]{2,1,0:T(8,128)(2,1)} %blocks_hbm.3), custom_call_target="tpu_custom_call" | custom-call | flops 134217728 | bytes 8700000 | tf_op jit(solution)/shard_map/near/pallas_call | solution.py:233
  49.0 0.0 copy-start
  49.0 0.0 copy-start.1
  49.0 0.0 copy-start.2
  49.0 0.0 copy-start.3
  49.0 0.0 copy-start.4
  49.0 0.0 copy-start.6
  49.1 0.0 copy-start.7
  49.2 0.0 collective-permute-done.10
  49.2 0.0 collective-permute-done.11
  49.2 0.1 pad_maximum_fusion.3
  49.3 0.3 collective-permute-start.15
  49.6 0.0 collective-permute-done.12
  49.6 0.1 constant_dynamic-update-slice_fusion.3
  49.8 0.0 collective-permute-done.13
  49.8 0.1 constant_dynamic-update-slice_fusion.2
  50.0 0.0 collective-permute-done.14
  50.0 0.1 constant_dynamic-update-slice_fusion.1
  50.1 1.4 %collective-permute-done.15 = bf16[144,16,128]{2,1,0:T(8,128)(2,1)S(1)} collective-permute-done((bf16[144,16,128]{2,1,0:T(8,128)(2,1)S(1)}, bf16[144,16,128]{2,1,0:T(8,128)(2,1)S(1)}, u32[]{:S(2)}, u32[]{:S(2)}) %collective-permute-start.15) | collective-permute-done | bytes 589856 | tf_op jit(solution)/shard_map/ppermute | solution.py:300
  51.5 0.1 constant_dynamic-update-slice_fusion.table
  51.7 0.3 copy-done.2
  52.0 0.1 copy-done.4
  52.1 0.0 copy-done.6
  52.1 0.0 copy-done.7
  52.1 4.8 %downward.1 = bf16[16,4096]{1,0:T(8,128)(2,1)} custom-call(s32[16,32]{1,0:T(8,128)S(1)} %copy-done.7, s32[2,32]{1,0:T(2,128)S(1)} %copy-done.10, s32[6,16]{1,0:T(8,128)S(1)} %copy-done.8, s32[2]{0:T(128)S(1)} %pad_add_fusion.own_ref, bf16[1152,16,128]{2,1,0:T(8,128)(2,1)S(1)} %constant_dynamic-update-slice_fusion.table, bf16[16,64,2048]{2,1,0:T(8,128)(2,1)S(1)} %copy-done, ...), custom_call_target="tpu_custom_call" | custom-call | tf_op jit(solution)/shard_map/downward/pallas_call | solution.py:303
  (19 shorter events, 0.3 us)
Async XLA Ops:
  2.2 3.1 %collective-permute-start = (bf16[9,16,128]{2,1,0:T(8,128)(2,1)S(1)}, bf16[9,16,128]{2,1,0:T(8,128)(2,1)S(1)}, u32[]{:S(2)}, u32[]{:S(2)}) collective-permute-start(bf16[9,16,128]{2,1,0:T(8,128)(2,1)S(1)} %get-tuple-element.49), channel_id=1, source_target_pairs={{0,1},{1,0},{2,3},{3,2},{4,5},{5,4},{6,7},{7,6},{8,9},{9,8},{10,11... | collective-permute-start | bytes 110600 | tf_op jit(solution)/shard_map/ppermute | solution.py:257
  5.4 5.3 %collective-permute-start.1 = (bf16[18,16,128]{2,1,0:T(8,128)(2,1)S(1)}, bf16[18,16,128]{2,1,0:T(8,128)(2,1)S(1)}, u32[]{:S(2)}, u32[]{:S(2)}) collective-permute-start(bf16[18,16,128]{2,1,0:T(8,128)(2,1)S(1)} %pad_maximum_fusion.5), channel_id=1, source_target_pairs={{0,3},{1,2},{2,1},{3,0},{4,7},{5,6},{6,5},{7,4},{8,11},{9,10},{10,... | collective-permute-start | bytes 221192 | tf_op jit(solution)/shard_map/ppermute | solution.py:270
  9.0 3.6 %collective-permute-start.2 = (bf16[16,2048]{1,0:T(8,128)(2,1)}, bf16[16,2048]{1,0:T(8,128)(2,1)S(1)}, u32[]{:S(2)}, u32[]{:S(2)}) collective-permute-start(bf16[16,2048]{1,0:T(8,128)(2,1)} %get-tuple-element.52), channel_id=1, source_target_pairs={{0,1},{1,0},{2,3},{3,2},{4,5},{5,4},{6,7},{7,6},{8,9},{9,8},{10,11... | collective-permute-start | bytes 196616 | tf_op jit(solution)/shard_map/ppermute | solution.py:258
  9.0 0.9 %copy-start.5 = (bf16[16,4096]{1,0:T(8,128)(2,1)S(1)}, bf16[16,4096]{1,0:T(8,128)(2,1)}, u32[]{:S(2)}) copy-start(bf16[16,4096]{1,0:T(8,128)(2,1)} %dens_ref) | copy-start | bytes 393220
  9.9 0.7 %copy-start.9 = (s32[8,16]{1,0:T(8,128)S(1)}, s32[8,16]{1,0:T(8,128)}, u32[]{:S(2)}) copy-start(s32[8,16]{1,0:T(8,128)} %get-tuple-element.54.code_ref) | copy-start | bytes 1540
  12.6 18.4 %copy-start.11 = (bf16[16,2048]{1,0:T(8,128)(2,1)S(1)}, bf16[16,2048]{1,0:T(8,128)(2,1)}, u32[]{:S(2)}) copy-start(bf16[16,2048]{1,0:T(8,128)(2,1)} %get-tuple-element.68) | copy-start | bytes 196612
  12.6 7.3 %collective-permute-start.3 = (bf16[36,16,128]{2,1,0:T(8,128)(2,1)S(1)}, bf16[36,16,128]{2,1,0:T(8,128)(2,1)S(1)}, u32[]{:S(2)}, u32[]{:S(2)}) collective-permute-start(bf16[36,16,128]{2,1,0:T(8,128)(2,1)S(1)} %pad_maximum_fusion.4), channel_id=1, source_target_pairs={{0,8},{1,9},{2,10},{3,11},{4,36},{5,37},{6,38},{7,39},{8,16},{9,17... | collective-permute-start | bytes 442376 | tf_op jit(solution)/shard_map/ppermute | solution.py:190
  13.5 6.4 %collective-permute-start.4 = (bf16[36,16,128]{2,1,0:T(8,128)(2,1)S(1)}, bf16[36,16,128]{2,1,0:T(8,128)(2,1)S(1)}, u32[]{:S(2)}, u32[]{:S(2)}) collective-permute-start(bf16[36,16,128]{2,1,0:T(8,128)(2,1)S(1)} %pad_maximum_fusion.4), channel_id=1, source_target_pairs={{0,16},{1,17},{2,18},{3,19},{4,68},{5,69},{6,70},{7,71},{8,24},{9,... | collective-permute-start | bytes 442376 | tf_op jit(solution)/shard_map/ppermute | solution.py:190
  14.0 6.3 %collective-permute-start.5 = (bf16[36,16,128]{2,1,0:T(8,128)(2,1)S(1)}, bf16[36,16,128]{2,1,0:T(8,128)(2,1)S(1)}, u32[]{:S(2)}, u32[]{:S(2)}) collective-permute-start(bf16[36,16,128]{2,1,0:T(8,128)(2,1)S(1)} %pad_maximum_fusion.4), channel_id=1, source_target_pairs={{0,24},{1,25},{2,26},{3,27},{4,100},{5,101},{6,102},{7,103},{8,0},... | collective-permute-start | bytes 442376 | tf_op jit(solution)/shard_map/ppermute | solution.py:190
  20.5 10.5 %collective-permute-start.6 = (bf16[72,16,128]{2,1,0:T(8,128)(2,1)S(1)}, bf16[72,16,128]{2,1,0:T(8,128)(2,1)S(1)}, u32[]{:S(2)}, u32[]{:S(2)}) collective-permute-start(bf16[72,16,128]{2,1,0:T(8,128)(2,1)S(1)} %get-tuple-element.70), channel_id=1, source_target_pairs={{0,32},{1,33},{2,34},{3,35},{4,12},{5,13},{6,14},{7,15},{8,40},{9,... | collective-permute-start | bytes 884744 | tf_op jit(solution)/shard_map/ppermute | solution.py:190
  21.9 14.3 %collective-permute-start.7 = (bf16[72,16,128]{2,1,0:T(8,128)(2,1)S(1)}, bf16[72,16,128]{2,1,0:T(8,128)(2,1)S(1)}, u32[]{:S(2)}, u32[]{:S(2)}) collective-permute-start(bf16[72,16,128]{2,1,0:T(8,128)(2,1)S(1)} %get-tuple-element.69), channel_id=1, source_target_pairs={{0,96},{1,97},{2,98},{3,99},{4,28},{5,29},{6,30},{7,31},{8,104},{9... | collective-permute-start | bytes 884744 | tf_op jit(solution)/shard_map/ppermute | solution.py:190
  23.5 13.2 %collective-permute-start.8 = (bf16[72,16,128]{2,1,0:T(8,128)(2,1)S(1)}, bf16[72,16,128]{2,1,0:T(8,128)(2,1)S(1)}, u32[]{:S(2)}, u32[]{:S(2)}) collective-permute-start(bf16[72,16,128]{2,1,0:T(8,128)(2,1)S(1)} %get-tuple-element.69), channel_id=1, source_target_pairs={{0,32},{1,33},{2,34},{3,35},{4,12},{5,13},{6,14},{7,15},{8,40},{9,... | collective-permute-start | bytes 884744 | tf_op jit(solution)/shard_map/ppermute | solution.py:190
  23.5 15.6 %collective-permute-start.9 = (bf16[72,16,128]{2,1,0:T(8,128)(2,1)S(1)}, bf16[72,16,128]{2,1,0:T(8,128)(2,1)S(1)}, u32[]{:S(2)}, u32[]{:S(2)}) collective-permute-start(bf16[72,16,128]{2,1,0:T(8,128)(2,1)S(1)} %get-tuple-element.70), channel_id=1, source_target_pairs={{0,96},{1,97},{2,98},{3,99},{4,28},{5,29},{6,30},{7,31},{8,104},{9... | collective-permute-start | bytes 884744 | tf_op jit(solution)/shard_map/ppermute | solution.py:190
  26.2 23.4 %collective-permute-start.12 = (bf16[144,16,128]{2,1,0:T(8,128)(2,1)S(1)}, bf16[144,16,128]{2,1,0:T(8,128)(2,1)S(1)}, u32[]{:S(2)}, u32[]{:S(2)}) collective-permute-start(bf16[144,16,128]{2,1,0:T(8,128)(2,1)S(1)} %pad_maximum_fusion), channel_id=1, source_target_pairs={{0,4},{4,0},{1,5},{5,1},{2,6},{6,2},{3,7},{7,3},{8,12},{12,8},{9,1... | collective-permute-start | bytes 1769480 | tf_op jit(solution)/shard_map/ppermute | solution.py:300
  31.0 8.3 %collective-permute-start.16 = (bf16[16,2048]{1,0:T(8,128)(2,1)S(1)}, bf16[16,2048]{1,0:T(8,128)(2,1)S(1)}, u32[]{:S(2)}, u32[]{:S(2)}) collective-permute-start(bf16[16,2048]{1,0:T(8,128)(2,1)S(1)} %copy-done.11), channel_id=1, source_target_pairs={{1,2},{3,4},{5,6},{7,8},{9,10},{11,12},{13,14},{15,16},{17,18},{19... | collective-permute-start | bytes 196616 | tf_op jit(solution)/shard_map/ppermute | solution.py:292
  36.1 13.1 %collective-permute-start.10 = (bf16[72,16,128]{2,1,0:T(8,128)(2,1)S(1)}, bf16[72,16,128]{2,1,0:T(8,128)(2,1)S(1)}, u32[]{:S(2)}, u32[]{:S(2)}) collective-permute-start(bf16[72,16,128]{2,1,0:T(8,128)(2,1)S(1)} %collective-permute-done.6), channel_id=1, source_target_pairs={{0,32},{1,33},{2,34},{3,35},{4,12},{5,13},{6,14},{7,15},{8,40},{9,... | collective-permute-start | bytes 884744 | tf_op jit(solution)/shard_map/ppermute | solution.py:190
  36.7 12.5 %collective-permute-start.11 = (bf16[72,16,128]{2,1,0:T(8,128)(2,1)S(1)}, bf16[72,16,128]{2,1,0:T(8,128)(2,1)S(1)}, u32[]{:S(2)}, u32[]{:S(2)}) collective-permute-start(bf16[72,16,128]{2,1,0:T(8,128)(2,1)S(1)} %collective-permute-done.7), channel_id=1, source_target_pairs={{0,96},{1,97},{2,98},{3,99},{4,28},{5,29},{6,30},{7,31},{8,104},{9... | collective-permute-start | bytes 884744 | tf_op jit(solution)/shard_map/ppermute | solution.py:190
  39.2 10.6 %collective-permute-start.13 = (bf16[144,16,128]{2,1,0:T(8,128)(2,1)S(1)}, bf16[144,16,128]{2,1,0:T(8,128)(2,1)S(1)}, u32[]{:S(2)}, u32[]{:S(2)}) collective-permute-start(bf16[144,16,128]{2,1,0:T(8,128)(2,1)S(1)} %pad_maximum_fusion.1), channel_id=1, source_target_pairs={{0,4},{4,0},{1,5},{5,1},{2,6},{6,2},{3,7},{7,3},{8,12},{12,8},{9,1... | collective-permute-start | bytes 1769480 | tf_op jit(solution)/shard_map/ppermute | solution.py:300
  39.3 10.7 %collective-permute-start.14 = (bf16[144,16,128]{2,1,0:T(8,128)(2,1)S(1)}, bf16[144,16,128]{2,1,0:T(8,128)(2,1)S(1)}, u32[]{:S(2)}, u32[]{:S(2)}) collective-permute-start(bf16[144,16,128]{2,1,0:T(8,128)(2,1)S(1)} %pad_maximum_fusion.2), channel_id=1, source_target_pairs={{0,4},{4,0},{1,5},{5,1},{2,6},{6,2},{3,7},{7,3},{8,12},{12,8},{9,1... | collective-permute-start | bytes 1769480 | tf_op jit(solution)/shard_map/ppermute | solution.py:300
  49.0 2.7 %copy-start = (bf16[16,64,2048]{2,1,0:T(8,128)(2,1)S(1)}, bf16[16,64,2048]{2,1,0:T(8,128)(2,1)}, u32[]{:S(2)}) copy-start(bf16[16,64,2048]{2,1,0:T(8,128)(2,1)} %lc.1) | copy-start | bytes 12582916
  49.0 2.7 %copy-start.1 = (bf16[16,64,256]{2,1,0:T(8,128)(2,1)S(1)}, bf16[16,64,256]{2,1,0:T(8,128)(2,1)}, u32[]{:S(2)}) copy-start(bf16[16,64,256]{2,1,0:T(8,128)(2,1)} %basis_ref.1) | copy-start | bytes 1572868
  49.0 3.0 %copy-start.2 = (bf16[32,64,512]{2,1,0:T(8,128)(2,1)S(1)}, bf16[32,64,512]{2,1,0:T(8,128)(2,1)}, u32[]{:S(2)}) copy-start(bf16[32,64,512]{2,1,0:T(8,128)(2,1)} %gt.1) | copy-start | bytes 6291460
  49.0 3.0 %copy-start.3 = (bf16[2,64,512]{2,1,0:T(8,128)(2,1)S(1)}, bf16[2,64,512]{2,1,0:T(8,128)(2,1)}, u32[]{:S(2)}) copy-start(bf16[2,64,512]{2,1,0:T(8,128)(2,1)} %pt_ref.1) | copy-start | bytes 393220
  49.0 3.1 %copy-start.4 = (bf16[2,64,2048]{2,1,0:T(8,128)(2,1)S(1)}, bf16[2,64,2048]{2,1,0:T(8,128)(2,1)}, u32[]{:S(2)}) copy-start(bf16[2,64,2048]{2,1,0:T(8,128)(2,1)} %pc.1) | copy-start | bytes 1572868
  49.0 3.0 %copy-start.6 = (bf16[1,64,1024]{2,1,0:T(8,128)(2,1)S(1)}, bf16[1,64,1024]{2,1,0:T(8,128)(2,1)}, u32[]{:S(2)}) copy-start(bf16[1,64,1024]{2,1,0:T(8,128)(2,1)} %gc.1) | copy-start | bytes 393220
  49.1 3.0 %copy-start.7 = (s32[16,32]{1,0:T(8,128)S(1)}, s32[16,32]{1,0:T(8,128)}, u32[]{:S(2)}) copy-start(s32[16,32]{1,0:T(8,128)} %get-tuple-element.46.leaf_ref) | copy-start | bytes 6148
  49.1 3.0 %copy-start.8 = (s32[6,16]{1,0:T(8,128)S(1)}, s32[6,16]{1,0:T(8,128)}, u32[]{:S(2)}) copy-start(s32[6,16]{1,0:T(8,128)} %get-tuple-element.48.grand_ref) | copy-start | bytes 1156
  49.1 3.0 %copy-start.10 = (s32[2,32]{1,0:T(2,128)S(1)}, s32[2,32]{1,0:T(2,128)}, u32[]{:S(2)}) copy-start(s32[2,32]{1,0:T(2,128)} %get-tuple-element.47.parent_ref) | copy-start | bytes 772
  49.3 2.3 %collective-permute-start.15 = (bf16[144,16,128]{2,1,0:T(8,128)(2,1)S(1)}, bf16[144,16,128]{2,1,0:T(8,128)(2,1)S(1)}, u32[]{:S(2)}, u32[]{:S(2)}) collective-permute-start(bf16[144,16,128]{2,1,0:T(8,128)(2,1)S(1)} %pad_maximum_fusion.3), channel_id=1, source_target_pairs={{0,4},{4,0},{1,5},{5,1},{2,6},{6,2},{3,7},{7,3},{8,12},{12,8},{9,1... | collective-permute-start | bytes 1769480 | tf_op jit(solution)/shard_map/ppermute | solution.py:300

commit v3 on v2

--- a/solution.py
+++ b/solution.py
@@ -11,7 +11,7 @@
 BF16, F32 = jnp.bfloat16, jnp.float32
 TILES = 9
 HALF = 8 * TILES
-UP_VMEM, CODE_VMEM, STAGE_VMEM, NEAR_VMEM = 56_500_000, 65_000_000, 1 << 20, 40_000_000
+UP_VMEM, CODE_VMEM, STAGE_VMEM, NEAR_VMEM = 56_300_000, 65_000_000, 1 << 20, 40_000_000
 AHEAD = 4
 DOWN_VMEM = 20 * 1024 * 1024
 
@@ -39,7 +39,7 @@
 
 
 def up_kernel(
-    dens_hbm, basis_hbm, pt_hbm, out_ref, inner_ref, outer_ref, dens_ref, basis_ref, pt_ref, sems
+    dens_hbm, basis_hbm, pt_hbm, out_ref, outer_ref, dens_ref, basis_ref, pt_ref, sems
 ):
     copies = [
         pltpu.make_async_copy(a, b, sems.at[k])
@@ -52,11 +52,10 @@
     for copy in copies:
         copy.wait()
     even = lax.axis_index("z") % 2 == 0
-    for i in range(8):
-        cols = slice(i * 256, (i + 1) * 256)
-        head, tail = dens_ref[:, cols], dens_ref[:, 2048 + i * 256 : 2304 + i * 256]
-        inner_ref[:, cols] = jnp.where(even, tail, head)
-        outer_ref[:, cols] = jnp.where(even, head, tail)
+    for i in range(16):
+        head, tail = (dens_ref[:, k * 128 : (k + 1) * 128] for k in (i, 16 + i))
+        out_ref[TILES + i] = jnp.where(even, tail, head)
+        outer_ref[i] = jnp.where(even, head, tail)
     tiles = []
     for i in range(8):
         pair = [
@@ -113,7 +112,7 @@
         tiles_ref[i] = dens_ref[:, i * 256 : (i + 1) * 256]
 
 
-def near_kernel(turn, idx_ref, halo_ref, tiles_ref, blocks_hbm, out_ref, padded, blocks, sems):
+def near_kernel(turn, skip, idx_ref, halo_ref, tiles_ref, blocks_hbm, out_ref, padded, blocks, sems):
     half = (lax.axis_index("z") + 1 + turn) & 1
     copies = [
         pltpu.make_async_copy(blocks_hbm.at[half * 8 + t], blocks.at[t], sems.at[t])
@@ -122,7 +121,8 @@
     for copy in copies[:AHEAD]:
         copy.start()
     for i in range(8):
-        padded[24 * half + i] = halo_ref[:, i * 256 : (i + 1) * 256]
+        pair = [halo_ref[skip + 2 * i + k] for k in range(2)]
+        padded[24 * half + i] = jnp.concatenate(pair, axis=1)
     for i in range(16):
         padded[8 + i] = tiles_ref[i]
     padded[32] = jnp.zeros((16, 256), BF16)
@@ -207,15 +207,14 @@
     mz = lax.axis_index("z")
     own = jnp.stack([lax.axis_index(("x", "y", "c")), mz]).astype(jnp.int32)
 
-    coefs, inner, outer = pl.pallas_call(
+    coefs, outer = pl.pallas_call(
         up_kernel,
         out_shape=[
-            jax.ShapeDtypeStruct((TILES, 16, 128), BF16),
-            jax.ShapeDtypeStruct((16, 2048), BF16),
-            jax.ShapeDtypeStruct((16, 2048), BF16),
+            jax.ShapeDtypeStruct((TILES + 16, 16, 128), BF16),
+            jax.ShapeDtypeStruct((16, 16, 128), BF16),
         ],
         in_specs=[anywhere] * 3,
-        out_specs=[vmem] * 3,
+        out_specs=[vmem] * 2,
         scratch_shapes=[
             pltpu.VMEM((16, 4096), BF16),
             pltpu.VMEM((16, 64, 256), BF16),
@@ -229,9 +228,9 @@
     barrier = lax.optimization_barrier
     swap = [(0, 1), (1, 0)]
 
-    def near_half(turn, halo, near_code):
+    def near_half(turn, skip, halo, near_code):
         return pl.pallas_call(
-            functools.partial(near_kernel, turn),
+            functools.partial(near_kernel, turn, skip),
             out_shape=jax.ShapeDtypeStruct((16, 2048), F32),
             in_specs=[smem, vmem, vmem, anywhere],
             out_specs=vmem,
@@ -247,15 +246,17 @@
             name="near",
         )(near_code, halo, tiles, near_blocks)
 
-    coefs, sources = barrier(
+    coefs, densities, sources = barrier(
         (
             coefs,
+            densities,
             (near_source.T, near_valid.T, leaf_source, leaf_valid, parent_source, parent_valid,
              grand_source, grand_valid),
         )
     )
-    step = lax.ppermute(coefs, "z", [(i, i ^ 1) for i in range(4)])
-    inner = lax.ppermute(inner, AXES, [(i, i ^ 1) for i in range(128)])
+    inner = lax.ppermute(coefs, "z", [(i, i ^ 1) for i in range(4)])
+    mine = coefs[:TILES]
+    steps = [lax.ppermute(mine, "z", [(i, i ^ k) for i in range(4)]) for k in (3, 2)]
     near_code, leaf_code, parent_code, grand_code = pl.pallas_call(
         code_kernel,
         out_shape=[
@@ -264,10 +265,6 @@
         compiler_params=pltpu.CompilerParams(vmem_limit_bytes=CODE_VMEM),
         name="codes",
     )(*sources)
-    coefs, near_code, densities = barrier(
-        (jnp.concatenate([coefs, step], axis=0), near_code, densities)
-    )
-    step = lax.ppermute(coefs, "z", [(i, i ^ 3) for i in range(4)])
     near_code, tiles = pl.pallas_call(
         stage_kernel,
         out_shape=[
@@ -280,22 +277,23 @@
         name="stage",
     )(near_code, densities)
     coefs, inner, outer, near_code, tiles = barrier(
-        (jnp.concatenate([coefs, step], axis=0), inner, outer, near_code, tiles)
+        (jnp.concatenate([mine, inner[:TILES]] + steps, axis=0), inner, outer, near_code, tiles)
+    )
+
+    outer = lax.ppermute(
+        outer, AXES, [(i, i + 1) for i in range(1, 127, 2)] + [(i + 1, i) for i in range(1, 127, 2)]
     )
 
     steps = [shift_plane(coefs, k, 0) for k in (1, 2, 3)]
-    near0 = near_half(0, inner, near_code)
-    coefs, near0, outer = barrier((jnp.concatenate([coefs] + steps, axis=0), near0, outer))
+    near0 = near_half(0, TILES, inner, near_code)
+    coefs, near0 = barrier((jnp.concatenate([coefs] + steps, axis=0), near0))
 
     first, second = coefs[:HALF], coefs[HALF:]
     ahead1, back2 = shift_plane(first, 1, 1), shift_plane(second, 3, 1)
-    outer = lax.ppermute(
-        outer, AXES, [(i, i + 1) for i in range(1, 127, 2)] + [(i + 1, i) for i in range(1, 127, 2)]
-    )
     ahead2, back1 = shift_plane(second, 1, 1), shift_plane(first, 3, 1)
     ahead1, back2, near_code = barrier((ahead1, back2, near_code))
     far1, far2 = shift_plane(ahead1, 1, 1), shift_plane(back2, 3, 1)
-    near1 = near_half(1, outer, near_code)
+    near1 = near_half(1, 0, outer, near_code)
     parts = [[coefs], [ahead1, back2], [ahead2, back1], [far1, far2]]
     other = [lax.ppermute(jnp.concatenate(p, axis=0), "c", swap) for p in parts]
     table = jnp.concatenate(sum(parts, []) + other, axis=0)

time: 57.1 us -> 51.4 us (0.900)
  the two profiles are of different devices: /device:TPU:5 before, /device:TPU:1 now
where the time goes in v3:
time: 51.4 us; the launch traced here: 51.1 us
  starting transfers between devices  24.3 us (47%)
  Pallas kernels  17.8 us (35%)
  waiting for transfers between devices  5.32 us (10%)
  local copies, waits for them, and re-layouts  3 us (6%)
    ppermute x9, starting transfers between devices, shift_plane(): lax.ppermute(v, AXES, pairs_of(lambda x, y, c, z: (x, (y + k) % 4, c, z)...  10.7 us
    pallas_call x2, Pallas kernels, near_half(): pl.pallas_call(functools.partial(near_kernel, turn, skip), out_shape=jax....  9.99 us
    ppermute x1, starting transfers between devices, body(): lax.ppermute(outer, AXES, [(i, i + 1) for i in range(1, 127, 2)] + [(i +...  6.28 us
    pallas_call x1, Pallas kernels, body(): pl.pallas_call(down_kernel, out_shape=jax.ShapeDtypeStruct((16, 4096), BF...  4.75 us
    ppermute x9, waiting for transfers between devices, shift_plane(): lax.ppermute(v, AXES, pairs_of(lambda x, y, c, z: (x, (y + k) % 4, c, z)...  3.72 us
    ppermute x2, starting transfers between devices, body(): lax.ppermute(mine, 'z', [(i, i ^ k) for i in range(4)])  3.31 us
    unnamed x32, local copies, waits for them, and re-layouts  2.75 us
    ppermute x1, starting transfers between devices, body(): inner = lax.ppermute(coefs, 'z', [(i, i ^ 1) for i in range(4)])  2.55 us
  transfers between devices with their start and end apart: 17, of which 3 were waited for; matrix products, arithmetic and copies ran while one was open for 2% of the time, Pallas kernels for 22%

profile of v3, /device:TPU:1, one launch (start us, length us, event | category | flops | bytes accessed | tf_op | source)
XLA Modules:
  0.0 51.1 jit_solution(425440895987959159)
XLA Ops:
  0.0 1.7 %upward.1 = (bf16[25,16,128]{2,1,0:T(8,128)(2,1)S(1)}, bf16[16,16,128]{2,1,0:T(8,128)(2,1)S(1)}) custom-call(bf16[16,4096]{1,0:T(8,128)(2,1)} %dens_ref, bf16[16,64,256]{2,1,0:T(8,128)(2,1)} %basis_ref.1, bf16[2,64,512]{2,1,0:T(8,128)(2,1)} %pt_ref.1), custom_call_target="tpu_custom_call" | custom-call | tf_op jit(solution)/shard_map/upward/pallas_call | solution.py:210
  1.7 2.5 %collective-permute-start = (bf16[25,16,128]{2,1,0:T(8,128)(2,1)S(1)}, bf16[25,16,128]{2,1,0:T(8,128)(2,1)S(1)}, u32[]{:S(2)}, u32[]{:S(2)}) collective-permute-start(bf16[25,16,128]{2,1,0:T(8,128)(2,1)S(1)} %get-tuple-element.45), channel_id=1, source_target_pairs={{0,1},{1,0},{2,3},{3,2},{4,5},{5,4},{6,7},{7,6},{8,9},{9,8},{10,11... | collective-permute-start | bytes 307208 | tf_op jit(solution)/shard_map/ppermute | solution.py:257
  4.2 2.2 %collective-permute-start.1 = (bf16[9,16,128]{2,1,0:T(8,128)(2,1)S(1)}, bf16[9,16,128]{2,1,0:T(8,128)(2,1)S(1)}, u32[]{:S(2)}, u32[]{:S(2)}) collective-permute-start(bf16[9,16,128]{2,1,0:T(8,128)(2,1)S(1)} %slice.12), channel_id=1, source_target_pairs={{0,3},{1,2},{2,1},{3,0},{4,7},{5,6},{6,5},{7,4},{8,11},{9,10},{10,... | collective-permute-start | bytes 110600 | tf_op jit(solution)/shard_map/ppermute | solution.py:259
  6.5 1.1 %collective-permute-start.2 = (bf16[9,16,128]{2,1,0:T(8,128)(2,1)S(1)}, bf16[9,16,128]{2,1,0:T(8,128)(2,1)S(1)}, u32[]{:S(2)}, u32[]{:S(2)}) collective-permute-start(bf16[9,16,128]{2,1,0:T(8,128)(2,1)S(1)} %slice.12), channel_id=1, source_target_pairs={{0,2},{1,3},{2,0},{3,1},{4,6},{5,7},{6,4},{7,5},{8,10},{9,11},{10,... | collective-permute-start | bytes 110600 | tf_op jit(solution)/shard_map/ppermute | solution.py:259
  7.5 1.4 %codes.1 = (s32[8,16]{1,0:T(8,128)}, s32[16,32]{1,0:T(8,128)}, s32[2,32]{1,0:T(2,128)}, s32[6,16]{1,0:T(8,128)}) custom-call(s32[8,16]{1,0:T(8,128)} %bitcast.4, s32[8,16]{1,0:T(8,128)} %bitcast.5, s32[16,32]{1,0:T(8,128)} %ls_ref, s32[16,32]{1,0:T(8,128)} %lv_ref, s32[2,32]{1,0:T(2,128)} %ps_ref, s32[2,32]{1,0:T(2,128)} %pv_ref, s32[1,16]{1,0:T(1,128)} %gs_ref, ...), custom_call_target="tpu_custom_call" | custom-call | tf_op jit(solution)/shard_map/codes/pallas_call | solution.py:260
  9.0 0.9 %copy-done.5 = bf16[16,4096]{1,0:T(8,128)(2,1)S(1)} copy-done((bf16[16,4096]{1,0:T(8,128)(2,1)S(1)}, bf16[16,4096]{1,0:T(8,128)(2,1)}, u32[]{:S(2)}) %copy-start.5) | copy-done | bytes 131096
  9.9 0.7 %copy-done.9 = s32[8,16]{1,0:T(8,128)S(1)} copy-done((s32[8,16]{1,0:T(8,128)S(1)}, s32[8,16]{1,0:T(8,128)}, u32[]{:S(2)}) %copy-start.9) | copy-done | bytes 536
  10.5 0.0 collective-permute-done.halo_ref
  10.6 0.0 collective-permute-done.1
  10.6 0.5 %collective-permute-done.2 = bf16[9,16,128]{2,1,0:T(8,128)(2,1)S(1)} collective-permute-done((bf16[9,16,128]{2,1,0:T(8,128)(2,1)S(1)}, bf16[9,16,128]{2,1,0:T(8,128)(2,1)S(1)}, u32[]{:S(2)}, u32[]{:S(2)}) %collective-permute-start.2) | collective-permute-done | bytes 36896 | tf_op jit(solution)/shard_map/ppermute | solution.py:259
  11.1 1.3 %collective-permute-start.3 = (bf16[36,16,128]{2,1,0:T(8,128)(2,1)S(1)}, bf16[36,16,128]{2,1,0:T(8,128)(2,1)S(1)}, u32[]{:S(2)}, u32[]{:S(2)}) collective-permute-start(bf16[36,16,128]{2,1,0:T(8,128)(2,1)S(1)} %pad_maximum_fusion.4), channel_id=1, source_target_pairs={{0,8},{1,9},{2,10},{3,11},{4,36},{5,37},{6,38},{7,39},{8,16},{9,17... | collective-permute-start | bytes 442376 | tf_op jit(solution)/shard_map/ppermute | solution.py:190
  12.4 2.5 %collective-permute-start.4 = (bf16[36,16,128]{2,1,0:T(8,128)(2,1)S(1)}, bf16[36,16,128]{2,1,0:T(8,128)(2,1)S(1)}, u32[]{:S(2)}, u32[]{:S(2)}) collective-permute-start(bf16[36,16,128]{2,1,0:T(8,128)(2,1)S(1)} %pad_maximum_fusion.4), channel_id=1, source_target_pairs={{0,16},{1,17},{2,18},{3,19},{4,68},{5,69},{6,70},{7,71},{8,24},{9,... | collective-permute-start | bytes 442376 | tf_op jit(solution)/shard_map/ppermute | solution.py:190
  14.9 1.2 %collective-permute-start.5 = (bf16[36,16,128]{2,1,0:T(8,128)(2,1)S(1)}, bf16[36,16,128]{2,1,0:T(8,128)(2,1)S(1)}, u32[]{:S(2)}, u32[]{:S(2)}) collective-permute-start(bf16[36,16,128]{2,1,0:T(8,128)(2,1)S(1)} %pad_maximum_fusion.4), channel_id=1, source_target_pairs={{0,24},{1,25},{2,26},{3,27},{4,100},{5,101},{6,102},{7,103},{8,0},... | collective-permute-start | bytes 442376 | tf_op jit(solution)/shard_map/ppermute | solution.py:190
  16.0 5.0 %near.2.near0_ref = f32[16,2048]{1,0:T(8,128)S(1)} custom-call(s32[8,16]{1,0:T(8,128)S(1)} %get-tuple-element.59.idx_ref, bf16[25,16,128]{2,1,0:T(8,128)(2,1)S(1)} %collective-permute-done.halo_ref, bf16[16,16,256]{2,1,0:T(8,128)(2,1)S(1)} %get-tuple-element.54.tiles_ref, bf16[16,2048,256]{2,1,0:T(8,128)(2,1)} %blocks_hbm.3), custom_call_target="tpu_custom_call" | custom-call | flops 134217728 | bytes 8700000 | tf_op jit(solution)/shard_map/near/pallas_call | solution.py:232
  21.0 0.0 collective-permute-done.3
  21.0 0.0 collective-permute-done.4
  21.0 0.0 collective-permute-done.5
  21.1 0.1 pad_maximum_fusion
  21.1 0.1 fusion
  21.3 1.4 %collective-permute-start.6 = (bf16[72,16,128]{2,1,0:T(8,128)(2,1)S(1)}, bf16[72,16,128]{2,1,0:T(8,128)(2,1)S(1)}, u32[]{:S(2)}, u32[]{:S(2)}) collective-permute-start(bf16[72,16,128]{2,1,0:T(8,128)(2,1)S(1)} %get-tuple-element.62), channel_id=1, source_target_pairs={{0,32},{1,33},{2,34},{3,35},{4,12},{5,13},{6,14},{7,15},{8,40},{9,... | collective-permute-start | bytes 884744 | tf_op jit(solution)/shard_map/ppermute | solution.py:190
  22.6 1.5 %collective-permute-start.7 = (bf16[72,16,128]{2,1,0:T(8,128)(2,1)S(1)}, bf16[72,16,128]{2,1,0:T(8,128)(2,1)S(1)}, u32[]{:S(2)}, u32[]{:S(2)}) collective-permute-start(bf16[72,16,128]{2,1,0:T(8,128)(2,1)S(1)} %get-tuple-element.61), channel_id=1, source_target_pairs={{0,96},{1,97},{2,98},{3,99},{4,28},{5,29},{6,30},{7,31},{8,104},{9... | collective-permute-start | bytes 884744 | tf_op jit(solution)/shard_map/ppermute | solution.py:190
  24.1 0.1 pad_add_fusion.own_ref
  24.2 6.3 %collective-permute-start.16 = (bf16[16,16,128]{2,1,0:T(8,128)(2,1)S(1)}, bf16[16,16,128]{2,1,0:T(8,128)(2,1)S(1)}, u32[]{:S(2)}, u32[]{:S(2)}) collective-permute-start(bf16[16,16,128]{2,1,0:T(8,128)(2,1)S(1)} %get-tuple-element.60), channel_id=1, source_target_pairs={{1,2},{3,4},{5,6},{7,8},{9,10},{11,12},{13,14},{15,16},{17,18},{19... | collective-permute-start | bytes 196616 | tf_op jit(solution)/shard_map/ppermute | solution.py:283
  30.5 0.5 collective-permute-start.8
  31.0 2.3 %collective-permute-start.9 = (bf16[72,16,128]{2,1,0:T(8,128)(2,1)S(1)}, bf16[72,16,128]{2,1,0:T(8,128)(2,1)S(1)}, u32[]{:S(2)}, u32[]{:S(2)}) collective-permute-start(bf16[72,16,128]{2,1,0:T(8,128)(2,1)S(1)} %get-tuple-element.62), channel_id=1, source_target_pairs={{0,96},{1,97},{2,98},{3,99},{4,28},{5,29},{6,30},{7,31},{8,104},{9... | collective-permute-start | bytes 884744 | tf_op jit(solution)/shard_map/ppermute | solution.py:190
  33.3 0.1 constant_dynamic-update-slice_fusion.10
  33.4 0.0 collective-permute-done.6
  33.4 0.1 collective-permute-start.12
  33.5 0.0 collective-permute-done.7
  33.5 0.1 collective-permute-start.10
  33.6 0.1 pad_maximum_fusion.1
  33.7 3.7 %collective-permute-done.8 = bf16[72,16,128]{2,1,0:T(8,128)(2,1)S(1)} collective-permute-done((bf16[72,16,128]{2,1,0:T(8,128)(2,1)S(1)}, bf16[72,16,128]{2,1,0:T(8,128)(2,1)S(1)}, u32[]{:S(2)}, u32[]{:S(2)}) %collective-permute-start.8) | collective-permute-done | bytes 294944 | tf_op jit(solution)/shard_map/ppermute | solution.py:190
  37.4 0.1 collective-permute-start.11
  37.5 0.0 collective-permute-done.9
  37.5 0.1 pad_maximum_fusion.2
  37.6 0.6 %collective-permute-start.13 = (bf16[144,16,128]{2,1,0:T(8,128)(2,1)S(1)}, bf16[144,16,128]{2,1,0:T(8,128)(2,1)S(1)}, u32[]{:S(2)}, u32[]{:S(2)}) collective-permute-start(bf16[144,16,128]{2,1,0:T(8,128)(2,1)S(1)} %pad_maximum_fusion.1), channel_id=1, source_target_pairs={{0,4},{4,0},{1,5},{5,1},{2,6},{6,2},{3,7},{7,3},{8,12},{12,8},{9,1... | collective-permute-start | bytes 1769480 | tf_op jit(solution)/shard_map/ppermute | solution.py:298
  38.2 0.0 collective-permute-done.16.halo_ref
  38.2 0.1 collective-permute-start.14
  38.3 5.0 %near.3.near1_ref = f32[16,2048]{1,0:T(8,128)S(1)} custom-call(s32[8,16]{1,0:T(8,128)S(1)} %get-tuple-element.59.idx_ref, bf16[16,16,128]{2,1,0:T(8,128)(2,1)S(1)} %collective-permute-done.16.halo_ref, bf16[16,16,256]{2,1,0:T(8,128)(2,1)S(1)} %get-tuple-element.54.tiles_ref, bf16[16,2048,256]{2,1,0:T(8,128)(2,1)} %blocks_hbm.3), custom_call_target="tpu_custom_call" | custom-call | flops 134217728 | bytes 8700000 | tf_op jit(solution)/shard_map/near/pallas_call | solution.py:232
  43.3 0.0 copy-start
  43.3 0.0 copy-start.1
  43.3 0.0 copy-start.2
  43.3 0.0 copy-start.3
  43.3 0.0 copy-start.4
  43.3 0.0 copy-start.6
  43.3 0.0 copy-start.7
  43.3 0.0 copy-start.8
  43.4 0.0 copy-start.10
  43.5 0.0 collective-permute-done.10
  43.5 0.0 collective-permute-done.11
  43.5 0.1 pad_maximum_fusion.3
  43.5 0.7 %collective-permute-start.15 = (bf16[144,16,128]{2,1,0:T(8,128)(2,1)S(1)}, bf16[144,16,128]{2,1,0:T(8,128)(2,1)S(1)}, u32[]{:S(2)}, u32[]{:S(2)}) collective-permute-start(bf16[144,16,128]{2,1,0:T(8,128)(2,1)S(1)} %pad_maximum_fusion.3), channel_id=1, source_target_pairs={{0,4},{4,0},{1,5},{5,1},{2,6},{6,2},{3,7},{7,3},{8,12},{12,8},{9,1... | collective-permute-start | bytes 1769480 | tf_op jit(solution)/shard_map/ppermute | solution.py:298
  44.3 0.0 collective-permute-done.12
  44.3 0.1 constant_dynamic-update-slice_fusion.3
  44.5 0.0 collective-permute-done.13
  44.5 0.1 constant_dynamic-update-slice_fusion.2
  44.6 0.0 collective-permute-done.14
  44.6 0.1 constant_dynamic-update-slice_fusion.1
  44.8 1.1 %collective-permute-done.15 = bf16[144,16,128]{2,1,0:T(8,128)(2,1)S(1)} collective-permute-done((bf16[144,16,128]{2,1,0:T(8,128)(2,1)S(1)}, bf16[144,16,128]{2,1,0:T(8,128)(2,1)S(1)}, u32[]{:S(2)}, u32[]{:S(2)}) %collective-permute-start.15) | collective-permute-done | bytes 589856 | tf_op jit(solution)/shard_map/ppermute | solution.py:298
  45.9 0.1 constant_dynamic-update-slice_fusion.table
  46.0 0.3 copy-done.2
  46.3 0.1 copy-done.4
  46.4 0.0 copy-done.6
  46.4 4.8 %downward.1 = bf16[16,4096]{1,0:T(8,128)(2,1)} custom-call(s32[16,32]{1,0:T(8,128)S(1)} %copy-done.7, s32[2,32]{1,0:T(2,128)S(1)} %copy-done.10, s32[6,16]{1,0:T(8,128)S(1)} %copy-done.8, s32[2]{0:T(128)S(1)} %pad_add_fusion.own_ref, bf16[1152,16,128]{2,1,0:T(8,128)(2,1)S(1)} %constant_dynamic-update-slice_fusion.table, bf16[16,64,2048]{2,1,0:T(8,128)(2,1)S(1)} %copy-done, ...), custom_call_target="tpu_custom_call" | custom-call | tf_op jit(solution)/shard_map/downward/pallas_call | solution.py:301
  (18 shorter events, 0.3 us)
Async XLA Ops:
  1.7 8.9 %collective-permute-start = (bf16[25,16,128]{2,1,0:T(8,128)(2,1)S(1)}, bf16[25,16,128]{2,1,0:T(8,128)(2,1)S(1)}, u32[]{:S(2)}, u32[]{:S(2)}) collective-permute-start(bf16[25,16,128]{2,1,0:T(8,128)(2,1)S(1)} %get-tuple-element.45), channel_id=1, source_target_pairs={{0,1},{1,0},{2,3},{3,2},{4,5},{5,4},{6,7},{7,6},{8,9},{9,8},{10,11... | collective-permute-start | bytes 307208 | tf_op jit(solution)/shard_map/ppermute | solution.py:257
  4.2 6.3 %collective-permute-start.1 = (bf16[9,16,128]{2,1,0:T(8,128)(2,1)S(1)}, bf16[9,16,128]{2,1,0:T(8,128)(2,1)S(1)}, u32[]{:S(2)}, u32[]{:S(2)}) collective-permute-start(bf16[9,16,128]{2,1,0:T(8,128)(2,1)S(1)} %slice.12), channel_id=1, source_target_pairs={{0,3},{1,2},{2,1},{3,0},{4,7},{5,6},{6,5},{7,4},{8,11},{9,10},{10,... | collective-permute-start | bytes 110600 | tf_op jit(solution)/shard_map/ppermute | solution.py:259
  6.5 4.6 %collective-permute-start.2 = (bf16[9,16,128]{2,1,0:T(8,128)(2,1)S(1)}, bf16[9,16,128]{2,1,0:T(8,128)(2,1)S(1)}, u32[]{:S(2)}, u32[]{:S(2)}) collective-permute-start(bf16[9,16,128]{2,1,0:T(8,128)(2,1)S(1)} %slice.12), channel_id=1, source_target_pairs={{0,2},{1,3},{2,0},{3,1},{4,6},{5,7},{6,4},{7,5},{8,10},{9,11},{10,... | collective-permute-start | bytes 110600 | tf_op jit(solution)/shard_map/ppermute | solution.py:259
  9.0 0.9 %copy-start.5 = (bf16[16,4096]{1,0:T(8,128)(2,1)S(1)}, bf16[16,4096]{1,0:T(8,128)(2,1)}, u32[]{:S(2)}) copy-start(bf16[16,4096]{1,0:T(8,128)(2,1)} %dens_ref) | copy-start | bytes 393220
  9.9 0.7 %copy-start.9 = (s32[8,16]{1,0:T(8,128)S(1)}, s32[8,16]{1,0:T(8,128)}, u32[]{:S(2)}) copy-start(s32[8,16]{1,0:T(8,128)} %get-tuple-element.47.code_ref) | copy-start | bytes 1540
  11.1 9.9 %collective-permute-start.3 = (bf16[36,16,128]{2,1,0:T(8,128)(2,1)S(1)}, bf16[36,16,128]{2,1,0:T(8,128)(2,1)S(1)}, u32[]{:S(2)}, u32[]{:S(2)}) collective-permute-start(bf16[36,16,128]{2,1,0:T(8,128)(2,1)S(1)} %pad_maximum_fusion.4), channel_id=1, source_target_pairs={{0,8},{1,9},{2,10},{3,11},{4,36},{5,37},{6,38},{7,39},{8,16},{9,17... | collective-permute-start | bytes 442376 | tf_op jit(solution)/shard_map/ppermute | solution.py:190
  12.4 8.6 %collective-permute-start.4 = (bf16[36,16,128]{2,1,0:T(8,128)(2,1)S(1)}, bf16[36,16,128]{2,1,0:T(8,128)(2,1)S(1)}, u32[]{:S(2)}, u32[]{:S(2)}) collective-permute-start(bf16[36,16,128]{2,1,0:T(8,128)(2,1)S(1)} %pad_maximum_fusion.4), channel_id=1, source_target_pairs={{0,16},{1,17},{2,18},{3,19},{4,68},{5,69},{6,70},{7,71},{8,24},{9,... | collective-permute-start | bytes 442376 | tf_op jit(solution)/shard_map/ppermute | solution.py:190
  14.9 6.2 %collective-permute-start.5 = (bf16[36,16,128]{2,1,0:T(8,128)(2,1)S(1)}, bf16[36,16,128]{2,1,0:T(8,128)(2,1)S(1)}, u32[]{:S(2)}, u32[]{:S(2)}) collective-permute-start(bf16[36,16,128]{2,1,0:T(8,128)(2,1)S(1)} %pad_maximum_fusion.4), channel_id=1, source_target_pairs={{0,24},{1,25},{2,26},{3,27},{4,100},{5,101},{6,102},{7,103},{8,0},... | collective-permute-start | bytes 442376 | tf_op jit(solution)/shard_map/ppermute | solution.py:190
  21.3 12.1 %collective-permute-start.6 = (bf16[72,16,128]{2,1,0:T(8,128)(2,1)S(1)}, bf16[72,16,128]{2,1,0:T(8,128)(2,1)S(1)}, u32[]{:S(2)}, u32[]{:S(2)}) collective-permute-start(bf16[72,16,128]{2,1,0:T(8,128)(2,1)S(1)} %get-tuple-element.62), channel_id=1, source_target_pairs={{0,32},{1,33},{2,34},{3,35},{4,12},{5,13},{6,14},{7,15},{8,40},{9,... | collective-permute-start | bytes 884744 | tf_op jit(solution)/shard_map/ppermute | solution.py:190
  22.6 10.8 %collective-permute-start.7 = (bf16[72,16,128]{2,1,0:T(8,128)(2,1)S(1)}, bf16[72,16,128]{2,1,0:T(8,128)(2,1)S(1)}, u32[]{:S(2)}, u32[]{:S(2)}) collective-permute-start(bf16[72,16,128]{2,1,0:T(8,128)(2,1)S(1)} %get-tuple-element.61), channel_id=1, source_target_pairs={{0,96},{1,97},{2,98},{3,99},{4,28},{5,29},{6,30},{7,31},{8,104},{9... | collective-permute-start | bytes 884744 | tf_op jit(solution)/shard_map/ppermute | solution.py:190
  24.2 13.9 %collective-permute-start.16 = (bf16[16,16,128]{2,1,0:T(8,128)(2,1)S(1)}, bf16[16,16,128]{2,1,0:T(8,128)(2,1)S(1)}, u32[]{:S(2)}, u32[]{:S(2)}) collective-permute-start(bf16[16,16,128]{2,1,0:T(8,128)(2,1)S(1)} %get-tuple-element.60), channel_id=1, source_target_pairs={{1,2},{3,4},{5,6},{7,8},{9,10},{11,12},{13,14},{15,16},{17,18},{19... | collective-permute-start | bytes 196616 | tf_op jit(solution)/shard_map/ppermute | solution.py:283
  30.5 6.9 %collective-permute-start.8 = (bf16[72,16,128]{2,1,0:T(8,128)(2,1)S(1)}, bf16[72,16,128]{2,1,0:T(8,128)(2,1)S(1)}, u32[]{:S(2)}, u32[]{:S(2)}) collective-permute-start(bf16[72,16,128]{2,1,0:T(8,128)(2,1)S(1)} %get-tuple-element.61), channel_id=1, source_target_pairs={{0,32},{1,33},{2,34},{3,35},{4,12},{5,13},{6,14},{7,15},{8,40},{9,... | collective-permute-start | bytes 884744 | tf_op jit(solution)/shard_map/ppermute | solution.py:190
  31.0 6.5 %collective-permute-start.9 = (bf16[72,16,128]{2,1,0:T(8,128)(2,1)S(1)}, bf16[72,16,128]{2,1,0:T(8,128)(2,1)S(1)}, u32[]{:S(2)}, u32[]{:S(2)}) collective-permute-start(bf16[72,16,128]{2,1,0:T(8,128)(2,1)S(1)} %get-tuple-element.62), channel_id=1, source_target_pairs={{0,96},{1,97},{2,98},{3,99},{4,28},{5,29},{6,30},{7,31},{8,104},{9... | collective-permute-start | bytes 884744 | tf_op jit(solution)/shard_map/ppermute | solution.py:190
  33.4 10.9 %collective-permute-start.12 = (bf16[144,16,128]{2,1,0:T(8,128)(2,1)S(1)}, bf16[144,16,128]{2,1,0:T(8,128)(2,1)S(1)}, u32[]{:S(2)}, u32[]{:S(2)}) collective-permute-start(bf16[144,16,128]{2,1,0:T(8,128)(2,1)S(1)} %pad_maximum_fusion), channel_id=1, source_target_pairs={{0,4},{4,0},{1,5},{5,1},{2,6},{6,2},{3,7},{7,3},{8,12},{12,8},{9,1... | collective-permute-start | bytes 1769480 | tf_op jit(solution)/shard_map/ppermute | solution.py:298
  33.5 10.0 %collective-permute-start.10 = (bf16[72,16,128]{2,1,0:T(8,128)(2,1)S(1)}, bf16[72,16,128]{2,1,0:T(8,128)(2,1)S(1)}, u32[]{:S(2)}, u32[]{:S(2)}) collective-permute-start(bf16[72,16,128]{2,1,0:T(8,128)(2,1)S(1)} %collective-permute-done.6), channel_id=1, source_target_pairs={{0,32},{1,33},{2,34},{3,35},{4,12},{5,13},{6,14},{7,15},{8,40},{9,... | collective-permute-start | bytes 884744 | tf_op jit(solution)/shard_map/ppermute | solution.py:190
  37.4 6.1 %collective-permute-start.11 = (bf16[72,16,128]{2,1,0:T(8,128)(2,1)S(1)}, bf16[72,16,128]{2,1,0:T(8,128)(2,1)S(1)}, u32[]{:S(2)}, u32[]{:S(2)}) collective-permute-start(bf16[72,16,128]{2,1,0:T(8,128)(2,1)S(1)} %collective-permute-done.7), channel_id=1, source_target_pairs={{0,96},{1,97},{2,98},{3,99},{4,28},{5,29},{6,30},{7,31},{8,104},{9... | collective-permute-start | bytes 884744 | tf_op jit(solution)/shard_map/ppermute | solution.py:190
  37.6 6.9 %collective-permute-start.13 = (bf16[144,16,128]{2,1,0:T(8,128)(2,1)S(1)}, bf16[144,16,128]{2,1,0:T(8,128)(2,1)S(1)}, u32[]{:S(2)}, u32[]{:S(2)}) collective-permute-start(bf16[144,16,128]{2,1,0:T(8,128)(2,1)S(1)} %pad_maximum_fusion.1), channel_id=1, source_target_pairs={{0,4},{4,0},{1,5},{5,1},{2,6},{6,2},{3,7},{7,3},{8,12},{12,8},{9,1... | collective-permute-start | bytes 1769480 | tf_op jit(solution)/shard_map/ppermute | solution.py:298
  38.2 6.5 %collective-permute-start.14 = (bf16[144,16,128]{2,1,0:T(8,128)(2,1)S(1)}, bf16[144,16,128]{2,1,0:T(8,128)(2,1)S(1)}, u32[]{:S(2)}, u32[]{:S(2)}) collective-permute-start(bf16[144,16,128]{2,1,0:T(8,128)(2,1)S(1)} %pad_maximum_fusion.2), channel_id=1, source_target_pairs={{0,4},{4,0},{1,5},{5,1},{2,6},{6,2},{3,7},{7,3},{8,12},{12,8},{9,1... | collective-permute-start | bytes 1769480 | tf_op jit(solution)/shard_map/ppermute | solution.py:298
  43.3 2.7 %copy-start = (bf16[16,64,2048]{2,1,0:T(8,128)(2,1)S(1)}, bf16[16,64,2048]{2,1,0:T(8,128)(2,1)}, u32[]{:S(2)}) copy-start(bf16[16,64,2048]{2,1,0:T(8,128)(2,1)} %lc.1) | copy-start | bytes 12582916
  43.3 2.7 %copy-start.1 = (bf16[16,64,256]{2,1,0:T(8,128)(2,1)S(1)}, bf16[16,64,256]{2,1,0:T(8,128)(2,1)}, u32[]{:S(2)}) copy-start(bf16[16,64,256]{2,1,0:T(8,128)(2,1)} %basis_ref.1) | copy-start | bytes 1572868
  43.3 3.0 %copy-start.2 = (bf16[32,64,512]{2,1,0:T(8,128)(2,1)S(1)}, bf16[32,64,512]{2,1,0:T(8,128)(2,1)}, u32[]{:S(2)}) copy-start(bf16[32,64,512]{2,1,0:T(8,128)(2,1)} %gt.1) | copy-start | bytes 6291460
  43.3 3.0 %copy-start.3 = (bf16[2,64,512]{2,1,0:T(8,128)(2,1)S(1)}, bf16[2,64,512]{2,1,0:T(8,128)(2,1)}, u32[]{:S(2)}) copy-start(bf16[2,64,512]{2,1,0:T(8,128)(2,1)} %pt_ref.1) | copy-start | bytes 393220
  43.3 3.1 %copy-start.4 = (bf16[2,64,2048]{2,1,0:T(8,128)(2,1)S(1)}, bf16[2,64,2048]{2,1,0:T(8,128)(2,1)}, u32[]{:S(2)}) copy-start(bf16[2,64,2048]{2,1,0:T(8,128)(2,1)} %pc.1) | copy-start | bytes 1572868
  43.3 3.0 %copy-start.6 = (bf16[1,64,1024]{2,1,0:T(8,128)(2,1)S(1)}, bf16[1,64,1024]{2,1,0:T(8,128)(2,1)}, u32[]{:S(2)}) copy-start(bf16[1,64,1024]{2,1,0:T(8,128)(2,1)} %gc.1) | copy-start | bytes 393220
  43.3 3.0 %copy-start.7 = (s32[16,32]{1,0:T(8,128)S(1)}, s32[16,32]{1,0:T(8,128)}, u32[]{:S(2)}) copy-start(s32[16,32]{1,0:T(8,128)} %get-tuple-element.42.leaf_ref) | copy-start | bytes 6148
  43.3 3.0 %copy-start.8 = (s32[6,16]{1,0:T(8,128)S(1)}, s32[6,16]{1,0:T(8,128)}, u32[]{:S(2)}) copy-start(s32[6,16]{1,0:T(8,128)} %get-tuple-element.44.grand_ref) | copy-start | bytes 1156
  43.4 3.0 %copy-start.10 = (s32[2,32]{1,0:T(2,128)S(1)}, s32[2,32]{1,0:T(2,128)}, u32[]{:S(2)}) copy-start(s32[2,32]{1,0:T(2,128)} %get-tuple-element.43.parent_ref) | copy-start | bytes 772
  43.5 2.3 %collective-permute-start.15 = (bf16[144,16,128]{2,1,0:T(8,128)(2,1)S(1)}, bf16[144,16,128]{2,1,0:T(8,128)(2,1)S(1)}, u32[]{:S(2)}, u32[]{:S(2)}) collective-permute-start(bf16[144,16,128]{2,1,0:T(8,128)(2,1)S(1)} %pad_maximum_fusion.3), channel_id=1, source_target_pairs={{0,4},{4,0},{1,5},{5,1},{2,6},{6,2},{3,7},{7,3},{8,12},{12,8},{9,1... | collective-permute-start | bytes 1769480 | tf_op jit(solution)/shard_map/ppermute | solution.py:298

commit v4 on v3

--- a/solution.py
+++ b/solution.py
@@ -294,6 +294,7 @@
     ahead1, back2, near_code = barrier((ahead1, back2, near_code))
     far1, far2 = shift_plane(ahead1, 1, 1), shift_plane(back2, 3, 1)
     near1 = near_half(1, 0, outer, near_code)
+    ahead2, back1, near1 = barrier((ahead2, back1, near1))
     parts = [[coefs], [ahead1, back2], [ahead2, back1], [far1, far2]]
     other = [lax.ppermute(jnp.concatenate(p, axis=0), "c", swap) for p in parts]
     table = jnp.concatenate(sum(parts, []) + other, axis=0)

time: 51.4 us -> 53.7 us (1.045)
  starting transfers between devices: 24.3 us -> 29.9 us
  waiting for transfers between devices: 5.32 us -> 2.26 us
    ppermute x9, waiting for transfers between devices: 3.72 us -> 0.02 us  [shift_plane(): lax.ppermute(v, AXES, pairs_of(lambda x, y, c, z: (x, (y + k) % 4, c, z)...]
    ppermute x4, starting transfers between devices: 1.43 us -> 4.5 us  [body(): other = [lax.ppermute(jnp.concatenate(p, axis=0), 'c', swap) for p in parts]]
    ppermute x9, starting transfers between devices: 10.7 us -> 13.3 us  [shift_plane(): lax.ppermute(v, AXES, pairs_of(lambda x, y, c, z: (x, (y + k) % 4, c, z)...]
    ppermute x4, waiting for transfers between devices: 1.07 us -> 1.7 us  [body(): other = [lax.ppermute(jnp.concatenate(p, axis=0), 'c', swap) for p in parts]]
  transfers between devices with their start and end apart: 17 -> 17, of which waited for: 3 -> 4; matrix products, arithmetic and copies ran while one was open for 2% -> 2% of each run, Pallas kernels for 22% -> 21%
where the time goes in v4:
time: 53.7 us; the launch traced here: 53.4 us
  starting transfers between devices  29.9 us (56%)
  Pallas kernels  17.8 us (33%)
  local copies, waits for them, and re-layouts  2.65 us (5%)
  waiting for transfers between devices  2.26 us (4%)
    ppermute x9, starting transfers between devices, shift_plane(): lax.ppermute(v, AXES, pairs_of(lambda x, y, c, z: (x, (y + k) % 4, c, z)...  13.3 us
    pallas_call x2, Pallas kernels, near_half(): pl.pallas_call(functools.partial(near_kernel, turn, skip), out_shape=jax....  9.99 us
    ppermute x1, starting transfers between devices, body(): lax.ppermute(outer, AXES, [(i, i + 1) for i in range(1, 127, 2)] + [(i +...  6.28 us
    pallas_call x1, Pallas kernels, body(): pl.pallas_call(down_kernel, out_shape=jax.ShapeDtypeStruct((16, 4096), BF...  4.76 us
    ppermute x4, starting transfers between devices, body(): other = [lax.ppermute(jnp.concatenate(p, axis=0), 'c', swap) for p in parts]  4.5 us
    ppermute x2, starting transfers between devices, body(): lax.ppermute(mine, 'z', [(i, i ^ k) for i in range(4)])  3.31 us
    ppermute x1, starting transfers between devices, body(): inner = lax.ppermute(coefs, 'z', [(i, i ^ 1) for i in range(4)])  2.55 us
    unnamed x32, local copies, waits for them, and re-layouts  2.39 us
  transfers between devices with their start and end apart: 17, of which 4 were waited for; matrix products, arithmetic and copies ran while one was open for 2% of the time, Pallas kernels for 21%

profile of v4, /device:TPU:1, one launch (start us, length us, event | category | flops | bytes accessed | tf_op | source)
XLA Modules:
  0.0 53.4 jit_solution(12906178399907130858)
XLA Ops:
  0.0 1.7 %upward.1 = (bf16[25,16,128]{2,1,0:T(8,128)(2,1)S(1)}, bf16[16,16,128]{2,1,0:T(8,128)(2,1)S(1)}) custom-call(bf16[16,4096]{1,0:T(8,128)(2,1)} %dens_ref, bf16[16,64,256]{2,1,0:T(8,128)(2,1)} %basis_ref.1, bf16[2,64,512]{2,1,0:T(8,128)(2,1)} %pt_ref.1), custom_call_target="tpu_custom_call" | custom-call | tf_op jit(solution)/shard_map/upward/pallas_call | solution.py:210
  1.7 2.5 %collective-permute-start = (bf16[25,16,128]{2,1,0:T(8,128)(2,1)S(1)}, bf16[25,16,128]{2,1,0:T(8,128)(2,1)S(1)}, u32[]{:S(2)}, u32[]{:S(2)}) collective-permute-start(bf16[25,16,128]{2,1,0:T(8,128)(2,1)S(1)} %get-tuple-element.48), channel_id=1, source_target_pairs={{0,1},{1,0},{2,3},{3,2},{4,5},{5,4},{6,7},{7,6},{8,9},{9,8},{10,11... | collective-permute-start | bytes 307208 | tf_op jit(solution)/shard_map/ppermute | solution.py:257
  4.2 2.2 %collective-permute-start.1 = (bf16[9,16,128]{2,1,0:T(8,128)(2,1)S(1)}, bf16[9,16,128]{2,1,0:T(8,128)(2,1)S(1)}, u32[]{:S(2)}, u32[]{:S(2)}) collective-permute-start(bf16[9,16,128]{2,1,0:T(8,128)(2,1)S(1)} %slice.12), channel_id=1, source_target_pairs={{0,3},{1,2},{2,1},{3,0},{4,7},{5,6},{6,5},{7,4},{8,11},{9,10},{10,... | collective-permute-start | bytes 110600 | tf_op jit(solution)/shard_map/ppermute | solution.py:259
  6.5 1.1 %collective-permute-start.2 = (bf16[9,16,128]{2,1,0:T(8,128)(2,1)S(1)}, bf16[9,16,128]{2,1,0:T(8,128)(2,1)S(1)}, u32[]{:S(2)}, u32[]{:S(2)}) collective-permute-start(bf16[9,16,128]{2,1,0:T(8,128)(2,1)S(1)} %slice.12), channel_id=1, source_target_pairs={{0,2},{1,3},{2,0},{3,1},{4,6},{5,7},{6,4},{7,5},{8,10},{9,11},{10,... | collective-permute-start | bytes 110600 | tf_op jit(solution)/shard_map/ppermute | solution.py:259
  7.5 1.4 %codes.1 = (s32[8,16]{1,0:T(8,128)}, s32[16,32]{1,0:T(8,128)}, s32[2,32]{1,0:T(2,128)}, s32[6,16]{1,0:T(8,128)}) custom-call(s32[8,16]{1,0:T(8,128)} %bitcast.4, s32[8,16]{1,0:T(8,128)} %bitcast.5, s32[16,32]{1,0:T(8,128)} %ls_ref, s32[16,32]{1,0:T(8,128)} %lv_ref, s32[2,32]{1,0:T(2,128)} %ps_ref, s32[2,32]{1,0:T(2,128)} %pv_ref, s32[1,16]{1,0:T(1,128)} %gs_ref, ...), custom_call_target="tpu_custom_call" | custom-call | tf_op jit(solution)/shard_map/codes/pallas_call | solution.py:260
  9.0 0.9 %copy-done.5 = bf16[16,4096]{1,0:T(8,128)(2,1)S(1)} copy-done((bf16[16,4096]{1,0:T(8,128)(2,1)S(1)}, bf16[16,4096]{1,0:T(8,128)(2,1)}, u32[]{:S(2)}) %copy-start.5) | copy-done | bytes 131096
  9.9 0.7 %copy-done.9 = s32[8,16]{1,0:T(8,128)S(1)} copy-done((s32[8,16]{1,0:T(8,128)S(1)}, s32[8,16]{1,0:T(8,128)}, u32[]{:S(2)}) %copy-start.9) | copy-done | bytes 536
  10.5 0.0 collective-permute-done.halo_ref
  10.6 0.0 collective-permute-done.1
  10.6 0.5 collective-permute-done.2
  11.1 1.3 %collective-permute-start.3 = (bf16[36,16,128]{2,1,0:T(8,128)(2,1)S(1)}, bf16[36,16,128]{2,1,0:T(8,128)(2,1)S(1)}, u32[]{:S(2)}, u32[]{:S(2)}) collective-permute-start(bf16[36,16,128]{2,1,0:T(8,128)(2,1)S(1)} %pad_maximum_fusion.4), channel_id=1, source_target_pairs={{0,8},{1,9},{2,10},{3,11},{4,36},{5,37},{6,38},{7,39},{8,16},{9,17... | collective-permute-start | bytes 442376 | tf_op jit(solution)/shard_map/ppermute | solution.py:190
  12.4 2.5 %collective-permute-start.4 = (bf16[36,16,128]{2,1,0:T(8,128)(2,1)S(1)}, bf16[36,16,128]{2,1,0:T(8,128)(2,1)S(1)}, u32[]{:S(2)}, u32[]{:S(2)}) collective-permute-start(bf16[36,16,128]{2,1,0:T(8,128)(2,1)S(1)} %pad_maximum_fusion.4), channel_id=1, source_target_pairs={{0,16},{1,17},{2,18},{3,19},{4,68},{5,69},{6,70},{7,71},{8,24},{9,... | collective-permute-start | bytes 442376 | tf_op jit(solution)/shard_map/ppermute | solution.py:190
  14.9 1.2 %collective-permute-start.5 = (bf16[36,16,128]{2,1,0:T(8,128)(2,1)S(1)}, bf16[36,16,128]{2,1,0:T(8,128)(2,1)S(1)}, u32[]{:S(2)}, u32[]{:S(2)}) collective-permute-start(bf16[36,16,128]{2,1,0:T(8,128)(2,1)S(1)} %pad_maximum_fusion.4), channel_id=1, source_target_pairs={{0,24},{1,25},{2,26},{3,27},{4,100},{5,101},{6,102},{7,103},{8,0},... | collective-permute-start | bytes 442376 | tf_op jit(solution)/shard_map/ppermute | solution.py:190
  16.0 5.0 %near.2.near0_ref = f32[16,2048]{1,0:T(8,128)S(1)} custom-call(s32[8,16]{1,0:T(8,128)S(1)} %get-tuple-element.61.idx_ref, bf16[25,16,128]{2,1,0:T(8,128)(2,1)S(1)} %collective-permute-done.halo_ref, bf16[16,16,256]{2,1,0:T(8,128)(2,1)S(1)} %get-tuple-element.57.tiles_ref, bf16[16,2048,256]{2,1,0:T(8,128)(2,1)} %blocks_hbm.3), custom_call_target="tpu_custom_call" | custom-call | flops 134217728 | bytes 8700000 | tf_op jit(solution)/shard_map/near/pallas_call | solution.py:232
  21.0 0.0 collective-permute-done.3
  21.0 0.0 collective-permute-done.4
  21.0 0.0 collective-permute-done.5
  21.1 0.1 pad_maximum_fusion
  21.1 0.1 fusion
  21.3 1.4 %collective-permute-start.6 = (bf16[72,16,128]{2,1,0:T(8,128)(2,1)S(1)}, bf16[72,16,128]{2,1,0:T(8,128)(2,1)S(1)}, u32[]{:S(2)}, u32[]{:S(2)}) collective-permute-start(bf16[72,16,128]{2,1,0:T(8,128)(2,1)S(1)} %get-tuple-element.68), channel_id=1, source_target_pairs={{0,32},{1,33},{2,34},{3,35},{4,12},{5,13},{6,14},{7,15},{8,40},{9,... | collective-permute-start | bytes 884744 | tf_op jit(solution)/shard_map/ppermute | solution.py:190
  22.6 1.5 %collective-permute-start.7 = (bf16[72,16,128]{2,1,0:T(8,128)(2,1)S(1)}, bf16[72,16,128]{2,1,0:T(8,128)(2,1)S(1)}, u32[]{:S(2)}, u32[]{:S(2)}) collective-permute-start(bf16[72,16,128]{2,1,0:T(8,128)(2,1)S(1)} %get-tuple-element.67), channel_id=1, source_target_pairs={{0,96},{1,97},{2,98},{3,99},{4,28},{5,29},{6,30},{7,31},{8,104},{9... | collective-permute-start | bytes 884744 | tf_op jit(solution)/shard_map/ppermute | solution.py:190
  24.1 0.1 pad_add_fusion.own_ref
  24.2 6.3 %collective-permute-start.10 = (bf16[16,16,128]{2,1,0:T(8,128)(2,1)S(1)}, bf16[16,16,128]{2,1,0:T(8,128)(2,1)S(1)}, u32[]{:S(2)}, u32[]{:S(2)}) collective-permute-start(bf16[16,16,128]{2,1,0:T(8,128)(2,1)S(1)} %get-tuple-element.62), channel_id=1, source_target_pairs={{1,2},{3,4},{5,6},{7,8},{9,10},{11,12},{13,14},{15,16},{17,18},{19... | collective-permute-start | bytes 196616 | tf_op jit(solution)/shard_map/ppermute | solution.py:283
  30.5 0.5 collective-permute-start.8
  31.0 2.3 %collective-permute-start.9 = (bf16[72,16,128]{2,1,0:T(8,128)(2,1)S(1)}, bf16[72,16,128]{2,1,0:T(8,128)(2,1)S(1)}, u32[]{:S(2)}, u32[]{:S(2)}) collective-permute-start(bf16[72,16,128]{2,1,0:T(8,128)(2,1)S(1)} %get-tuple-element.68), channel_id=1, source_target_pairs={{0,96},{1,97},{2,98},{3,99},{4,28},{5,29},{6,30},{7,31},{8,104},{9... | collective-permute-start | bytes 884744 | tf_op jit(solution)/shard_map/ppermute | solution.py:190
  33.3 0.1 constant_dynamic-update-slice_fusion.10
  33.4 0.0 collective-permute-done.6
  33.4 0.1 collective-permute-start.13
  33.5 0.0 collective-permute-done.7
  33.5 0.1 collective-permute-start.11
  33.6 0.0 collective-permute-done.10.halo_ref
  33.6 2.7 %collective-permute-start.12 = (bf16[72,16,128]{2,1,0:T(8,128)(2,1)S(1)}, bf16[72,16,128]{2,1,0:T(8,128)(2,1)S(1)}, u32[]{:S(2)}, u32[]{:S(2)}) collective-permute-start(bf16[72,16,128]{2,1,0:T(8,128)(2,1)S(1)} %collective-permute-done.7), channel_id=1, source_target_pairs={{0,96},{1,97},{2,98},{3,99},{4,28},{5,29},{6,30},{7,31},{8,104},{9... | collective-permute-start | bytes 884744 | tf_op jit(solution)/shard_map/ppermute | solution.py:190
  36.3 5.0 %near.3.near1_ref = f32[16,2048]{1,0:T(8,128)S(1)} custom-call(s32[8,16]{1,0:T(8,128)S(1)} %get-tuple-element.61.idx_ref, bf16[16,16,128]{2,1,0:T(8,128)(2,1)S(1)} %collective-permute-done.10.halo_ref, bf16[16,16,256]{2,1,0:T(8,128)(2,1)S(1)} %get-tuple-element.57.tiles_ref, bf16[16,2048,256]{2,1,0:T(8,128)(2,1)} %blocks_hbm.3), custom_call_target="tpu_custom_call" | custom-call | flops 134217728 | bytes 8700000 | tf_op jit(solution)/shard_map/near/pallas_call | solution.py:232
  41.4 0.1 pad_maximum_fusion.1
  41.5 0.0 copy-start
  41.5 0.0 copy-start.1
  41.5 0.0 copy-start.2
  41.5 0.0 copy-start.3
  41.5 0.0 copy-start.4
  41.5 0.0 copy-start.6
  41.5 0.0 copy-start.7
  41.5 0.0 copy-start.8
  41.5 0.0 copy-start.10
  41.6 0.0 collective-permute-done.8
  41.6 0.0 collective-permute-done.9
  41.6 3.6 %collective-permute-start.14 = (bf16[144,16,128]{2,1,0:T(8,128)(2,1)S(1)}, bf16[144,16,128]{2,1,0:T(8,128)(2,1)S(1)}, u32[]{:S(2)}, u32[]{:S(2)}) collective-permute-start(bf16[144,16,128]{2,1,0:T(8,128)(2,1)S(1)} %pad_maximum_fusion.1), channel_id=1, source_target_pairs={{0,4},{4,0},{1,5},{5,1},{2,6},{6,2},{3,7},{7,3},{8,12},{12,8},{9,1... | collective-permute-start | bytes 1769480 | tf_op jit(solution)/shard_map/ppermute | solution.py:299
  45.1 0.1 pad_maximum_fusion.2
  45.2 0.1 collective-permute-start.15
  45.4 0.0 collective-permute-done.11
  45.4 0.0 collective-permute-done.12
  45.4 0.1 pad_maximum_fusion.3
  45.5 0.8 %collective-permute-start.16 = (bf16[144,16,128]{2,1,0:T(8,128)(2,1)S(1)}, bf16[144,16,128]{2,1,0:T(8,128)(2,1)S(1)}, u32[]{:S(2)}, u32[]{:S(2)}) collective-permute-start(bf16[144,16,128]{2,1,0:T(8,128)(2,1)S(1)} %pad_maximum_fusion.3), channel_id=1, source_target_pairs={{0,4},{4,0},{1,5},{5,1},{2,6},{6,2},{3,7},{7,3},{8,12},{12,8},{9,1... | collective-permute-start | bytes 1769480 | tf_op jit(solution)/shard_map/ppermute | solution.py:299
  46.3 0.0 collective-permute-done.13
  46.3 0.1 constant_dynamic-update-slice_fusion.3
  46.5 0.3 collective-permute-done.14
  46.8 0.1 constant_dynamic-update-slice_fusion.2
  46.9 0.7 %collective-permute-done.15 = bf16[144,16,128]{2,1,0:T(8,128)(2,1)S(1)} collective-permute-done((bf16[144,16,128]{2,1,0:T(8,128)(2,1)S(1)}, bf16[144,16,128]{2,1,0:T(8,128)(2,1)S(1)}, u32[]{:S(2)}, u32[]{:S(2)}) %collective-permute-start.15) | collective-permute-done | bytes 589856 | tf_op jit(solution)/shard_map/ppermute | solution.py:299
  47.6 0.1 constant_dynamic-update-slice_fusion.1
  47.8 0.7 %collective-permute-done.16 = bf16[144,16,128]{2,1,0:T(8,128)(2,1)S(1)} collective-permute-done((bf16[144,16,128]{2,1,0:T(8,128)(2,1)S(1)}, bf16[144,16,128]{2,1,0:T(8,128)(2,1)S(1)}, u32[]{:S(2)}, u32[]{:S(2)}) %collective-permute-start.16) | collective-permute-done | bytes 589856 | tf_op jit(solution)/shard_map/ppermute | solution.py:299
  48.5 0.1 constant_dynamic-update-slice_fusion.table
  48.6 0.0 copy-done
  48.6 0.0 copy-done.1
  48.6 0.0 copy-done.2
  48.7 4.8 %downward.1 = bf16[16,4096]{1,0:T(8,128)(2,1)} custom-call(s32[16,32]{1,0:T(8,128)S(1)} %copy-done.7, s32[2,32]{1,0:T(2,128)S(1)} %copy-done.10, s32[6,16]{1,0:T(8,128)S(1)} %copy-done.8, s32[2]{0:T(128)S(1)} %pad_add_fusion.own_ref, bf16[1152,16,128]{2,1,0:T(8,128)(2,1)S(1)} %constant_dynamic-update-slice_fusion.table, bf16[16,64,2048]{2,1,0:T(8,128)(2,1)S(1)} %copy-done, ...), custom_call_target="tpu_custom_call" | custom-call | tf_op jit(solution)/shard_map/downward/pallas_call | solution.py:302
  (18 shorter events, 0.3 us)
Async XLA Ops:
  1.7 8.9 %collective-permute-start = (bf16[25,16,128]{2,1,0:T(8,128)(2,1)S(1)}, bf16[25,16,128]{2,1,0:T(8,128)(2,1)S(1)}, u32[]{:S(2)}, u32[]{:S(2)}) collective-permute-start(bf16[25,16,128]{2,1,0:T(8,128)(2,1)S(1)} %get-tuple-element.48), channel_id=1, source_target_pairs={{0,1},{1,0},{2,3},{3,2},{4,5},{5,4},{6,7},{7,6},{8,9},{9,8},{10,11... | collective-permute-start | bytes 307208 | tf_op jit(solution)/shard_map/ppermute | solution.py:257
  4.2 6.3 %collective-permute-start.1 = (bf16[9,16,128]{2,1,0:T(8,128)(2,1)S(1)}, bf16[9,16,128]{2,1,0:T(8,128)(2,1)S(1)}, u32[]{:S(2)}, u32[]{:S(2)}) collective-permute-start(bf16[9,16,128]{2,1,0:T(8,128)(2,1)S(1)} %slice.12), channel_id=1, source_target_pairs={{0,3},{1,2},{2,1},{3,0},{4,7},{5,6},{6,5},{7,4},{8,11},{9,10},{10,... | collective-permute-start | bytes 110600 | tf_op jit(solution)/shard_map/ppermute | solution.py:259
  6.5 4.6 %collective-permute-start.2 = (bf16[9,16,128]{2,1,0:T(8,128)(2,1)S(1)}, bf16[9,16,128]{2,1,0:T(8,128)(2,1)S(1)}, u32[]{:S(2)}, u32[]{:S(2)}) collective-permute-start(bf16[9,16,128]{2,1,0:T(8,128)(2,1)S(1)} %slice.12), channel_id=1, source_target_pairs={{0,2},{1,3},{2,0},{3,1},{4,6},{5,7},{6,4},{7,5},{8,10},{9,11},{10,... | collective-permute-start | bytes 110600 | tf_op jit(solution)/shard_map/ppermute | solution.py:259
  9.0 0.9 %copy-start.5 = (bf16[16,4096]{1,0:T(8,128)(2,1)S(1)}, bf16[16,4096]{1,0:T(8,128)(2,1)}, u32[]{:S(2)}) copy-start(bf16[16,4096]{1,0:T(8,128)(2,1)} %dens_ref) | copy-start | bytes 393220
  9.9 0.7 %copy-start.9 = (s32[8,16]{1,0:T(8,128)S(1)}, s32[8,16]{1,0:T(8,128)}, u32[]{:S(2)}) copy-start(s32[8,16]{1,0:T(8,128)} %get-tuple-element.50.code_ref) | copy-start | bytes 1540
  11.1 9.9 %collective-permute-start.3 = (bf16[36,16,128]{2,1,0:T(8,128)(2,1)S(1)}, bf16[36,16,128]{2,1,0:T(8,128)(2,1)S(1)}, u32[]{:S(2)}, u32[]{:S(2)}) collective-permute-start(bf16[36,16,128]{2,1,0:T(8,128)(2,1)S(1)} %pad_maximum_fusion.4), channel_id=1, source_target_pairs={{0,8},{1,9},{2,10},{3,11},{4,36},{5,37},{6,38},{7,39},{8,16},{9,17... | collective-permute-start | bytes 442376 | tf_op jit(solution)/shard_map/ppermute | solution.py:190
  12.4 8.6 %collective-permute-start.4 = (bf16[36,16,128]{2,1,0:T(8,128)(2,1)S(1)}, bf16[36,16,128]{2,1,0:T(8,128)(2,1)S(1)}, u32[]{:S(2)}, u32[]{:S(2)}) collective-permute-start(bf16[36,16,128]{2,1,0:T(8,128)(2,1)S(1)} %pad_maximum_fusion.4), channel_id=1, source_target_pairs={{0,16},{1,17},{2,18},{3,19},{4,68},{5,69},{6,70},{7,71},{8,24},{9,... | collective-permute-start | bytes 442376 | tf_op jit(solution)/shard_map/ppermute | solution.py:190
  14.9 6.2 %collective-permute-start.5 = (bf16[36,16,128]{2,1,0:T(8,128)(2,1)S(1)}, bf16[36,16,128]{2,1,0:T(8,128)(2,1)S(1)}, u32[]{:S(2)}, u32[]{:S(2)}) collective-permute-start(bf16[36,16,128]{2,1,0:T(8,128)(2,1)S(1)} %pad_maximum_fusion.4), channel_id=1, source_target_pairs={{0,24},{1,25},{2,26},{3,27},{4,100},{5,101},{6,102},{7,103},{8,0},... | collective-permute-start | bytes 442376 | tf_op jit(solution)/shard_map/ppermute | solution.py:190
  21.3 12.1 %collective-permute-start.6 = (bf16[72,16,128]{2,1,0:T(8,128)(2,1)S(1)}, bf16[72,16,128]{2,1,0:T(8,128)(2,1)S(1)}, u32[]{:S(2)}, u32[]{:S(2)}) collective-permute-start(bf16[72,16,128]{2,1,0:T(8,128)(2,1)S(1)} %get-tuple-element.68), channel_id=1, source_target_pairs={{0,32},{1,33},{2,34},{3,35},{4,12},{5,13},{6,14},{7,15},{8,40},{9,... | collective-permute-start | bytes 884744 | tf_op jit(solution)/shard_map/ppermute | solution.py:190
  22.6 10.8 %collective-permute-start.7 = (bf16[72,16,128]{2,1,0:T(8,128)(2,1)S(1)}, bf16[72,16,128]{2,1,0:T(8,128)(2,1)S(1)}, u32[]{:S(2)}, u32[]{:S(2)}) collective-permute-start(bf16[72,16,128]{2,1,0:T(8,128)(2,1)S(1)} %get-tuple-element.67), channel_id=1, source_target_pairs={{0,96},{1,97},{2,98},{3,99},{4,28},{5,29},{6,30},{7,31},{8,104},{9... | collective-permute-start | bytes 884744 | tf_op jit(solution)/shard_map/ppermute | solution.py:190
  24.2 9.4 %collective-permute-start.10 = (bf16[16,16,128]{2,1,0:T(8,128)(2,1)S(1)}, bf16[16,16,128]{2,1,0:T(8,128)(2,1)S(1)}, u32[]{:S(2)}, u32[]{:S(2)}) collective-permute-start(bf16[16,16,128]{2,1,0:T(8,128)(2,1)S(1)} %get-tuple-element.62), channel_id=1, source_target_pairs={{1,2},{3,4},{5,6},{7,8},{9,10},{11,12},{13,14},{15,16},{17,18},{19... | collective-permute-start | bytes 196616 | tf_op jit(solution)/shard_map/ppermute | solution.py:283
  30.5 11.1 %collective-permute-start.8 = (bf16[72,16,128]{2,1,0:T(8,128)(2,1)S(1)}, bf16[72,16,128]{2,1,0:T(8,128)(2,1)S(1)}, u32[]{:S(2)}, u32[]{:S(2)}) collective-permute-start(bf16[72,16,128]{2,1,0:T(8,128)(2,1)S(1)} %get-tuple-element.67), channel_id=1, source_target_pairs={{0,32},{1,33},{2,34},{3,35},{4,12},{5,13},{6,14},{7,15},{8,40},{9,... | collective-permute-start | bytes 884744 | tf_op jit(solution)/shard_map/ppermute | solution.py:190
  31.0 10.6 %collective-permute-start.9 = (bf16[72,16,128]{2,1,0:T(8,128)(2,1)S(1)}, bf16[72,16,128]{2,1,0:T(8,128)(2,1)S(1)}, u32[]{:S(2)}, u32[]{:S(2)}) collective-permute-start(bf16[72,16,128]{2,1,0:T(8,128)(2,1)S(1)} %get-tuple-element.68), channel_id=1, source_target_pairs={{0,96},{1,97},{2,98},{3,99},{4,28},{5,29},{6,30},{7,31},{8,104},{9... | collective-permute-start | bytes 884744 | tf_op jit(solution)/shard_map/ppermute | solution.py:190
  33.4 12.9 %collective-permute-start.13 = (bf16[144,16,128]{2,1,0:T(8,128)(2,1)S(1)}, bf16[144,16,128]{2,1,0:T(8,128)(2,1)S(1)}, u32[]{:S(2)}, u32[]{:S(2)}) collective-permute-start(bf16[144,16,128]{2,1,0:T(8,128)(2,1)S(1)} %pad_maximum_fusion), channel_id=1, source_target_pairs={{0,4},{4,0},{1,5},{5,1},{2,6},{6,2},{3,7},{7,3},{8,12},{12,8},{9,1... | collective-permute-start | bytes 1769480 | tf_op jit(solution)/shard_map/ppermute | solution.py:299
  33.5 11.9 %collective-permute-start.11 = (bf16[72,16,128]{2,1,0:T(8,128)(2,1)S(1)}, bf16[72,16,128]{2,1,0:T(8,128)(2,1)S(1)}, u32[]{:S(2)}, u32[]{:S(2)}) collective-permute-start(bf16[72,16,128]{2,1,0:T(8,128)(2,1)S(1)} %collective-permute-done.6), channel_id=1, source_target_pairs={{0,32},{1,33},{2,34},{3,35},{4,12},{5,13},{6,14},{7,15},{8,40},{9,... | collective-permute-start | bytes 884744 | tf_op jit(solution)/shard_map/ppermute | solution.py:190
  33.6 11.8 %collective-permute-start.12 = (bf16[72,16,128]{2,1,0:T(8,128)(2,1)S(1)}, bf16[72,16,128]{2,1,0:T(8,128)(2,1)S(1)}, u32[]{:S(2)}, u32[]{:S(2)}) collective-permute-start(bf16[72,16,128]{2,1,0:T(8,128)(2,1)S(1)} %collective-permute-done.7), channel_id=1, source_target_pairs={{0,96},{1,97},{2,98},{3,99},{4,28},{5,29},{6,30},{7,31},{8,104},{9... | collective-permute-start | bytes 884744 | tf_op jit(solution)/shard_map/ppermute | solution.py:190
  41.5 7.2 %copy-start = (bf16[16,64,2048]{2,1,0:T(8,128)(2,1)S(1)}, bf16[16,64,2048]{2,1,0:T(8,128)(2,1)}, u32[]{:S(2)}) copy-start(bf16[16,64,2048]{2,1,0:T(8,128)(2,1)} %lc.1) | copy-start | bytes 12582916
  41.5 7.1 %copy-start.1 = (bf16[16,64,256]{2,1,0:T(8,128)(2,1)S(1)}, bf16[16,64,256]{2,1,0:T(8,128)(2,1)}, u32[]{:S(2)}) copy-start(bf16[16,64,256]{2,1,0:T(8,128)(2,1)} %basis_ref.1) | copy-start | bytes 1572868
  41.5 7.1 %copy-start.2 = (bf16[32,64,512]{2,1,0:T(8,128)(2,1)S(1)}, bf16[32,64,512]{2,1,0:T(8,128)(2,1)}, u32[]{:S(2)}) copy-start(bf16[32,64,512]{2,1,0:T(8,128)(2,1)} %gt.1) | copy-start | bytes 6291460
  41.5 7.1 %copy-start.3 = (bf16[2,64,512]{2,1,0:T(8,128)(2,1)S(1)}, bf16[2,64,512]{2,1,0:T(8,128)(2,1)}, u32[]{:S(2)}) copy-start(bf16[2,64,512]{2,1,0:T(8,128)(2,1)} %pt_ref.1) | copy-start | bytes 393220
  41.5 7.1 %copy-start.4 = (bf16[2,64,2048]{2,1,0:T(8,128)(2,1)S(1)}, bf16[2,64,2048]{2,1,0:T(8,128)(2,1)}, u32[]{:S(2)}) copy-start(bf16[2,64,2048]{2,1,0:T(8,128)(2,1)} %pc.1) | copy-start | bytes 1572868
  41.5 7.1 %copy-start.6 = (bf16[1,64,1024]{2,1,0:T(8,128)(2,1)S(1)}, bf16[1,64,1024]{2,1,0:T(8,128)(2,1)}, u32[]{:S(2)}) copy-start(bf16[1,64,1024]{2,1,0:T(8,128)(2,1)} %gc.1) | copy-start | bytes 393220
  41.5 7.1 %copy-start.7 = (s32[16,32]{1,0:T(8,128)S(1)}, s32[16,32]{1,0:T(8,128)}, u32[]{:S(2)}) copy-start(s32[16,32]{1,0:T(8,128)} %get-tuple-element.45.leaf_ref) | copy-start | bytes 6148
  41.5 7.1 %copy-start.8 = (s32[6,16]{1,0:T(8,128)S(1)}, s32[6,16]{1,0:T(8,128)}, u32[]{:S(2)}) copy-start(s32[6,16]{1,0:T(8,128)} %get-tuple-element.47.grand_ref) | copy-start | bytes 1156
  41.5 7.1 %copy-start.10 = (s32[2,32]{1,0:T(2,128)S(1)}, s32[2,32]{1,0:T(2,128)}, u32[]{:S(2)}) copy-start(s32[2,32]{1,0:T(2,128)} %get-tuple-element.46.parent_ref) | copy-start | bytes 772
  41.6 5.2 %collective-permute-start.14 = (bf16[144,16,128]{2,1,0:T(8,128)(2,1)S(1)}, bf16[144,16,128]{2,1,0:T(8,128)(2,1)S(1)}, u32[]{:S(2)}, u32[]{:S(2)}) collective-permute-start(bf16[144,16,128]{2,1,0:T(8,128)(2,1)S(1)} %pad_maximum_fusion.1), channel_id=1, source_target_pairs={{0,4},{4,0},{1,5},{5,1},{2,6},{6,2},{3,7},{7,3},{8,12},{12,8},{9,1... | collective-permute-start | bytes 1769480 | tf_op jit(solution)/shard_map/ppermute | solution.py:299
  45.2 2.4 %collective-permute-start.15 = (bf16[144,16,128]{2,1,0:T(8,128)(2,1)S(1)}, bf16[144,16,128]{2,1,0:T(8,128)(2,1)S(1)}, u32[]{:S(2)}, u32[]{:S(2)}) collective-permute-start(bf16[144,16,128]{2,1,0:T(8,128)(2,1)S(1)} %pad_maximum_fusion.2), channel_id=1, source_target_pairs={{0,4},{4,0},{1,5},{5,1},{2,6},{6,2},{3,7},{7,3},{8,12},{12,8},{9,1... | collective-permute-start | bytes 1769480 | tf_op jit(solution)/shard_map/ppermute | solution.py:299
  45.5 3.0 %collective-permute-start.16 = (bf16[144,16,128]{2,1,0:T(8,128)(2,1)S(1)}, bf16[144,16,128]{2,1,0:T(8,128)(2,1)S(1)}, u32[]{:S(2)}, u32[]{:S(2)}) collective-permute-start(bf16[144,16,128]{2,1,0:T(8,128)(2,1)S(1)} %pad_maximum_fusion.3), channel_id=1, source_target_pairs={{0,4},{4,0},{1,5},{5,1},{2,6},{6,2},{3,7},{7,3},{8,12},{12,8},{9,1... | collective-permute-start | bytes 1769480 | tf_op jit(solution)/shard_map/ppermute | solution.py:299

commit v5 on v4

--- a/solution.py
+++ b/solution.py
@@ -152,21 +152,7 @@
         kind = jnp.where(low, first, second) & 3
         return jnp.where(kind == 2, straight, jnp.where(kind == 3, crossed, zero))
 
-    ups = []
-    for j in range(16):
-        children = jnp.concatenate([table[grand_ref[1 + z, j]] for z in range(4)], axis=1)
-        up = dot_t(children, gt[grand_ref[0, j]])
-        ups.append(jnp.where(grand_ref[5, j] == 1, up, 0.0).astype(BF16))
-    grand_total = dot_t(jnp.concatenate(ups, axis=1), gc[0]).astype(BF16)
-    down_two = dot(grand_total, gt[own_ref[0], :, pl.ds(pl.multiple_of(own_ref[1] * 128, 128), 128)])
-
-    down_one = []
-    for p in range(2):
-        coefs = jnp.concatenate([pair_tile(parent_ref, p, 2 * i) for i in range(16)], axis=1)
-        far = dot_t(coefs, pc[p])
-        total = (far + down_two[:, p * 64 : (p + 1) * 64]).astype(BF16)
-        down_one.append(dot(total, pt_ref[p]))
-
+    fars = []
     for g in range(4):
         coefs = jnp.concatenate(
             [
@@ -175,7 +161,25 @@
             ],
             axis=0,
         )
-        far = dot_t(coefs, lc[4 * g : 4 * g + 4].reshape(256, 2048))
+        fars.append(dot_t(coefs, lc[4 * g : 4 * g + 4].reshape(256, 2048)))
+
+    ups = []
+    for j in range(16):
+        children = jnp.concatenate([table[grand_ref[1 + z, j]] for z in range(4)], axis=1)
+        up = dot_t(children, gt[grand_ref[0, j]])
+        ups.append(jnp.where(grand_ref[5, j] == 1, up, 0.0).astype(BF16))
+    grand_total = dot_t(jnp.concatenate(ups, axis=1), gc[0]).astype(BF16)
+    down_two = dot(grand_total, gt[own_ref[0], :, pl.ds(pl.multiple_of(own_ref[1] * 128, 128), 128)])
+
+    down_one = []
+    for p in range(2):
+        coefs = jnp.concatenate([pair_tile(parent_ref, p, 2 * i) for i in range(16)], axis=1)
+        far = dot_t(coefs, pc[p])
+        total = (far + down_two[:, p * 64 : (p + 1) * 64]).astype(BF16)
+        down_one.append(dot(total, pt_ref[p]))
+
+    for g in range(4):
+        far = fars[g]
         for k in range(4):
             t = 4 * g + k
             total = far[k * 16 : (k + 1) * 16, k * 64 : (k + 1) * 64]
@@ -287,16 +291,17 @@
     steps = [shift_plane(coefs, k, 0) for k in (1, 2, 3)]
     near0 = near_half(0, TILES, inner, near_code)
     coefs, near0 = barrier((jnp.concatenate([coefs] + steps, axis=0), near0))
+    own_swap = lax.ppermute(coefs, "c", swap)
 
     first, second = coefs[:HALF], coefs[HALF:]
     ahead1, back2 = shift_plane(first, 1, 1), shift_plane(second, 3, 1)
     ahead2, back1 = shift_plane(second, 1, 1), shift_plane(first, 3, 1)
-    ahead1, back2, near_code = barrier((ahead1, back2, near_code))
+    ahead1, back2, near_code, own_swap = barrier((ahead1, back2, near_code, own_swap))
     far1, far2 = shift_plane(ahead1, 1, 1), shift_plane(back2, 3, 1)
     near1 = near_half(1, 0, outer, near_code)
     ahead2, back1, near1 = barrier((ahead2, back1, near1))
     parts = [[coefs], [ahead1, back2], [ahead2, back1], [far1, far2]]
-    other = [lax.ppermute(jnp.concatenate(p, axis=0), "c", swap) for p in parts]
+    other = [own_swap] + [lax.ppermute(jnp.concatenate(p, axis=0), "c", swap) for p in parts[1:]]
     table = jnp.concatenate(sum(parts, []) + other, axis=0)
 
     return pl.pallas_call(

time: 53.7 us -> 51.2 us (0.953)
  starting transfers between devices: 29.9 us -> 28.5 us
  waiting for transfers between devices: 2.26 us -> 1.64 us
    ppermute x1, starting transfers between devices: 6.28 us -> 3.37 us  [body(): lax.ppermute(outer, AXES, [(i, i + 1) for i in range(1, 127, 2)] + [(i +...]
    ppermute x4, starting transfers between devices: 4.5 us -> 7.33 us  [the longest x3 4.17 us: body(): lax.ppermute(jnp.concatenate(p, axis=0), 'c', swap)]
    ppermute x9, starting transfers between devices: 13.3 us -> 12 us  [shift_plane(): lax.ppermute(v, AXES, pairs_of(lambda x, y, c, z: (x, (y + k) % 4, c, z)...]
    ppermute x4, waiting for transfers between devices: 1.7 us -> 1.08 us  [the longest x3 1.08 us: body(): lax.ppermute(jnp.concatenate(p, axis=0), 'c', swap)]
  transfers between devices with their start and end apart: 17 -> 17, of which waited for: 4 -> 2; matrix products, arithmetic and copies ran while one was open for 2% -> 2% of each run, Pallas kernels for 21% -> 22%
where the time goes in v5:
time: 51.2 us; the launch traced here: 50.9 us
  starting transfers between devices  28.5 us (56%)
  Pallas kernels  17.4 us (34%)
  local copies, waits for them, and re-layouts  2.65 us (5%)
  waiting for transfers between devices  1.64 us (3%)
    ppermute x9, starting transfers between devices, shift_plane(): lax.ppermute(v, AXES, pairs_of(lambda x, y, c, z: (x, (y + k) % 4, c, z)...  12 us
    pallas_call x2, Pallas kernels, near_half(): pl.pallas_call(functools.partial(near_kernel, turn, skip), out_shape=jax....  9.99 us
    pallas_call x1, Pallas kernels, body(): pl.pallas_call(down_kernel, out_shape=jax.ShapeDtypeStruct((16, 4096), BF...  4.32 us
    ppermute x3, starting transfers between devices, body(): lax.ppermute(jnp.concatenate(p, axis=0), 'c', swap)  4.17 us
    ppermute x1, starting transfers between devices, body(): lax.ppermute(outer, AXES, [(i, i + 1) for i in range(1, 127, 2)] + [(i +...  3.37 us
    ppermute x2, starting transfers between devices, body(): lax.ppermute(mine, 'z', [(i, i ^ k) for i in range(4)])  3.31 us
    ppermute x1, starting transfers between devices, body(): own_swap = lax.ppermute(coefs, 'c', swap)  3.16 us
    ppermute x1, starting transfers between devices, body(): inner = lax.ppermute(coefs, 'z', [(i, i ^ 1) for i in range(4)])  2.55 us
  transfers between devices with their start and end apart: 17, of which 2 were waited for; matrix products, arithmetic and copies ran while one was open for 2% of the time, Pallas kernels for 22%

profile of v5, /device:TPU:1, one launch (start us, length us, event | category | flops | bytes accessed | tf_op | source)
XLA Modules:
  0.0 50.9 jit_solution(10233646218240260271)
XLA Ops:
  0.0 1.7 %upward.1 = (bf16[25,16,128]{2,1,0:T(8,128)(2,1)S(1)}, bf16[16,16,128]{2,1,0:T(8,128)(2,1)S(1)}) custom-call(bf16[16,4096]{1,0:T(8,128)(2,1)} %dens_ref, bf16[16,64,256]{2,1,0:T(8,128)(2,1)} %basis_ref.1, bf16[2,64,512]{2,1,0:T(8,128)(2,1)} %pt_ref.1), custom_call_target="tpu_custom_call" | custom-call | tf_op jit(solution)/shard_map/upward/pallas_call | solution.py:214
  1.7 2.5 %collective-permute-start = (bf16[25,16,128]{2,1,0:T(8,128)(2,1)S(1)}, bf16[25,16,128]{2,1,0:T(8,128)(2,1)S(1)}, u32[]{:S(2)}, u32[]{:S(2)}) collective-permute-start(bf16[25,16,128]{2,1,0:T(8,128)(2,1)S(1)} %get-tuple-element.49), channel_id=1, source_target_pairs={{0,1},{1,0},{2,3},{3,2},{4,5},{5,4},{6,7},{7,6},{8,9},{9,8},{10,11... | collective-permute-start | bytes 307208 | tf_op jit(solution)/shard_map/ppermute | solution.py:261
  4.2 2.2 %collective-permute-start.1 = (bf16[9,16,128]{2,1,0:T(8,128)(2,1)S(1)}, bf16[9,16,128]{2,1,0:T(8,128)(2,1)S(1)}, u32[]{:S(2)}, u32[]{:S(2)}) collective-permute-start(bf16[9,16,128]{2,1,0:T(8,128)(2,1)S(1)} %slice.12), channel_id=1, source_target_pairs={{0,3},{1,2},{2,1},{3,0},{4,7},{5,6},{6,5},{7,4},{8,11},{9,10},{10,... | collective-permute-start | bytes 110600 | tf_op jit(solution)/shard_map/ppermute | solution.py:263
  6.5 1.1 %collective-permute-start.2 = (bf16[9,16,128]{2,1,0:T(8,128)(2,1)S(1)}, bf16[9,16,128]{2,1,0:T(8,128)(2,1)S(1)}, u32[]{:S(2)}, u32[]{:S(2)}) collective-permute-start(bf16[9,16,128]{2,1,0:T(8,128)(2,1)S(1)} %slice.12), channel_id=1, source_target_pairs={{0,2},{1,3},{2,0},{3,1},{4,6},{5,7},{6,4},{7,5},{8,10},{9,11},{10,... | collective-permute-start | bytes 110600 | tf_op jit(solution)/shard_map/ppermute | solution.py:263
  7.5 1.4 %codes.1 = (s32[8,16]{1,0:T(8,128)}, s32[16,32]{1,0:T(8,128)}, s32[2,32]{1,0:T(2,128)}, s32[6,16]{1,0:T(8,128)}) custom-call(s32[8,16]{1,0:T(8,128)} %bitcast.4, s32[8,16]{1,0:T(8,128)} %bitcast.5, s32[16,32]{1,0:T(8,128)} %ls_ref, s32[16,32]{1,0:T(8,128)} %lv_ref, s32[2,32]{1,0:T(2,128)} %ps_ref, s32[2,32]{1,0:T(2,128)} %pv_ref, s32[1,16]{1,0:T(1,128)} %gs_ref, ...), custom_call_target="tpu_custom_call" | custom-call | tf_op jit(solution)/shard_map/codes/pallas_call | solution.py:264
  9.0 0.9 %copy-done.5 = bf16[16,4096]{1,0:T(8,128)(2,1)S(1)} copy-done((bf16[16,4096]{1,0:T(8,128)(2,1)S(1)}, bf16[16,4096]{1,0:T(8,128)(2,1)}, u32[]{:S(2)}) %copy-start.5) | copy-done | bytes 131096
  9.9 0.7 %copy-done.9 = s32[8,16]{1,0:T(8,128)S(1)} copy-done((s32[8,16]{1,0:T(8,128)S(1)}, s32[8,16]{1,0:T(8,128)}, u32[]{:S(2)}) %copy-start.9) | copy-done | bytes 536
  10.5 0.0 collective-permute-done.halo_ref
  10.6 0.0 collective-permute-done.1
  10.6 0.5 %collective-permute-done.2 = bf16[9,16,128]{2,1,0:T(8,128)(2,1)S(1)} collective-permute-done((bf16[9,16,128]{2,1,0:T(8,128)(2,1)S(1)}, bf16[9,16,128]{2,1,0:T(8,128)(2,1)S(1)}, u32[]{:S(2)}, u32[]{:S(2)}) %collective-permute-start.2) | collective-permute-done | bytes 36896 | tf_op jit(solution)/shard_map/ppermute | solution.py:263
  11.1 1.3 %collective-permute-start.3 = (bf16[36,16,128]{2,1,0:T(8,128)(2,1)S(1)}, bf16[36,16,128]{2,1,0:T(8,128)(2,1)S(1)}, u32[]{:S(2)}, u32[]{:S(2)}) collective-permute-start(bf16[36,16,128]{2,1,0:T(8,128)(2,1)S(1)} %pad_maximum_fusion.4), channel_id=1, source_target_pairs={{0,8},{1,9},{2,10},{3,11},{4,36},{5,37},{6,38},{7,39},{8,16},{9,17... | collective-permute-start | bytes 442376 | tf_op jit(solution)/shard_map/ppermute | solution.py:194
  12.4 2.5 %collective-permute-start.4 = (bf16[36,16,128]{2,1,0:T(8,128)(2,1)S(1)}, bf16[36,16,128]{2,1,0:T(8,128)(2,1)S(1)}, u32[]{:S(2)}, u32[]{:S(2)}) collective-permute-start(bf16[36,16,128]{2,1,0:T(8,128)(2,1)S(1)} %pad_maximum_fusion.4), channel_id=1, source_target_pairs={{0,16},{1,17},{2,18},{3,19},{4,68},{5,69},{6,70},{7,71},{8,24},{9,... | collective-permute-start | bytes 442376 | tf_op jit(solution)/shard_map/ppermute | solution.py:194
  14.9 1.2 %collective-permute-start.5 = (bf16[36,16,128]{2,1,0:T(8,128)(2,1)S(1)}, bf16[36,16,128]{2,1,0:T(8,128)(2,1)S(1)}, u32[]{:S(2)}, u32[]{:S(2)}) collective-permute-start(bf16[36,16,128]{2,1,0:T(8,128)(2,1)S(1)} %pad_maximum_fusion.4), channel_id=1, source_target_pairs={{0,24},{1,25},{2,26},{3,27},{4,100},{5,101},{6,102},{7,103},{8,0},... | collective-permute-start | bytes 442376 | tf_op jit(solution)/shard_map/ppermute | solution.py:194
  16.0 5.0 %near.2.near0_ref = f32[16,2048]{1,0:T(8,128)S(1)} custom-call(s32[8,16]{1,0:T(8,128)S(1)} %get-tuple-element.62.idx_ref, bf16[25,16,128]{2,1,0:T(8,128)(2,1)S(1)} %collective-permute-done.halo_ref, bf16[16,16,256]{2,1,0:T(8,128)(2,1)S(1)} %get-tuple-element.58.tiles_ref, bf16[16,2048,256]{2,1,0:T(8,128)(2,1)} %blocks_hbm.3), custom_call_target="tpu_custom_call" | custom-call | flops 134217728 | bytes 8700000 | tf_op jit(solution)/shard_map/near/pallas_call | solution.py:236
  21.0 0.0 collective-permute-done.3
  21.0 0.0 collective-permute-done.4
  21.0 0.0 collective-permute-done.5
  21.1 0.1 pad_maximum_fusion
  21.1 3.2 %collective-permute-start.8 = (bf16[144,16,128]{2,1,0:T(8,128)(2,1)S(1)}, bf16[144,16,128]{2,1,0:T(8,128)(2,1)S(1)}, u32[]{:S(2)}, u32[]{:S(2)}) collective-permute-start(bf16[144,16,128]{2,1,0:T(8,128)(2,1)S(1)} %pad_maximum_fusion), channel_id=1, source_target_pairs={{0,4},{4,0},{1,5},{5,1},{2,6},{6,2},{3,7},{7,3},{8,12},{12,8},{9,1... | collective-permute-start | bytes 1769480 | tf_op jit(solution)/shard_map/ppermute | solution.py:294
  24.3 0.1 fusion
  24.4 0.5 collective-permute-start.6
  24.9 2.3 %collective-permute-start.7 = (bf16[72,16,128]{2,1,0:T(8,128)(2,1)S(1)}, bf16[72,16,128]{2,1,0:T(8,128)(2,1)S(1)}, u32[]{:S(2)}, u32[]{:S(2)}) collective-permute-start(bf16[72,16,128]{2,1,0:T(8,128)(2,1)S(1)} %get-tuple-element.69), channel_id=1, source_target_pairs={{0,96},{1,97},{2,98},{3,99},{4,28},{5,29},{6,30},{7,31},{8,104},{9... | collective-permute-start | bytes 884744 | tf_op jit(solution)/shard_map/ppermute | solution.py:194
  27.1 0.1 pad_add_fusion.own_ref
  27.2 3.4 %collective-permute-start.11 = (bf16[16,16,128]{2,1,0:T(8,128)(2,1)S(1)}, bf16[16,16,128]{2,1,0:T(8,128)(2,1)S(1)}, u32[]{:S(2)}, u32[]{:S(2)}) collective-permute-start(bf16[16,16,128]{2,1,0:T(8,128)(2,1)S(1)} %get-tuple-element.63), channel_id=1, source_target_pairs={{1,2},{3,4},{5,6},{7,8},{9,10},{11,12},{13,14},{15,16},{17,18},{19... | collective-permute-start | bytes 196616 | tf_op jit(solution)/shard_map/ppermute | solution.py:287
  30.6 1.1 %collective-permute-start.10 = (bf16[72,16,128]{2,1,0:T(8,128)(2,1)S(1)}, bf16[72,16,128]{2,1,0:T(8,128)(2,1)S(1)}, u32[]{:S(2)}, u32[]{:S(2)}) collective-permute-start(bf16[72,16,128]{2,1,0:T(8,128)(2,1)S(1)} %get-tuple-element.70), channel_id=1, source_target_pairs={{0,96},{1,97},{2,98},{3,99},{4,28},{5,29},{6,30},{7,31},{8,104},{9... | collective-permute-start | bytes 884744 | tf_op jit(solution)/shard_map/ppermute | solution.py:194
  31.7 0.1 constant_dynamic-update-slice_fusion.10
  31.8 0.0 collective-permute-done.6
  31.8 0.5 collective-permute-start.9
  32.3 0.0 collective-permute-done.7
  32.3 0.0 collective-permute-done.8
  32.3 0.4 collective-permute-start.12
  32.8 2.3 %collective-permute-start.13 = (bf16[72,16,128]{2,1,0:T(8,128)(2,1)S(1)}, bf16[72,16,128]{2,1,0:T(8,128)(2,1)S(1)}, u32[]{:S(2)}, u32[]{:S(2)}) collective-permute-start(bf16[72,16,128]{2,1,0:T(8,128)(2,1)S(1)} %collective-permute-done.7), channel_id=1, source_target_pairs={{0,96},{1,97},{2,98},{3,99},{4,28},{5,29},{6,30},{7,31},{8,104},{9... | collective-permute-start | bytes 884744 | tf_op jit(solution)/shard_map/ppermute | solution.py:194
  35.1 0.0 collective-permute-done.11.halo_ref
  35.1 5.0 %near.3.near1_ref = f32[16,2048]{1,0:T(8,128)S(1)} custom-call(s32[8,16]{1,0:T(8,128)S(1)} %get-tuple-element.62.idx_ref, bf16[16,16,128]{2,1,0:T(8,128)(2,1)S(1)} %collective-permute-done.11.halo_ref, bf16[16,16,256]{2,1,0:T(8,128)(2,1)S(1)} %get-tuple-element.58.tiles_ref, bf16[16,2048,256]{2,1,0:T(8,128)(2,1)} %blocks_hbm.3), custom_call_target="tpu_custom_call" | custom-call | flops 134217728 | bytes 8700000 | tf_op jit(solution)/shard_map/near/pallas_call | solution.py:236
  40.2 0.1 pad_maximum_fusion.1
  40.2 0.0 copy-start
  40.2 0.0 copy-start.1
  40.3 0.0 copy-start.2
  40.3 0.0 copy-start.3
  40.3 0.0 copy-start.4
  40.3 0.0 copy-start.6
  40.3 0.0 copy-start.7
  40.3 0.0 copy-start.8
  40.3 0.0 copy-start.10
  40.3 0.0 collective-permute-done.10
  40.3 0.0 collective-permute-done.9
  40.4 1.9 %collective-permute-start.14 = (bf16[144,16,128]{2,1,0:T(8,128)(2,1)S(1)}, bf16[144,16,128]{2,1,0:T(8,128)(2,1)S(1)}, u32[]{:S(2)}, u32[]{:S(2)}) collective-permute-start(bf16[144,16,128]{2,1,0:T(8,128)(2,1)S(1)} %pad_maximum_fusion.1), channel_id=1, source_target_pairs={{0,4},{4,0},{1,5},{5,1},{2,6},{6,2},{3,7},{7,3},{8,12},{12,8},{9,1... | collective-permute-start | bytes 1769480 | tf_op jit(solution)/shard_map/ppermute | solution.py:304
  42.3 0.1 pad_maximum_fusion.2
  42.4 0.1 collective-permute-start.15
  42.5 0.0 collective-permute-done.12
  42.6 0.0 collective-permute-done.13
  42.6 0.1 pad_maximum_fusion.3
  42.6 2.1 %collective-permute-start.16 = (bf16[144,16,128]{2,1,0:T(8,128)(2,1)S(1)}, bf16[144,16,128]{2,1,0:T(8,128)(2,1)S(1)}, u32[]{:S(2)}, u32[]{:S(2)}) collective-permute-start(bf16[144,16,128]{2,1,0:T(8,128)(2,1)S(1)} %pad_maximum_fusion.3), channel_id=1, source_target_pairs={{0,4},{4,0},{1,5},{5,1},{2,6},{6,2},{3,7},{7,3},{8,12},{12,8},{9,1... | collective-permute-start | bytes 1769480 | tf_op jit(solution)/shard_map/ppermute | solution.py:304
  44.9 0.1 constant_dynamic-update-slice_fusion.3
  45.0 0.0 collective-permute-done.14
  45.0 0.1 constant_dynamic-update-slice_fusion.2
  45.2 0.0 collective-permute-done.15
  45.2 0.1 constant_dynamic-update-slice_fusion.1
  45.3 1.1 %collective-permute-done.16 = bf16[144,16,128]{2,1,0:T(8,128)(2,1)S(1)} collective-permute-done((bf16[144,16,128]{2,1,0:T(8,128)(2,1)S(1)}, bf16[144,16,128]{2,1,0:T(8,128)(2,1)S(1)}, u32[]{:S(2)}, u32[]{:S(2)}) %collective-permute-start.16) | collective-permute-done | bytes 589856 | tf_op jit(solution)/shard_map/ppermute | solution.py:304
  46.4 0.1 constant_dynamic-update-slice_fusion.table
  46.5 0.0 copy-done
  46.5 0.0 copy-done.1
  46.6 0.0 copy-done.2
  46.6 4.3 %downward.1 = bf16[16,4096]{1,0:T(8,128)(2,1)} custom-call(s32[16,32]{1,0:T(8,128)S(1)} %copy-done.7, s32[2,32]{1,0:T(2,128)S(1)} %copy-done.10, s32[6,16]{1,0:T(8,128)S(1)} %copy-done.8, s32[2]{0:T(128)S(1)} %pad_add_fusion.own_ref, bf16[1152,16,128]{2,1,0:T(8,128)(2,1)S(1)} %constant_dynamic-update-slice_fusion.table, bf16[16,64,2048]{2,1,0:T(8,128)(2,1)S(1)} %copy-done, ...), custom_call_target="tpu_custom_call" | custom-call | tf_op jit(solution)/shard_map/downward/pallas_call | solution.py:307
  (18 shorter events, 0.3 us)
Async XLA Ops:
  1.7 8.9 %collective-permute-start = (bf16[25,16,128]{2,1,0:T(8,128)(2,1)S(1)}, bf16[25,16,128]{2,1,0:T(8,128)(2,1)S(1)}, u32[]{:S(2)}, u32[]{:S(2)}) collective-permute-start(bf16[25,16,128]{2,1,0:T(8,128)(2,1)S(1)} %get-tuple-element.49), channel_id=1, source_target_pairs={{0,1},{1,0},{2,3},{3,2},{4,5},{5,4},{6,7},{7,6},{8,9},{9,8},{10,11... | collective-permute-start | bytes 307208 | tf_op jit(solution)/shard_map/ppermute | solution.py:261
  4.2 6.3 %collective-permute-start.1 = (bf16[9,16,128]{2,1,0:T(8,128)(2,1)S(1)}, bf16[9,16,128]{2,1,0:T(8,128)(2,1)S(1)}, u32[]{:S(2)}, u32[]{:S(2)}) collective-permute-start(bf16[9,16,128]{2,1,0:T(8,128)(2,1)S(1)} %slice.12), channel_id=1, source_target_pairs={{0,3},{1,2},{2,1},{3,0},{4,7},{5,6},{6,5},{7,4},{8,11},{9,10},{10,... | collective-permute-start | bytes 110600 | tf_op jit(solution)/shard_map/ppermute | solution.py:263
  6.5 4.6 %collective-permute-start.2 = (bf16[9,16,128]{2,1,0:T(8,128)(2,1)S(1)}, bf16[9,16,128]{2,1,0:T(8,128)(2,1)S(1)}, u32[]{:S(2)}, u32[]{:S(2)}) collective-permute-start(bf16[9,16,128]{2,1,0:T(8,128)(2,1)S(1)} %slice.12), channel_id=1, source_target_pairs={{0,2},{1,3},{2,0},{3,1},{4,6},{5,7},{6,4},{7,5},{8,10},{9,11},{10,... | collective-permute-start | bytes 110600 | tf_op jit(solution)/shard_map/ppermute | solution.py:263
  9.0 0.9 %copy-start.5 = (bf16[16,4096]{1,0:T(8,128)(2,1)S(1)}, bf16[16,4096]{1,0:T(8,128)(2,1)}, u32[]{:S(2)}) copy-start(bf16[16,4096]{1,0:T(8,128)(2,1)} %dens_ref) | copy-start | bytes 393220
  9.9 0.7 %copy-start.9 = (s32[8,16]{1,0:T(8,128)S(1)}, s32[8,16]{1,0:T(8,128)}, u32[]{:S(2)}) copy-start(s32[8,16]{1,0:T(8,128)} %get-tuple-element.51.code_ref) | copy-start | bytes 1540
  11.1 9.9 %collective-permute-start.3 = (bf16[36,16,128]{2,1,0:T(8,128)(2,1)S(1)}, bf16[36,16,128]{2,1,0:T(8,128)(2,1)S(1)}, u32[]{:S(2)}, u32[]{:S(2)}) collective-permute-start(bf16[36,16,128]{2,1,0:T(8,128)(2,1)S(1)} %pad_maximum_fusion.4), channel_id=1, source_target_pairs={{0,8},{1,9},{2,10},{3,11},{4,36},{5,37},{6,38},{7,39},{8,16},{9,17... | collective-permute-start | bytes 442376 | tf_op jit(solution)/shard_map/ppermute | solution.py:194
  12.4 8.6 %collective-permute-start.4 = (bf16[36,16,128]{2,1,0:T(8,128)(2,1)S(1)}, bf16[36,16,128]{2,1,0:T(8,128)(2,1)S(1)}, u32[]{:S(2)}, u32[]{:S(2)}) collective-permute-start(bf16[36,16,128]{2,1,0:T(8,128)(2,1)S(1)} %pad_maximum_fusion.4), channel_id=1, source_target_pairs={{0,16},{1,17},{2,18},{3,19},{4,68},{5,69},{6,70},{7,71},{8,24},{9,... | collective-permute-start | bytes 442376 | tf_op jit(solution)/shard_map/ppermute | solution.py:194
  14.9 6.2 %collective-permute-start.5 = (bf16[36,16,128]{2,1,0:T(8,128)(2,1)S(1)}, bf16[36,16,128]{2,1,0:T(8,128)(2,1)S(1)}, u32[]{:S(2)}, u32[]{:S(2)}) collective-permute-start(bf16[36,16,128]{2,1,0:T(8,128)(2,1)S(1)} %pad_maximum_fusion.4), channel_id=1, source_target_pairs={{0,24},{1,25},{2,26},{3,27},{4,100},{5,101},{6,102},{7,103},{8,0},... | collective-permute-start | bytes 442376 | tf_op jit(solution)/shard_map/ppermute | solution.py:194
  21.1 11.2 %collective-permute-start.8 = (bf16[144,16,128]{2,1,0:T(8,128)(2,1)S(1)}, bf16[144,16,128]{2,1,0:T(8,128)(2,1)S(1)}, u32[]{:S(2)}, u32[]{:S(2)}) collective-permute-start(bf16[144,16,128]{2,1,0:T(8,128)(2,1)S(1)} %pad_maximum_fusion), channel_id=1, source_target_pairs={{0,4},{4,0},{1,5},{5,1},{2,6},{6,2},{3,7},{7,3},{8,12},{12,8},{9,1... | collective-permute-start | bytes 1769480 | tf_op jit(solution)/shard_map/ppermute | solution.py:294
  24.4 7.4 %collective-permute-start.6 = (bf16[72,16,128]{2,1,0:T(8,128)(2,1)S(1)}, bf16[72,16,128]{2,1,0:T(8,128)(2,1)S(1)}, u32[]{:S(2)}, u32[]{:S(2)}) collective-permute-start(bf16[72,16,128]{2,1,0:T(8,128)(2,1)S(1)} %get-tuple-element.70), channel_id=1, source_target_pairs={{0,32},{1,33},{2,34},{3,35},{4,12},{5,13},{6,14},{7,15},{8,40},{9,... | collective-permute-start | bytes 884744 | tf_op jit(solution)/shard_map/ppermute | solution.py:194
  24.9 7.5 %collective-permute-start.7 = (bf16[72,16,128]{2,1,0:T(8,128)(2,1)S(1)}, bf16[72,16,128]{2,1,0:T(8,128)(2,1)S(1)}, u32[]{:S(2)}, u32[]{:S(2)}) collective-permute-start(bf16[72,16,128]{2,1,0:T(8,128)(2,1)S(1)} %get-tuple-element.69), channel_id=1, source_target_pairs={{0,96},{1,97},{2,98},{3,99},{4,28},{5,29},{6,30},{7,31},{8,104},{9... | collective-permute-start | bytes 884744 | tf_op jit(solution)/shard_map/ppermute | solution.py:194
  27.2 7.9 %collective-permute-start.11 = (bf16[16,16,128]{2,1,0:T(8,128)(2,1)S(1)}, bf16[16,16,128]{2,1,0:T(8,128)(2,1)S(1)}, u32[]{:S(2)}, u32[]{:S(2)}) collective-permute-start(bf16[16,16,128]{2,1,0:T(8,128)(2,1)S(1)} %get-tuple-element.63), channel_id=1, source_target_pairs={{1,2},{3,4},{5,6},{7,8},{9,10},{11,12},{13,14},{15,16},{17,18},{19... | collective-permute-start | bytes 196616 | tf_op jit(solution)/shard_map/ppermute | solution.py:287
  30.6 9.7 %collective-permute-start.10 = (bf16[72,16,128]{2,1,0:T(8,128)(2,1)S(1)}, bf16[72,16,128]{2,1,0:T(8,128)(2,1)S(1)}, u32[]{:S(2)}, u32[]{:S(2)}) collective-permute-start(bf16[72,16,128]{2,1,0:T(8,128)(2,1)S(1)} %get-tuple-element.70), channel_id=1, source_target_pairs={{0,96},{1,97},{2,98},{3,99},{4,28},{5,29},{6,30},{7,31},{8,104},{9... | collective-permute-start | bytes 884744 | tf_op jit(solution)/shard_map/ppermute | solution.py:194
  31.8 8.5 %collective-permute-start.9 = (bf16[72,16,128]{2,1,0:T(8,128)(2,1)S(1)}, bf16[72,16,128]{2,1,0:T(8,128)(2,1)S(1)}, u32[]{:S(2)}, u32[]{:S(2)}) collective-permute-start(bf16[72,16,128]{2,1,0:T(8,128)(2,1)S(1)} %get-tuple-element.69), channel_id=1, source_target_pairs={{0,32},{1,33},{2,34},{3,35},{4,12},{5,13},{6,14},{7,15},{8,40},{9,... | collective-permute-start | bytes 884744 | tf_op jit(solution)/shard_map/ppermute | solution.py:194
  32.3 10.2 %collective-permute-start.12 = (bf16[72,16,128]{2,1,0:T(8,128)(2,1)S(1)}, bf16[72,16,128]{2,1,0:T(8,128)(2,1)S(1)}, u32[]{:S(2)}, u32[]{:S(2)}) collective-permute-start(bf16[72,16,128]{2,1,0:T(8,128)(2,1)S(1)} %collective-permute-done.6), channel_id=1, source_target_pairs={{0,32},{1,33},{2,34},{3,35},{4,12},{5,13},{6,14},{7,15},{8,40},{9,... | collective-permute-start | bytes 884744 | tf_op jit(solution)/shard_map/ppermute | solution.py:194
  32.8 9.8 %collective-permute-start.13 = (bf16[72,16,128]{2,1,0:T(8,128)(2,1)S(1)}, bf16[72,16,128]{2,1,0:T(8,128)(2,1)S(1)}, u32[]{:S(2)}, u32[]{:S(2)}) collective-permute-start(bf16[72,16,128]{2,1,0:T(8,128)(2,1)S(1)} %collective-permute-done.7), channel_id=1, source_target_pairs={{0,96},{1,97},{2,98},{3,99},{4,28},{5,29},{6,30},{7,31},{8,104},{9... | collective-permute-start | bytes 884744 | tf_op jit(solution)/shard_map/ppermute | solution.py:194
  40.2 6.3 %copy-start = (bf16[16,64,2048]{2,1,0:T(8,128)(2,1)S(1)}, bf16[16,64,2048]{2,1,0:T(8,128)(2,1)}, u32[]{:S(2)}) copy-start(bf16[16,64,2048]{2,1,0:T(8,128)(2,1)} %lc.1) | copy-start | bytes 12582916
  40.2 6.3 %copy-start.1 = (bf16[16,64,256]{2,1,0:T(8,128)(2,1)S(1)}, bf16[16,64,256]{2,1,0:T(8,128)(2,1)}, u32[]{:S(2)}) copy-start(bf16[16,64,256]{2,1,0:T(8,128)(2,1)} %basis_ref.1) | copy-start | bytes 1572868
  40.3 6.3 %copy-start.2 = (bf16[32,64,512]{2,1,0:T(8,128)(2,1)S(1)}, bf16[32,64,512]{2,1,0:T(8,128)(2,1)}, u32[]{:S(2)}) copy-start(bf16[32,64,512]{2,1,0:T(8,128)(2,1)} %gt.1) | copy-start | bytes 6291460
  40.3 6.3 %copy-start.3 = (bf16[2,64,512]{2,1,0:T(8,128)(2,1)S(1)}, bf16[2,64,512]{2,1,0:T(8,128)(2,1)}, u32[]{:S(2)}) copy-start(bf16[2,64,512]{2,1,0:T(8,128)(2,1)} %pt_ref.1) | copy-start | bytes 393220
  40.3 6.3 %copy-start.4 = (bf16[2,64,2048]{2,1,0:T(8,128)(2,1)S(1)}, bf16[2,64,2048]{2,1,0:T(8,128)(2,1)}, u32[]{:S(2)}) copy-start(bf16[2,64,2048]{2,1,0:T(8,128)(2,1)} %pc.1) | copy-start | bytes 1572868
  40.3 6.3 %copy-start.6 = (bf16[1,64,1024]{2,1,0:T(8,128)(2,1)S(1)}, bf16[1,64,1024]{2,1,0:T(8,128)(2,1)}, u32[]{:S(2)}) copy-start(bf16[1,64,1024]{2,1,0:T(8,128)(2,1)} %gc.1) | copy-start | bytes 393220
  40.3 6.3 %copy-start.7 = (s32[16,32]{1,0:T(8,128)S(1)}, s32[16,32]{1,0:T(8,128)}, u32[]{:S(2)}) copy-start(s32[16,32]{1,0:T(8,128)} %get-tuple-element.46.leaf_ref) | copy-start | bytes 6148
  40.3 6.3 %copy-start.8 = (s32[6,16]{1,0:T(8,128)S(1)}, s32[6,16]{1,0:T(8,128)}, u32[]{:S(2)}) copy-start(s32[6,16]{1,0:T(8,128)} %get-tuple-element.48.grand_ref) | copy-start | bytes 1156
  40.3 6.3 %copy-start.10 = (s32[2,32]{1,0:T(2,128)S(1)}, s32[2,32]{1,0:T(2,128)}, u32[]{:S(2)}) copy-start(s32[2,32]{1,0:T(2,128)} %get-tuple-element.47.parent_ref) | copy-start | bytes 772
  40.4 4.6 %collective-permute-start.14 = (bf16[144,16,128]{2,1,0:T(8,128)(2,1)S(1)}, bf16[144,16,128]{2,1,0:T(8,128)(2,1)S(1)}, u32[]{:S(2)}, u32[]{:S(2)}) collective-permute-start(bf16[144,16,128]{2,1,0:T(8,128)(2,1)S(1)} %pad_maximum_fusion.1), channel_id=1, source_target_pairs={{0,4},{4,0},{1,5},{5,1},{2,6},{6,2},{3,7},{7,3},{8,12},{12,8},{9,1... | collective-permute-start | bytes 1769480 | tf_op jit(solution)/shard_map/ppermute | solution.py:304
  42.4 2.8 %collective-permute-start.15 = (bf16[144,16,128]{2,1,0:T(8,128)(2,1)S(1)}, bf16[144,16,128]{2,1,0:T(8,128)(2,1)S(1)}, u32[]{:S(2)}, u32[]{:S(2)}) collective-permute-start(bf16[144,16,128]{2,1,0:T(8,128)(2,1)S(1)} %pad_maximum_fusion.2), channel_id=1, source_target_pairs={{0,4},{4,0},{1,5},{5,1},{2,6},{6,2},{3,7},{7,3},{8,12},{12,8},{9,1... | collective-permute-start | bytes 1769480 | tf_op jit(solution)/shard_map/ppermute | solution.py:304
  42.6 3.8 %collective-permute-start.16 = (bf16[144,16,128]{2,1,0:T(8,128)(2,1)S(1)}, bf16[144,16,128]{2,1,0:T(8,128)(2,1)S(1)}, u32[]{:S(2)}, u32[]{:S(2)}) collective-permute-start(bf16[144,16,128]{2,1,0:T(8,128)(2,1)S(1)} %pad_maximum_fusion.3), channel_id=1, source_target_pairs={{0,4},{4,0},{1,5},{5,1},{2,6},{6,2},{3,7},{7,3},{8,12},{12,8},{9,1... | collective-permute-start | bytes 1769480 | tf_op jit(solution)/shard_map/ppermute | solution.py:304

commit v6 on v5

--- a/solution.py
+++ b/solution.py
@@ -258,9 +258,10 @@
              grand_source, grand_valid),
         )
     )
+    mine = coefs[:TILES]
+    opposite = lax.ppermute(mine, "z", [(i, i ^ 2) for i in range(4)])
     inner = lax.ppermute(coefs, "z", [(i, i ^ 1) for i in range(4)])
-    mine = coefs[:TILES]
-    steps = [lax.ppermute(mine, "z", [(i, i ^ k) for i in range(4)]) for k in (3, 2)]
+    steps = [lax.ppermute(mine, "z", [(i, i ^ 3) for i in range(4)]), opposite]
     near_code, leaf_code, parent_code, grand_code = pl.pallas_call(
         code_kernel,
         out_shape=[
@@ -288,7 +289,8 @@
         outer, AXES, [(i, i + 1) for i in range(1, 127, 2)] + [(i + 1, i) for i in range(1, 127, 2)]
     )
 
-    steps = [shift_plane(coefs, k, 0) for k in (1, 2, 3)]
+    opposite = shift_plane(coefs, 2, 0)
+    steps = [shift_plane(coefs, 1, 0), opposite, shift_plane(coefs, 3, 0)]
     near0 = near_half(0, TILES, inner, near_code)
     coefs, near0 = barrier((jnp.concatenate([coefs] + steps, axis=0), near0))
     own_swap = lax.ppermute(coefs, "c", swap)

time: 51.2 us -> 51.2 us (level)
  no operation moved by 1% of the time
where the time goes in v6:
time: 51.2 us; the launch traced here: 50.9 us
  starting transfers between devices  28.5 us (56%)
  Pallas kernels  17.4 us (34%)
  local copies, waits for them, and re-layouts  2.65 us (5%)
  waiting for transfers between devices  1.64 us (3%)
    ppermute x9, starting transfers between devices, shift_plane(): lax.ppermute(v, AXES, pairs_of(lambda x, y, c, z: (x, (y + k) % 4, c, z)...  12 us
    pallas_call x2, Pallas kernels, near_half(): pl.pallas_call(functools.partial(near_kernel, turn, skip), out_shape=jax....  9.99 us
    pallas_call x1, Pallas kernels, body(): pl.pallas_call(down_kernel, out_shape=jax.ShapeDtypeStruct((16, 4096), BF...  4.32 us
    ppermute x3, starting transfers between devices, body(): lax.ppermute(jnp.concatenate(p, axis=0), 'c', swap)  4.17 us
    ppermute x1, starting transfers between devices, body(): lax.ppermute(outer, AXES, [(i, i + 1) for i in range(1, 127, 2)] + [(i +...  3.36 us
    ppermute x1, starting transfers between devices, body(): own_swap = lax.ppermute(coefs, 'c', swap)  3.16 us
    ppermute x1, starting transfers between devices, body(): inner = lax.ppermute(coefs, 'z', [(i, i ^ 1) for i in range(4)])  2.55 us
    unnamed x32, local copies, waits for them, and re-layouts  2.4 us
  transfers between devices with their start and end apart: 17, of which 2 were waited for; matrix products, arithmetic and copies ran while one was open for 2% of the time, Pallas kernels for 22%

profile of v6, /device:TPU:1, one launch (start us, length us, event | category | flops | bytes accessed | tf_op | source)
XLA Modules:
  0.0 50.9 jit_solution(10233646218240260271)
XLA Ops:
  0.0 1.7 %upward.1 = (bf16[25,16,128]{2,1,0:T(8,128)(2,1)S(1)}, bf16[16,16,128]{2,1,0:T(8,128)(2,1)S(1)}) custom-call(bf16[16,4096]{1,0:T(8,128)(2,1)} %dens_ref, bf16[16,64,256]{2,1,0:T(8,128)(2,1)} %basis_ref.1, bf16[2,64,512]{2,1,0:T(8,128)(2,1)} %pt_ref.1), custom_call_target="tpu_custom_call" | custom-call | tf_op jit(solution)/shard_map/upward/pallas_call | solution.py:214
  1.7 2.5 %collective-permute-start = (bf16[25,16,128]{2,1,0:T(8,128)(2,1)S(1)}, bf16[25,16,128]{2,1,0:T(8,128)(2,1)S(1)}, u32[]{:S(2)}, u32[]{:S(2)}) collective-permute-start(bf16[25,16,128]{2,1,0:T(8,128)(2,1)S(1)} %get-tuple-element.49), channel_id=1, source_target_pairs={{0,1},{1,0},{2,3},{3,2},{4,5},{5,4},{6,7},{7,6},{8,9},{9,8},{10,11... | collective-permute-start | bytes 307208 | tf_op jit(solution)/shard_map/ppermute | solution.py:263
  4.2 2.2 %collective-permute-start.1 = (bf16[9,16,128]{2,1,0:T(8,128)(2,1)S(1)}, bf16[9,16,128]{2,1,0:T(8,128)(2,1)S(1)}, u32[]{:S(2)}, u32[]{:S(2)}) collective-permute-start(bf16[9,16,128]{2,1,0:T(8,128)(2,1)S(1)} %slice.12), channel_id=1, source_target_pairs={{0,3},{1,2},{2,1},{3,0},{4,7},{5,6},{6,5},{7,4},{8,11},{9,10},{10,... | collective-permute-start | bytes 110600 | tf_op jit(solution)/shard_map/ppermute | solution.py:264
  6.5 1.1 %collective-permute-start.2 = (bf16[9,16,128]{2,1,0:T(8,128)(2,1)S(1)}, bf16[9,16,128]{2,1,0:T(8,128)(2,1)S(1)}, u32[]{:S(2)}, u32[]{:S(2)}) collective-permute-start(bf16[9,16,128]{2,1,0:T(8,128)(2,1)S(1)} %slice.12), channel_id=1, source_target_pairs={{0,2},{1,3},{2,0},{3,1},{4,6},{5,7},{6,4},{7,5},{8,10},{9,11},{10,... | collective-permute-start | bytes 110600 | tf_op jit(solution)/shard_map/ppermute | solution.py:262
  7.5 1.4 %codes.1 = (s32[8,16]{1,0:T(8,128)}, s32[16,32]{1,0:T(8,128)}, s32[2,32]{1,0:T(2,128)}, s32[6,16]{1,0:T(8,128)}) custom-call(s32[8,16]{1,0:T(8,128)} %bitcast.4, s32[8,16]{1,0:T(8,128)} %bitcast.5, s32[16,32]{1,0:T(8,128)} %ls_ref, s32[16,32]{1,0:T(8,128)} %lv_ref, s32[2,32]{1,0:T(2,128)} %ps_ref, s32[2,32]{1,0:T(2,128)} %pv_ref, s32[1,16]{1,0:T(1,128)} %gs_ref, ...), custom_call_target="tpu_custom_call" | custom-call | tf_op jit(solution)/shard_map/codes/pallas_call | solution.py:265
  9.0 0.9 %copy-done.5 = bf16[16,4096]{1,0:T(8,128)(2,1)S(1)} copy-done((bf16[16,4096]{1,0:T(8,128)(2,1)S(1)}, bf16[16,4096]{1,0:T(8,128)(2,1)}, u32[]{:S(2)}) %copy-start.5) | copy-done | bytes 131096
  9.9 0.7 %copy-done.9 = s32[8,16]{1,0:T(8,128)S(1)} copy-done((s32[8,16]{1,0:T(8,128)S(1)}, s32[8,16]{1,0:T(8,128)}, u32[]{:S(2)}) %copy-start.9) | copy-done | bytes 536
  10.5 0.0 collective-permute-done.halo_ref
  10.6 0.0 collective-permute-done.1
  10.6 0.5 %collective-permute-done.2 = bf16[9,16,128]{2,1,0:T(8,128)(2,1)S(1)} collective-permute-done((bf16[9,16,128]{2,1,0:T(8,128)(2,1)S(1)}, bf16[9,16,128]{2,1,0:T(8,128)(2,1)S(1)}, u32[]{:S(2)}, u32[]{:S(2)}) %collective-permute-start.2) | collective-permute-done | bytes 36896 | tf_op jit(solution)/shard_map/ppermute | solution.py:262
  11.1 1.3 %collective-permute-start.3 = (bf16[36,16,128]{2,1,0:T(8,128)(2,1)S(1)}, bf16[36,16,128]{2,1,0:T(8,128)(2,1)S(1)}, u32[]{:S(2)}, u32[]{:S(2)}) collective-permute-start(bf16[36,16,128]{2,1,0:T(8,128)(2,1)S(1)} %pad_maximum_fusion.4), channel_id=1, source_target_pairs={{0,8},{1,9},{2,10},{3,11},{4,36},{5,37},{6,38},{7,39},{8,16},{9,17... | collective-permute-start | bytes 442376 | tf_op jit(solution)/shard_map/ppermute | solution.py:194
  12.4 2.5 %collective-permute-start.4 = (bf16[36,16,128]{2,1,0:T(8,128)(2,1)S(1)}, bf16[36,16,128]{2,1,0:T(8,128)(2,1)S(1)}, u32[]{:S(2)}, u32[]{:S(2)}) collective-permute-start(bf16[36,16,128]{2,1,0:T(8,128)(2,1)S(1)} %pad_maximum_fusion.4), channel_id=1, source_target_pairs={{0,16},{1,17},{2,18},{3,19},{4,68},{5,69},{6,70},{7,71},{8,24},{9,... | collective-permute-start | bytes 442376 | tf_op jit(solution)/shard_map/ppermute | solution.py:194
  14.9 1.2 %collective-permute-start.5 = (bf16[36,16,128]{2,1,0:T(8,128)(2,1)S(1)}, bf16[36,16,128]{2,1,0:T(8,128)(2,1)S(1)}, u32[]{:S(2)}, u32[]{:S(2)}) collective-permute-start(bf16[36,16,128]{2,1,0:T(8,128)(2,1)S(1)} %pad_maximum_fusion.4), channel_id=1, source_target_pairs={{0,24},{1,25},{2,26},{3,27},{4,100},{5,101},{6,102},{7,103},{8,0},... | collective-permute-start | bytes 442376 | tf_op jit(solution)/shard_map/ppermute | solution.py:194
  16.0 5.0 %near.2.near0_ref = f32[16,2048]{1,0:T(8,128)S(1)} custom-call(s32[8,16]{1,0:T(8,128)S(1)} %get-tuple-element.62.idx_ref, bf16[25,16,128]{2,1,0:T(8,128)(2,1)S(1)} %collective-permute-done.halo_ref, bf16[16,16,256]{2,1,0:T(8,128)(2,1)S(1)} %get-tuple-element.58.tiles_ref, bf16[16,2048,256]{2,1,0:T(8,128)(2,1)} %blocks_hbm.3), custom_call_target="tpu_custom_call" | custom-call | flops 134217728 | bytes 8700000 | tf_op jit(solution)/shard_map/near/pallas_call | solution.py:236
  21.0 0.0 collective-permute-done.3
  21.0 0.0 collective-permute-done.4
  21.0 0.0 collective-permute-done.5
  21.1 0.1 pad_maximum_fusion
  21.1 3.2 %collective-permute-start.8 = (bf16[144,16,128]{2,1,0:T(8,128)(2,1)S(1)}, bf16[144,16,128]{2,1,0:T(8,128)(2,1)S(1)}, u32[]{:S(2)}, u32[]{:S(2)}) collective-permute-start(bf16[144,16,128]{2,1,0:T(8,128)(2,1)S(1)} %pad_maximum_fusion), channel_id=1, source_target_pairs={{0,4},{4,0},{1,5},{5,1},{2,6},{6,2},{3,7},{7,3},{8,12},{12,8},{9,1... | collective-permute-start | bytes 1769480 | tf_op jit(solution)/shard_map/ppermute | solution.py:296
  24.3 0.1 fusion
  24.4 0.5 collective-permute-start.6
  24.9 2.3 %collective-permute-start.7 = (bf16[72,16,128]{2,1,0:T(8,128)(2,1)S(1)}, bf16[72,16,128]{2,1,0:T(8,128)(2,1)S(1)}, u32[]{:S(2)}, u32[]{:S(2)}) collective-permute-start(bf16[72,16,128]{2,1,0:T(8,128)(2,1)S(1)} %get-tuple-element.69), channel_id=1, source_target_pairs={{0,96},{1,97},{2,98},{3,99},{4,28},{5,29},{6,30},{7,31},{8,104},{9... | collective-permute-start | bytes 884744 | tf_op jit(solution)/shard_map/ppermute | solution.py:194
  27.2 0.1 pad_add_fusion.own_ref
  27.2 3.4 %collective-permute-start.11 = (bf16[16,16,128]{2,1,0:T(8,128)(2,1)S(1)}, bf16[16,16,128]{2,1,0:T(8,128)(2,1)S(1)}, u32[]{:S(2)}, u32[]{:S(2)}) collective-permute-start(bf16[16,16,128]{2,1,0:T(8,128)(2,1)S(1)} %get-tuple-element.63), channel_id=1, source_target_pairs={{1,2},{3,4},{5,6},{7,8},{9,10},{11,12},{13,14},{15,16},{17,18},{19... | collective-permute-start | bytes 196616 | tf_op jit(solution)/shard_map/ppermute | solution.py:288
  30.6 1.1 %collective-permute-start.10 = (bf16[72,16,128]{2,1,0:T(8,128)(2,1)S(1)}, bf16[72,16,128]{2,1,0:T(8,128)(2,1)S(1)}, u32[]{:S(2)}, u32[]{:S(2)}) collective-permute-start(bf16[72,16,128]{2,1,0:T(8,128)(2,1)S(1)} %get-tuple-element.70), channel_id=1, source_target_pairs={{0,96},{1,97},{2,98},{3,99},{4,28},{5,29},{6,30},{7,31},{8,104},{9... | collective-permute-start | bytes 884744 | tf_op jit(solution)/shard_map/ppermute | solution.py:194
  31.7 0.1 constant_dynamic-update-slice_fusion.10
  31.8 0.0 collective-permute-done.6
  31.8 0.5 collective-permute-start.9
  32.3 0.0 collective-permute-done.7
  32.3 0.0 collective-permute-done.8
  32.3 0.4 collective-permute-start.12
  32.8 2.3 %collective-permute-start.13 = (bf16[72,16,128]{2,1,0:T(8,128)(2,1)S(1)}, bf16[72,16,128]{2,1,0:T(8,128)(2,1)S(1)}, u32[]{:S(2)}, u32[]{:S(2)}) collective-permute-start(bf16[72,16,128]{2,1,0:T(8,128)(2,1)S(1)} %collective-permute-done.7), channel_id=1, source_target_pairs={{0,96},{1,97},{2,98},{3,99},{4,28},{5,29},{6,30},{7,31},{8,104},{9... | collective-permute-start | bytes 884744 | tf_op jit(solution)/shard_map/ppermute | solution.py:194
  35.1 0.0 collective-permute-done.11.halo_ref
  35.1 5.0 %near.3.near1_ref = f32[16,2048]{1,0:T(8,128)S(1)} custom-call(s32[8,16]{1,0:T(8,128)S(1)} %get-tuple-element.62.idx_ref, bf16[16,16,128]{2,1,0:T(8,128)(2,1)S(1)} %collective-permute-done.11.halo_ref, bf16[16,16,256]{2,1,0:T(8,128)(2,1)S(1)} %get-tuple-element.58.tiles_ref, bf16[16,2048,256]{2,1,0:T(8,128)(2,1)} %blocks_hbm.3), custom_call_target="tpu_custom_call" | custom-call | flops 134217728 | bytes 8700000 | tf_op jit(solution)/shard_map/near/pallas_call | solution.py:236
  40.2 0.1 pad_maximum_fusion.1
  40.2 0.0 copy-start
  40.2 0.0 copy-start.1
  40.3 0.0 copy-start.2
  40.3 0.0 copy-start.3
  40.3 0.0 copy-start.4
  40.3 0.0 copy-start.6
  40.3 0.0 copy-start.7
  40.3 0.0 copy-start.8
  40.3 0.0 copy-start.10
  40.3 0.0 collective-permute-done.10
  40.3 0.0 collective-permute-done.9
  40.4 1.9 %collective-permute-start.14 = (bf16[144,16,128]{2,1,0:T(8,128)(2,1)S(1)}, bf16[144,16,128]{2,1,0:T(8,128)(2,1)S(1)}, u32[]{:S(2)}, u32[]{:S(2)}) collective-permute-start(bf16[144,16,128]{2,1,0:T(8,128)(2,1)S(1)} %pad_maximum_fusion.1), channel_id=1, source_target_pairs={{0,4},{4,0},{1,5},{5,1},{2,6},{6,2},{3,7},{7,3},{8,12},{12,8},{9,1... | collective-permute-start | bytes 1769480 | tf_op jit(solution)/shard_map/ppermute | solution.py:306
  42.3 0.1 pad_maximum_fusion.2
  42.4 0.1 collective-permute-start.15
  42.5 0.0 collective-permute-done.12
  42.6 0.0 collective-permute-done.13
  42.6 0.1 pad_maximum_fusion.3
  42.6 2.1 %collective-permute-start.16 = (bf16[144,16,128]{2,1,0:T(8,128)(2,1)S(1)}, bf16[144,16,128]{2,1,0:T(8,128)(2,1)S(1)}, u32[]{:S(2)}, u32[]{:S(2)}) collective-permute-start(bf16[144,16,128]{2,1,0:T(8,128)(2,1)S(1)} %pad_maximum_fusion.3), channel_id=1, source_target_pairs={{0,4},{4,0},{1,5},{5,1},{2,6},{6,2},{3,7},{7,3},{8,12},{12,8},{9,1... | collective-permute-start | bytes 1769480 | tf_op jit(solution)/shard_map/ppermute | solution.py:306
  44.9 0.1 constant_dynamic-update-slice_fusion.3
  45.0 0.0 collective-permute-done.14
  45.0 0.1 constant_dynamic-update-slice_fusion.2
  45.2 0.0 collective-permute-done.15
  45.2 0.1 constant_dynamic-update-slice_fusion.1
  45.3 1.1 %collective-permute-done.16 = bf16[144,16,128]{2,1,0:T(8,128)(2,1)S(1)} collective-permute-done((bf16[144,16,128]{2,1,0:T(8,128)(2,1)S(1)}, bf16[144,16,128]{2,1,0:T(8,128)(2,1)S(1)}, u32[]{:S(2)}, u32[]{:S(2)}) %collective-permute-start.16) | collective-permute-done | bytes 589856 | tf_op jit(solution)/shard_map/ppermute | solution.py:306
  46.4 0.1 constant_dynamic-update-slice_fusion.table
  46.5 0.0 copy-done
  46.5 0.0 copy-done.1
  46.6 0.0 copy-done.2
  46.6 4.3 %downward.1 = bf16[16,4096]{1,0:T(8,128)(2,1)} custom-call(s32[16,32]{1,0:T(8,128)S(1)} %copy-done.7, s32[2,32]{1,0:T(2,128)S(1)} %copy-done.10, s32[6,16]{1,0:T(8,128)S(1)} %copy-done.8, s32[2]{0:T(128)S(1)} %pad_add_fusion.own_ref, bf16[1152,16,128]{2,1,0:T(8,128)(2,1)S(1)} %constant_dynamic-update-slice_fusion.table, bf16[16,64,2048]{2,1,0:T(8,128)(2,1)S(1)} %copy-done, ...), custom_call_target="tpu_custom_call" | custom-call | tf_op jit(solution)/shard_map/downward/pallas_call | solution.py:309
  (18 shorter events, 0.3 us)
Async XLA Ops:
  1.7 8.9 %collective-permute-start = (bf16[25,16,128]{2,1,0:T(8,128)(2,1)S(1)}, bf16[25,16,128]{2,1,0:T(8,128)(2,1)S(1)}, u32[]{:S(2)}, u32[]{:S(2)}) collective-permute-start(bf16[25,16,128]{2,1,0:T(8,128)(2,1)S(1)} %get-tuple-element.49), channel_id=1, source_target_pairs={{0,1},{1,0},{2,3},{3,2},{4,5},{5,4},{6,7},{7,6},{8,9},{9,8},{10,11... | collective-permute-start | bytes 307208 | tf_op jit(solution)/shard_map/ppermute | solution.py:263
  4.2 6.3 %collective-permute-start.1 = (bf16[9,16,128]{2,1,0:T(8,128)(2,1)S(1)}, bf16[9,16,128]{2,1,0:T(8,128)(2,1)S(1)}, u32[]{:S(2)}, u32[]{:S(2)}) collective-permute-start(bf16[9,16,128]{2,1,0:T(8,128)(2,1)S(1)} %slice.12), channel_id=1, source_target_pairs={{0,3},{1,2},{2,1},{3,0},{4,7},{5,6},{6,5},{7,4},{8,11},{9,10},{10,... | collective-permute-start | bytes 110600 | tf_op jit(solution)/shard_map/ppermute | solution.py:264
  6.5 4.6 %collective-permute-start.2 = (bf16[9,16,128]{2,1,0:T(8,128)(2,1)S(1)}, bf16[9,16,128]{2,1,0:T(8,128)(2,1)S(1)}, u32[]{:S(2)}, u32[]{:S(2)}) collective-permute-start(bf16[9,16,128]{2,1,0:T(8,128)(2,1)S(1)} %slice.12), channel_id=1, source_target_pairs={{0,2},{1,3},{2,0},{3,1},{4,6},{5,7},{6,4},{7,5},{8,10},{9,11},{10,... | collective-permute-start | bytes 110600 | tf_op jit(solution)/shard_map/ppermute | solution.py:262
  9.0 0.9 %copy-start.5 = (bf16[16,4096]{1,0:T(8,128)(2,1)S(1)}, bf16[16,4096]{1,0:T(8,128)(2,1)}, u32[]{:S(2)}) copy-start(bf16[16,4096]{1,0:T(8,128)(2,1)} %dens_ref) | copy-start | bytes 393220
  9.9 0.7 %copy-start.9 = (s32[8,16]{1,0:T(8,128)S(1)}, s32[8,16]{1,0:T(8,128)}, u32[]{:S(2)}) copy-start(s32[8,16]{1,0:T(8,128)} %get-tuple-element.51.code_ref) | copy-start | bytes 1540
  11.1 9.9 %collective-permute-start.3 = (bf16[36,16,128]{2,1,0:T(8,128)(2,1)S(1)}, bf16[36,16,128]{2,1,0:T(8,128)(2,1)S(1)}, u32[]{:S(2)}, u32[]{:S(2)}) collective-permute-start(bf16[36,16,128]{2,1,0:T(8,128)(2,1)S(1)} %pad_maximum_fusion.4), channel_id=1, source_target_pairs={{0,8},{1,9},{2,10},{3,11},{4,36},{5,37},{6,38},{7,39},{8,16},{9,17... | collective-permute-start | bytes 442376 | tf_op jit(solution)/shard_map/ppermute | solution.py:194
  12.4 8.6 %collective-permute-start.4 = (bf16[36,16,128]{2,1,0:T(8,128)(2,1)S(1)}, bf16[36,16,128]{2,1,0:T(8,128)(2,1)S(1)}, u32[]{:S(2)}, u32[]{:S(2)}) collective-permute-start(bf16[36,16,128]{2,1,0:T(8,128)(2,1)S(1)} %pad_maximum_fusion.4), channel_id=1, source_target_pairs={{0,16},{1,17},{2,18},{3,19},{4,68},{5,69},{6,70},{7,71},{8,24},{9,... | collective-permute-start | bytes 442376 | tf_op jit(solution)/shard_map/ppermute | solution.py:194
  14.9 6.2 %collective-permute-start.5 = (bf16[36,16,128]{2,1,0:T(8,128)(2,1)S(1)}, bf16[36,16,128]{2,1,0:T(8,128)(2,1)S(1)}, u32[]{:S(2)}, u32[]{:S(2)}) collective-permute-start(bf16[36,16,128]{2,1,0:T(8,128)(2,1)S(1)} %pad_maximum_fusion.4), channel_id=1, source_target_pairs={{0,24},{1,25},{2,26},{3,27},{4,100},{5,101},{6,102},{7,103},{8,0},... | collective-permute-start | bytes 442376 | tf_op jit(solution)/shard_map/ppermute | solution.py:194
  21.1 11.2 %collective-permute-start.8 = (bf16[144,16,128]{2,1,0:T(8,128)(2,1)S(1)}, bf16[144,16,128]{2,1,0:T(8,128)(2,1)S(1)}, u32[]{:S(2)}, u32[]{:S(2)}) collective-permute-start(bf16[144,16,128]{2,1,0:T(8,128)(2,1)S(1)} %pad_maximum_fusion), channel_id=1, source_target_pairs={{0,4},{4,0},{1,5},{5,1},{2,6},{6,2},{3,7},{7,3},{8,12},{12,8},{9,1... | collective-permute-start | bytes 1769480 | tf_op jit(solution)/shard_map/ppermute | solution.py:296
  24.4 7.4 %collective-permute-start.6 = (bf16[72,16,128]{2,1,0:T(8,128)(2,1)S(1)}, bf16[72,16,128]{2,1,0:T(8,128)(2,1)S(1)}, u32[]{:S(2)}, u32[]{:S(2)}) collective-permute-start(bf16[72,16,128]{2,1,0:T(8,128)(2,1)S(1)} %get-tuple-element.70), channel_id=1, source_target_pairs={{0,32},{1,33},{2,34},{3,35},{4,12},{5,13},{6,14},{7,15},{8,40},{9,... | collective-permute-start | bytes 884744 | tf_op jit(solution)/shard_map/ppermute | solution.py:194
  24.9 7.4 %collective-permute-start.7 = (bf16[72,16,128]{2,1,0:T(8,128)(2,1)S(1)}, bf16[72,16,128]{2,1,0:T(8,128)(2,1)S(1)}, u32[]{:S(2)}, u32[]{:S(2)}) collective-permute-start(bf16[72,16,128]{2,1,0:T(8,128)(2,1)S(1)} %get-tuple-element.69), channel_id=1, source_target_pairs={{0,96},{1,97},{2,98},{3,99},{4,28},{5,29},{6,30},{7,31},{8,104},{9... | collective-permute-start | bytes 884744 | tf_op jit(solution)/shard_map/ppermute | solution.py:194
  27.2 7.9 %collective-permute-start.11 = (bf16[16,16,128]{2,1,0:T(8,128)(2,1)S(1)}, bf16[16,16,128]{2,1,0:T(8,128)(2,1)S(1)}, u32[]{:S(2)}, u32[]{:S(2)}) collective-permute-start(bf16[16,16,128]{2,1,0:T(8,128)(2,1)S(1)} %get-tuple-element.63), channel_id=1, source_target_pairs={{1,2},{3,4},{5,6},{7,8},{9,10},{11,12},{13,14},{15,16},{17,18},{19... | collective-permute-start | bytes 196616 | tf_op jit(solution)/shard_map/ppermute | solution.py:288
  30.6 9.7 %collective-permute-start.10 = (bf16[72,16,128]{2,1,0:T(8,128)(2,1)S(1)}, bf16[72,16,128]{2,1,0:T(8,128)(2,1)S(1)}, u32[]{:S(2)}, u32[]{:S(2)}) collective-permute-start(bf16[72,16,128]{2,1,0:T(8,128)(2,1)S(1)} %get-tuple-element.70), channel_id=1, source_target_pairs={{0,96},{1,97},{2,98},{3,99},{4,28},{5,29},{6,30},{7,31},{8,104},{9... | collective-permute-start | bytes 884744 | tf_op jit(solution)/shard_map/ppermute | solution.py:194
  31.8 8.5 %collective-permute-start.9 = (bf16[72,16,128]{2,1,0:T(8,128)(2,1)S(1)}, bf16[72,16,128]{2,1,0:T(8,128)(2,1)S(1)}, u32[]{:S(2)}, u32[]{:S(2)}) collective-permute-start(bf16[72,16,128]{2,1,0:T(8,128)(2,1)S(1)} %get-tuple-element.69), channel_id=1, source_target_pairs={{0,32},{1,33},{2,34},{3,35},{4,12},{5,13},{6,14},{7,15},{8,40},{9,... | collective-permute-start | bytes 884744 | tf_op jit(solution)/shard_map/ppermute | solution.py:194
  32.3 10.2 %collective-permute-start.12 = (bf16[72,16,128]{2,1,0:T(8,128)(2,1)S(1)}, bf16[72,16,128]{2,1,0:T(8,128)(2,1)S(1)}, u32[]{:S(2)}, u32[]{:S(2)}) collective-permute-start(bf16[72,16,128]{2,1,0:T(8,128)(2,1)S(1)} %collective-permute-done.6), channel_id=1, source_target_pairs={{0,32},{1,33},{2,34},{3,35},{4,12},{5,13},{6,14},{7,15},{8,40},{9,... | collective-permute-start | bytes 884744 | tf_op jit(solution)/shard_map/ppermute | solution.py:194
  32.8 9.8 %collective-permute-start.13 = (bf16[72,16,128]{2,1,0:T(8,128)(2,1)S(1)}, bf16[72,16,128]{2,1,0:T(8,128)(2,1)S(1)}, u32[]{:S(2)}, u32[]{:S(2)}) collective-permute-start(bf16[72,16,128]{2,1,0:T(8,128)(2,1)S(1)} %collective-permute-done.7), channel_id=1, source_target_pairs={{0,96},{1,97},{2,98},{3,99},{4,28},{5,29},{6,30},{7,31},{8,104},{9... | collective-permute-start | bytes 884744 | tf_op jit(solution)/shard_map/ppermute | solution.py:194
  40.2 6.3 %copy-start = (bf16[16,64,2048]{2,1,0:T(8,128)(2,1)S(1)}, bf16[16,64,2048]{2,1,0:T(8,128)(2,1)}, u32[]{:S(2)}) copy-start(bf16[16,64,2048]{2,1,0:T(8,128)(2,1)} %lc.1) | copy-start | bytes 12582916
  40.2 6.3 %copy-start.1 = (bf16[16,64,256]{2,1,0:T(8,128)(2,1)S(1)}, bf16[16,64,256]{2,1,0:T(8,128)(2,1)}, u32[]{:S(2)}) copy-start(bf16[16,64,256]{2,1,0:T(8,128)(2,1)} %basis_ref.1) | copy-start | bytes 1572868
  40.3 6.3 %copy-start.2 = (bf16[32,64,512]{2,1,0:T(8,128)(2,1)S(1)}, bf16[32,64,512]{2,1,0:T(8,128)(2,1)}, u32[]{:S(2)}) copy-start(bf16[32,64,512]{2,1,0:T(8,128)(2,1)} %gt.1) | copy-start | bytes 6291460
  40.3 6.3 %copy-start.3 = (bf16[2,64,512]{2,1,0:T(8,128)(2,1)S(1)}, bf16[2,64,512]{2,1,0:T(8,128)(2,1)}, u32[]{:S(2)}) copy-start(bf16[2,64,512]{2,1,0:T(8,128)(2,1)} %pt_ref.1) | copy-start | bytes 393220
  40.3 6.3 %copy-start.4 = (bf16[2,64,2048]{2,1,0:T(8,128)(2,1)S(1)}, bf16[2,64,2048]{2,1,0:T(8,128)(2,1)}, u32[]{:S(2)}) copy-start(bf16[2,64,2048]{2,1,0:T(8,128)(2,1)} %pc.1) | copy-start | bytes 1572868
  40.3 6.3 %copy-start.6 = (bf16[1,64,1024]{2,1,0:T(8,128)(2,1)S(1)}, bf16[1,64,1024]{2,1,0:T(8,128)(2,1)}, u32[]{:S(2)}) copy-start(bf16[1,64,1024]{2,1,0:T(8,128)(2,1)} %gc.1) | copy-start | bytes 393220
  40.3 6.3 %copy-start.7 = (s32[16,32]{1,0:T(8,128)S(1)}, s32[16,32]{1,0:T(8,128)}, u32[]{:S(2)}) copy-start(s32[16,32]{1,0:T(8,128)} %get-tuple-element.46.leaf_ref) | copy-start | bytes 6148
  40.3 6.3 %copy-start.8 = (s32[6,16]{1,0:T(8,128)S(1)}, s32[6,16]{1,0:T(8,128)}, u32[]{:S(2)}) copy-start(s32[6,16]{1,0:T(8,128)} %get-tuple-element.48.grand_ref) | copy-start | bytes 1156
  40.3 6.3 %copy-start.10 = (s32[2,32]{1,0:T(2,128)S(1)}, s32[2,32]{1,0:T(2,128)}, u32[]{:S(2)}) copy-start(s32[2,32]{1,0:T(2,128)} %get-tuple-element.47.parent_ref) | copy-start | bytes 772
  40.4 4.6 %collective-permute-start.14 = (bf16[144,16,128]{2,1,0:T(8,128)(2,1)S(1)}, bf16[144,16,128]{2,1,0:T(8,128)(2,1)S(1)}, u32[]{:S(2)}, u32[]{:S(2)}) collective-permute-start(bf16[144,16,128]{2,1,0:T(8,128)(2,1)S(1)} %pad_maximum_fusion.1), channel_id=1, source_target_pairs={{0,4},{4,0},{1,5},{5,1},{2,6},{6,2},{3,7},{7,3},{8,12},{12,8},{9,1... | collective-permute-start | bytes 1769480 | tf_op jit(solution)/shard_map/ppermute | solution.py:306
  42.4 2.8 %collective-permute-start.15 = (bf16[144,16,128]{2,1,0:T(8,128)(2,1)S(1)}, bf16[144,16,128]{2,1,0:T(8,128)(2,1)S(1)}, u32[]{:S(2)}, u32[]{:S(2)}) collective-permute-start(bf16[144,16,128]{2,1,0:T(8,128)(2,1)S(1)} %pad_maximum_fusion.2), channel_id=1, source_target_pairs={{0,4},{4,0},{1,5},{5,1},{2,6},{6,2},{3,7},{7,3},{8,12},{12,8},{9,1... | collective-permute-start | bytes 1769480 | tf_op jit(solution)/shard_map/ppermute | solution.py:306
  42.6 3.8 %collective-permute-start.16 = (bf16[144,16,128]{2,1,0:T(8,128)(2,1)S(1)}, bf16[144,16,128]{2,1,0:T(8,128)(2,1)S(1)}, u32[]{:S(2)}, u32[]{:S(2)}) collective-permute-start(bf16[144,16,128]{2,1,0:T(8,128)(2,1)S(1)} %pad_maximum_fusion.3), channel_id=1, source_target_pairs={{0,4},{4,0},{1,5},{5,1},{2,6},{6,2},{3,7},{7,3},{8,12},{12,8},{9,1... | collective-permute-start | bytes 1769480 | tf_op jit(solution)/shard_map/ppermute | solution.py:306
